TPU v7x, 32 devices: a whole 2x2x4 slice. The times are simulated.
32 devices in a mesh: groups: 2 (over y), lat: 8 (over z, x), seq: 2 (over core).
Axes of the slice: x: 2, y: 2, z: 4, core: 2. Of those that a mesh axis runs over, the one named last changes fastest.
Arguments:
- residual: bfloat16 [1024, 3584], P(('groups', 'lat', 'seq')), parts along dimension 0, may hold values from -6 to 6
- gradient: bfloat16 [1024, 3584], P(('groups', 'lat', 'seq')), parts along dimension 0, may hold values from -6 to 6
- block_ids: int32 [1024, 4], P(('groups', 'lat', 'seq')), parts along dimension 0, may hold values from 0 to 7, all different within a row; in each aligned block of 32 rows (0 to 31, 32 to 63, ...) at most 24 rows name the same one
- jump_mask: int32 [1024, 4, 128], P(('groups', 'lat', 'seq')), parts along dimension 0, may hold values 0 or 1
- encoder: bfloat16 [3584, 1024], P(None, 'lat'), may hold values from -0.09375 to 0.09375
- enc_bias: float32 [1024], P('lat'), may hold values from -6 to 6
- decoder: bfloat16 [1024, 3584], P('lat'), may hold values from -0.25 to 0.25
- dec_bias: float32 [3584], replicated, may hold values from -6 to 6
Outputs:
- latent_codes: bfloat16 [1024, 4, 128], P(('groups', 'lat', 'seq')), parts along dimension 0
- attribution: float32 [1024, 4, 128], P(('groups', 'lat', 'seq')), parts along dimension 0
- recon_error: bfloat16 [1024, 3584], P(('groups', 'lat', 'seq')), parts along dimension 0
- latent_totals: float32 [2048], P(('groups', 'lat', 'seq')), parts along dimension 0
There are 2 independent parts, one for each index of `groups`. A program takes and returns all parts, laid end to end along the dimension named above; an argument that names none is the same for every part. Nothing has to cross between parts.
Inputs may be any that keep to these rules, and one draw needn't show every extreme that they name: `block_ids`: each token names 4 different blocks. Among the rows of one device no block is named more than 24 times, and in every draw some device's rows name one block exactly 24 times.
All inputs are finite; a program needn't handle non-finite values. No bound on the sum of `jump_mask` on one device may be relied on, other than what follows from the above.
Results may differ from a plain program's by a relative error of at most 0.0044.
Values may be sent and summed in bfloat16 or wider, within the bound.
No kernel may reach another device: no remote copies, remote signals or barrier semaphores. Data moves between devices by JAX's collectives and lax.ppermute only.
A program may use at most 64 MiB of HBM per device.

v0:
```python
import jax
import jax.numpy as jnp
from jax import lax
from jax.sharding import PartitionSpec as P


def place_rows(values, source, filled, leading):
    picked = jnp.where(filled[:, None], values[source], jnp.zeros((), values.dtype))
    return picked.reshape(leading + (values.shape[-1],))


def on_device(residual, gradient, block_ids, jump_mask, encoder, enc_bias, decoder, dec_bias):
    tok_rows, width = residual.shape
    active = block_ids.shape[1]
    lanes = jump_mask.shape[2]
    lat_count = lax.axis_size("lat")
    seq_count = lax.axis_size("seq")
    local_blocks = encoder.shape[1] // lanes
    block_count = local_blocks * lat_count
    capacity = max(
        2, min(tok_rows, (3 * tok_rows * active + 2 * block_count - 1) // (2 * block_count))
    )
    slot_count = tok_rows * active
    flat_blocks = block_ids.reshape(slot_count)
    one_hot = (flat_blocks[:, None] == jnp.arange(block_count, dtype=jnp.int32)[None, :]).astype(
        jnp.int32
    )
    earlier = jnp.sum(jnp.cumsum(one_hot, axis=0) * one_hot, axis=1) - 1
    slot_id = flat_blocks * capacity + earlier
    owner_row = (
        jnp.zeros((block_count * capacity,), jnp.int32)
        .at[slot_id]
        .set(jnp.arange(slot_count, dtype=jnp.int32) + 1)
    )
    filled = owner_row > 0
    slot_source = jnp.maximum(owner_row - 1, 0)
    token_source = slot_source // active
    leading = (lat_count, local_blocks, capacity)
    enc_blocks = encoder.reshape(width, local_blocks, lanes)
    dec_blocks = decoder.reshape(local_blocks, lanes, width)
    bias_blocks = enc_bias.reshape(1, local_blocks, 1, lanes)
    mask_values = jump_mask.astype(jnp.float32)
    total_tokens = tok_rows * lat_count * seq_count
    factor = (total_tokens * active / block_count) ** (-0.5)

    def gather_home(slotted):
        last = slotted.shape[-1]
        return slotted.reshape(block_count * capacity, last)[slot_id].reshape(
            tok_rows, active, last
        )

    residual_slots = place_rows(residual, token_source, filled, leading)
    gradient_slots = place_rows(gradient, token_source, filled, leading)
    preact = lax.all_to_all(
        (
            jnp.einsum(
                "sbcd,dbj->sbcj",
                lax.all_to_all(residual_slots, "lat", split_axis=0, concat_axis=0, tiled=True),
                enc_blocks,
                preferred_element_type=jnp.float32,
            )
            + bias_blocks
        ).astype(jnp.bfloat16),
        "lat",
        split_axis=0,
        concat_axis=0,
        tiled=True,
    ).astype(jnp.float32)
    latent_codes = (gather_home(preact) * mask_values).astype(jnp.bfloat16)
    code_slots = place_rows(latent_codes.reshape(slot_count, lanes), slot_source, filled, leading)
    code_data = lax.all_to_all(code_slots, "lat", split_axis=0, concat_axis=0, tiled=True)
    grad_data = lax.all_to_all(gradient_slots, "lat", split_axis=0, concat_axis=0, tiled=True)
    score_data = code_data.astype(jnp.float32) * jnp.einsum(
        "sbcd,bjd->sbcj", grad_data, dec_blocks, preferred_element_type=jnp.float32
    )
    recon_home = lax.all_to_all(
        jnp.einsum(
            "sbcj,bjd->sbcd", code_data, dec_blocks, preferred_element_type=jnp.float32
        ).astype(jnp.bfloat16),
        "lat",
        split_axis=0,
        concat_axis=0,
        tiled=True,
    )
    score_home = lax.all_to_all(score_data, "lat", split_axis=0, concat_axis=0, tiled=True)
    recon_slots = recon_home
    attribution = gather_home(score_home)
    recon_home = gather_home(recon_slots)
    recon_error = (
        residual.astype(jnp.float32) - dec_bias - jnp.sum(recon_home.astype(jnp.float32), axis=1)
    ).astype(jnp.bfloat16)
    term = jnp.dot(
        one_hot.T.astype(jnp.float32),
        attribution.reshape(slot_count, lanes),
        precision=lax.Precision.HIGHEST,
    )
    latent_totals = (
        lax.psum_scatter(
            term.reshape(block_count * lanes), ("lat", "seq"), scatter_dimension=0, tiled=True
        )
        * factor
    )
    return (latent_codes, attribution, recon_error, latent_totals)


def solution(mesh):
    return jax.shard_map(
        on_device,
        mesh=mesh,
        in_specs=(
            P(("groups", "lat", "seq"), None),
            P(("groups", "lat", "seq"), None),
            P(("groups", "lat", "seq"), None),
            P(("groups", "lat", "seq"), None, None),
            P(None, "lat"),
            P("lat"),
            P("lat", None),
            P(),
        ),
        out_specs=(
            P(("groups", "lat", "seq"), None, None),
            P(("groups", "lat", "seq"), None, None),
            P(("groups", "lat", "seq"), None),
            P(("groups", "lat", "seq")),
        ),
        check_vma=False,
    )
```

profile of v0, /device:TPU:0, one launch (start us, length us, event | category | flops | bytes accessed | tf_op | source)
XLA Modules:
  0.0 176.0 jit_solution(1404245234708414342)
XLA Ops:
  0.7 0.9 copy.17
  1.5 0.7 broadcast_multiply_fusion
  2.2 0.1 eq.22
  2.4 0.2 reduce_window_sum.11
  2.6 0.2 select_reduce_fusion
  2.8 0.1 mul.33
  3.0 1.0 scatter_custom_fusion
  4.0 1.4 gather_fusion.3
  5.5 2.5 %gather_fusion = bf16[192,3584]{1,0:T(8,128)(2,1)} fusion(bf16[32,3584]{1,0:T(8,128)(2,1)S(1)} %copy-done.1, s32[1024]{0:T(1024)S(1)} %get-tuple-element.9), kind=kCustom, calls=%fused_computation | custom fusion | bytes 2753280 | tf_op jit(solution)/shard_map/gather | solution.py:8
  8.1 2.7 %broadcast_select_fusion = (bf16[8,1,24,3584]{3,2,1,0:T(8,128)(2,1)}, bf16[8,1,24,3584]{3,2,1,0:T(8,128)(2,1)S(1)}) fusion(bf16[8,1,24,3584]{3,2,1,0:T(8,128)(2,1)S(1)} %bitcast.96, pred[8,24]{1,0:T(8,128)(4,1)S(1)} %broadcast_in_dim.46, bf16[8,1,24,3584]{3,2,1,0:T(8,128)(2,1)} %bitcast.97), kind=kLoop, calls=%fused_computation.13 | loop fusion | flops 1376256 | bytes 5505216 | tf_op jit(solution)/shard_map/jit(_where)/select_n | solution.py:8
  10.8 40.6 %all_to_all.30 = bf16[8,1,24,3584]{3,2,1,0:T(8,128)(2,1)S(1)} all-to-all(bf16[8,1,24,3584]{3,2,1,0:T(8,128)(2,1)S(1)} %get-tuple-element.7), channel_id=1, replica_groups=mesh['groups'=2,'lat'=8,'seq'=2] {'lat'}, dimensions={0} | all-to-all | bytes 2752512 | tf_op jit(solution)/shard_map/all_to_all | solution.py:58
  51.3 0.5 fusion.23
  51.9 9.6 %all_to_all.31 = bf16[8,1,24,128]{3,2,1,0:T(8,128)(2,1)S(1)} all-to-all(bf16[8,1,24,128]{3,2,1,0:T(8,128)(2,1)S(1)} %fusion.23), channel_id=1, replica_groups=mesh['groups'=2,'lat'=8,'seq'=2] {'lat'}, dimensions={0} | all-to-all | bytes 98304 | tf_op jit(solution)/shard_map/all_to_all | solution.py:54
  61.4 3.7 %all-to-all-start.3 = ((bf16[8,1,24,3584]{3,2,1,0:T(8,128)(2,1)}), bf16[8,1,24,3584]{3,2,1,0:T(8,128)(2,1)S(1)}, u32[]{:S(2)}, u32[]{:S(2)}) async-start(bf16[8,1,24,3584]{3,2,1,0:T(8,128)(2,1)} %get-tuple-element.6), calls=%async_computation.3 | async-start | bytes 2752512 | tf_op jit(solution)/shard_map/all_to_all | solution.py:72
  65.2 0.6 gather_fusion.1
  65.9 0.8 gather_fusion.2
  66.8 29.9 %all-to-all-done.3 = bf16[8,1,24,3584]{3,2,1,0:T(8,128)(2,1)S(1)} async-done(((bf16[8,1,24,3584]{3,2,1,0:T(8,128)(2,1)}), bf16[8,1,24,3584]{3,2,1,0:T(8,128)(2,1)S(1)}, u32[]{:S(2)}, u32[]{:S(2)}) %all-to-all-start.3) | async-done | bytes 1376288 | tf_op jit(solution)/shard_map/all_to_all | solution.py:72
  96.7 10.0 %all_to_all.32 = bf16[8,1,24,128]{3,2,1,0:T(8,128)(2,1)S(1)} all-to-all(bf16[8,1,24,128]{3,2,1,0:T(8,128)(2,1)S(1)} %broadcast_select_fusion.2), channel_id=1, replica_groups=mesh['groups'=2,'lat'=8,'seq'=2] {'lat'}, dimensions={0} | all-to-all | bytes 98304 | tf_op jit(solution)/shard_map/all_to_all | solution.py:71
  106.7 1.2 fusion.14
  107.9 3.4 %all-to-all-start.4 = ((f32[8,1,24,128]{3,2,1,0:T(8,128)}), f32[8,1,24,128]{3,2,1,0:T(8,128)S(1)}, u32[]{:S(2)}, u32[]{:S(2)}) async-start(f32[8,1,24,128]{3,2,1,0:T(8,128)} %fusion.14), calls=%async_computation.4 | async-start | bytes 196608 | tf_op jit(solution)/shard_map/all_to_all | solution.py:85
  111.2 1.6 fusion
  112.9 5.4 %all-to-all-done.4 = f32[8,1,24,128]{3,2,1,0:T(8,128)S(1)} async-done(((f32[8,1,24,128]{3,2,1,0:T(8,128)}), f32[8,1,24,128]{3,2,1,0:T(8,128)S(1)}, u32[]{:S(2)}, u32[]{:S(2)}) %all-to-all-start.4) | async-done | bytes 98336 | tf_op jit(solution)/shard_map/all_to_all | solution.py:85
  118.3 3.6 %all-to-all-start.5 = ((bf16[8,1,24,3584]{3,2,1,0:T(8,128)(2,1)}), bf16[8,1,24,3584]{3,2,1,0:T(8,128)(2,1)S(1)}, u32[]{:S(2)}, u32[]{:S(2)}) async-start(bf16[8,1,24,3584]{3,2,1,0:T(8,128)(2,1)} %fusion), calls=%async_computation.5 | async-start | bytes 2752512 | tf_op jit(solution)/shard_map/all_to_all | solution.py:76
  121.9 0.6 dynamic-slice
  123.1 0.6 gather_fusion.4
  123.8 0.2 convolution_bitcast_fusion
  123.9 45.8 %all-reduce = f32[1024]{0:T(1024)S(1)} all-reduce(f32[1024]{0:T(1024)S(1)} %convolution_bitcast_fusion), channel_id=2, replica_groups=mesh['groups'=2,'lat'=8,'seq'=2] {'lat','seq'}, use_global_device_ids=true, to_apply=%region_4.5.clone | all-reduce | flops 1024 | bytes 8192
  169.7 0.6 dynamic-slice_multiply_fusion
  170.3 2.1 %gather_fusion.5 = bf16[128,3584]{1,0:T(8,128)(2,1)} fusion(bf16[192,3584]{1,0:T(8,128)(2,1)S(1)} %bitcast.94, s32[1024]{0:T(1024)S(1)} %pad_clamp_fusion.1), kind=kCustom, calls=%fused_computation.5 | custom fusion | bytes 1835520 | tf_op jit(solution)/shard_map/gather | solution.py:48
  172.3 1.8 %reshape.162 = f32[32,4,3584]{2,1,0:T(4,128)S(1)} reshape(bf16[128,3584]{1,0:T(8,128)(2,1)} %gather_fusion.5) | data formatting | bytes 2752512 | tf_op jit(solution)/shard_map/convert_element_type | solution.py:90
  174.2 1.1 reduce_sum.19
  175.3 0.7 subtract_convert_fusion
  (33 shorter events, 0.5 us)
Async XLA Ops:
  0.6 106.1 %copy-start = (bf16[128,3584]{1,0:T(8,128)(2,1)S(1)}, bf16[128,3584]{1,0:T(8,128)(2,1)}, u32[]{:S(2)}) copy-start(bf16[128,3584]{1,0:T(8,128)(2,1)} %param.14) | copy-start | bytes 2752516
  0.6 3.4 %copy-start.2 = (bf16[32,3584]{1,0:T(8,128)(2,1)S(1)}, bf16[32,3584]{1,0:T(8,128)(2,1)}, u32[]{:S(2)}) copy-start(bf16[32,3584]{1,0:T(8,128)(2,1)} %param.9) | copy-start | bytes 688132
  4.0 1.4 copy-start.1
  10.7 40.6 %copy-start.4 = (bf16[3584,128]{1,0:T(8,128)(2,1)S(1)}, bf16[3584,128]{1,0:T(8,128)(2,1)}, u32[]{:S(2)}) copy-start(bf16[3584,128]{1,0:T(8,128)(2,1)} %param.12) | copy-start | bytes 2752516
  10.7 40.6 %copy-start.8 = (f32[128]{0:T(128)S(1)}, f32[128]{0:T(128)}, u32[]{:S(2)}) copy-start(f32[128]{0:T(128)} %param.13) | copy-start | bytes 1540
  61.4 4.4 %copy-start.6 = (s32[32,4,128]{2,1,0:T(4,128)S(1)}, s32[32,4,128]{2,1,0:T(4,128)}, u32[]{:S(2)}) copy-start(s32[32,4,128]{2,1,0:T(4,128)} %param.11) | copy-start | bytes 196612
  61.4 35.3 %all-to-all-start.3 = ((bf16[8,1,24,3584]{3,2,1,0:T(8,128)(2,1)}), bf16[8,1,24,3584]{3,2,1,0:T(8,128)(2,1)S(1)}, u32[]{:S(2)}, u32[]{:S(2)}) async-start(bf16[8,1,24,3584]{3,2,1,0:T(8,128)(2,1)} %get-tuple-element.6), calls=%async_computation.3 | async-start | bytes 2752512 | tf_op jit(solution)/shard_map/all_to_all | solution.py:72
  65.9 42.0 %copy-start.3 = (bf16[32,4,128]{2,1,0:T(4,128)(2,1)}, bf16[32,4,128]{2,1,0:T(4,128)(2,1)S(1)}, u32[]{:S(2)}) copy-start(bf16[32,4,128]{2,1,0:T(4,128)(2,1)S(1)} %multiply_convert_fusion) | copy-start | bytes 98308
  107.9 10.4 %all-to-all-start.4 = ((f32[8,1,24,128]{3,2,1,0:T(8,128)}), f32[8,1,24,128]{3,2,1,0:T(8,128)S(1)}, u32[]{:S(2)}, u32[]{:S(2)}) async-start(f32[8,1,24,128]{3,2,1,0:T(8,128)} %fusion.14), calls=%async_computation.4 | async-start | bytes 196608 | tf_op jit(solution)/shard_map/all_to_all | solution.py:85
  112.9 9.0 %copy-start.9 = (u32[32]{0:T(128)S(1)}, u32[32]{0:T(128)}, u32[]{:S(2)}) copy-start(u32[32]{0:T(128)} %constant.45) | copy-start | bytes 388
  118.3 52.0 %all-to-all-start.5 = ((bf16[8,1,24,3584]{3,2,1,0:T(8,128)(2,1)}), bf16[8,1,24,3584]{3,2,1,0:T(8,128)(2,1)S(1)}, u32[]{:S(2)}, u32[]{:S(2)}) async-start(bf16[8,1,24,3584]{3,2,1,0:T(8,128)(2,1)} %fusion), calls=%async_computation.5 | async-start | bytes 2752512 | tf_op jit(solution)/shard_map/all_to_all | solution.py:76
  123.8 48.6 %copy-start.5 = (f32[128,128]{1,0:T(8,128)}, f32[128,128]{1,0:T(8,128)S(1)}, u32[]{:S(2)}) copy-start(f32[128,128]{1,0:T(8,128)S(1)} %gather_fusion.4) | copy-start | bytes 196612
  174.1 1.1 copy-start.7
where the time goes:
time: 177 us; the launch traced here: 176 us
  blocking collectives  106 us (60%)
  waiting for transfers between devices  35.4 us (20%)
  local copies, waits for them, and re-layouts  12.7 us (7%)
  starting transfers between devices  10.6 us (6%)
  other arithmetic  6.36 us (4%)
  matrix products  3.48 us (2%)
    unnamed x1, blocking collectives  45.8 us
    all_to_all x1, blocking collectives, on_device(): lax.all_to_all(residual_slots, 'lat', split_axis=0, concat_axis=0, tiled=...  40.6 us
    all_to_all x1, waiting for transfers between devices, on_device(): lax.all_to_all(gradient_slots, 'lat', split_axis=0, concat_axis=0, tiled=...  29.9 us
    all_to_all x1, blocking collectives, on_device(): lax.all_to_all(code_slots, 'lat', split_axis=0, concat_axis=0, tiled=True)  9.97 us
    all_to_all x1, blocking collectives, on_device(): lax.all_to_all((jnp.einsum('sbcd,dbj->sbcj', lax.all_to_all(residual_slot...  9.55 us
    all_to_all x1, waiting for transfers between devices, on_device(): lax.all_to_all(score_data, 'lat', split_axis=0, concat_axis=0, tiled=True)  5.44 us
    gather x3, local copies, waits for them, and re-layouts, place_rows(): values[source]  4.73 us
    all_to_all x1, starting transfers between devices, on_device(): lax.all_to_all(gradient_slots, 'lat', split_axis=0, concat_axis=0, tiled=...  3.7 us
  transfers between devices with their start and end apart: 3, of which 2 were waited for; matrix products, arithmetic and copies ran while one was open for 3% of the time, Pallas kernels for 0%

commit v1 on v0

v1 whole, which is shorter than its diff:
```python
import jax
import jax.numpy as jnp
from jax import lax
from jax.sharding import PartitionSpec as P

AXES = ("groups", "lat", "seq")


def place_rows(values, source, filled, leading):
    picked = jnp.where(filled[:, None], values[source], jnp.zeros((), values.dtype))
    return picked.reshape(leading + (values.shape[-1],))


def move_tokens(residual, gradient, block_ids, jump_mask, encoder, enc_bias, decoder, dec_bias):
    tok_rows, width = residual.shape
    active = block_ids.shape[1]
    lanes = jump_mask.shape[2]
    lat_count = lax.axis_size("lat")
    seq_count = lax.axis_size("seq")
    local_blocks = encoder.shape[1] // lanes
    block_count = local_blocks * lat_count
    capacity = max(
        2, min(tok_rows, (3 * tok_rows * active + 2 * block_count - 1) // (2 * block_count))
    )
    slot_count = tok_rows * active
    flat_blocks = block_ids.reshape(slot_count)
    one_hot = (flat_blocks[:, None] == jnp.arange(block_count, dtype=jnp.int32)[None, :]).astype(
        jnp.int32
    )
    earlier = jnp.sum(jnp.cumsum(one_hot, axis=0) * one_hot, axis=1) - 1
    slot_id = flat_blocks * capacity + earlier
    owner_row = (
        jnp.zeros((block_count * capacity,), jnp.int32)
        .at[slot_id]
        .set(jnp.arange(slot_count, dtype=jnp.int32) + 1)
    )
    filled = owner_row > 0
    slot_source = jnp.maximum(owner_row - 1, 0)
    token_source = slot_source // active
    leading = (lat_count, local_blocks, capacity)
    enc_blocks = encoder.reshape(width, local_blocks, lanes)
    dec_blocks = decoder.reshape(local_blocks, lanes, width)
    bias_blocks = enc_bias.reshape(1, local_blocks, 1, lanes)
    mask_values = jump_mask.astype(jnp.float32)
    total_tokens = tok_rows * lat_count * seq_count
    factor = (total_tokens * active / block_count) ** (-0.5)

    def gather_home(slotted):
        last = slotted.shape[-1]
        return slotted.reshape(block_count * capacity, last)[slot_id].reshape(
            tok_rows, active, last
        )

    def swap(values):
        return lax.all_to_all(values, "lat", split_axis=0, concat_axis=0, tiled=True)

    residual_slots = place_rows(residual, token_source, filled, leading)
    gradient_slots = place_rows(gradient, token_source, filled, leading)
    preact = jnp.einsum(
        "sbcd,dbj->sbcj", swap(residual_slots), enc_blocks, preferred_element_type=jnp.float32
    )
    preact = swap((preact + bias_blocks).astype(jnp.bfloat16)).astype(jnp.float32)
    latent_codes = (gather_home(preact) * mask_values).astype(jnp.bfloat16)
    code_slots = place_rows(latent_codes.reshape(slot_count, lanes), slot_source, filled, leading)
    code_data = swap(code_slots)
    grad_data = swap(gradient_slots)
    score_data = code_data.astype(jnp.float32) * jnp.einsum(
        "sbcd,bjd->sbcj", grad_data, dec_blocks, preferred_element_type=jnp.float32
    )
    recon_data = jnp.einsum(
        "sbcj,bjd->sbcd", code_data, dec_blocks, preferred_element_type=jnp.float32
    )
    recon_home = gather_home(swap(recon_data.astype(jnp.bfloat16)))
    attribution = gather_home(swap(score_data))
    recon_error = (
        residual.astype(jnp.float32) - dec_bias - jnp.sum(recon_home.astype(jnp.float32), axis=1)
    ).astype(jnp.bfloat16)
    term = jnp.dot(
        one_hot.T.astype(jnp.float32),
        attribution.reshape(slot_count, lanes),
        precision=lax.Precision.HIGHEST,
    )
    latent_totals = (
        lax.psum_scatter(
            term.reshape(block_count * lanes), ("lat", "seq"), scatter_dimension=0, tiled=True
        )
        * factor
    )
    return (latent_codes, attribution, recon_error, latent_totals)


def nt(a, b):
    return lax.dot_general(a, b, (((1,), (1,)), ((), ())), preferred_element_type=jnp.float32)


def move_weights(residual, gradient, block_ids, jump_mask, encoder, enc_bias, decoder, dec_bias):
    tok, width = residual.shape
    active = block_ids.shape[1]
    lanes = jump_mask.shape[2]
    lat_count = lax.axis_size("lat")
    ring = lat_count // 2
    per = lanes // 4
    half = width // 2
    bf = jnp.bfloat16
    f32 = jnp.float32
    g = lax.axis_index("groups")
    lat = lax.axis_index("lat")
    s = lax.axis_index("seq")
    z, x = lat // 2, lat % 2
    q = 2 * s + g

    def permute(values, to):
        pairs = []
        for gg in range(2):
            for ll in range(lat_count):
                for ss in range(2):
                    a, b, c = to(gg, ll, ss)
                    pairs.append(((gg * lat_count + ll) * 2 + ss, (a * lat_count + b) * 2 + c))
        return lax.ppermute(values, AXES, pairs)

    def by_x(v):
        return permute(v, lambda gg, ll, ss: (gg, ll ^ 1, ss))

    def by_y(v):
        return permute(v, lambda gg, ll, ss: (1 - gg, ll, ss))

    def by_core(v):
        return permute(v, lambda gg, ll, ss: (gg, ll, 1 - ss))

    def by_z(v, k):
        return permute(v, lambda gg, ll, ss: (gg, (ll + 2 * k) % lat_count, ss))

    lane_id = lax.broadcasted_iota(jnp.int32, (per, lanes), 1)
    row_id = lax.broadcasted_iota(jnp.int32, (per, lanes), 0)
    pick = (lane_id == row_id + per * q).astype(bf)
    enc_q = nt(pick, encoder).astype(bf)
    bias_q = lax.dynamic_slice_in_dim(enc_bias, q * per, per)
    hi = lax.reduce_precision(bias_q, 8, 7)
    mid = lax.reduce_precision(bias_q - hi, 8, 7)
    low = lax.reduce_precision(bias_q - hi - mid, 8, 7)
    bias_cols = jnp.stack([hi, mid, low], axis=1).astype(bf)
    enc_q = jnp.concatenate([enc_q, jnp.pad(bias_cols, ((0, 0), (0, 125)))], axis=1)
    dec_q = lax.dynamic_slice_in_dim(decoder, q * per, per)
    enc_parts, dec_parts = [enc_q], [dec_q]
    for _ in range(ring - 1):
        enc_parts.append(by_z(enc_parts[-1], 1))
        dec_parts.append(by_z(dec_parts[-1], 1))
    enc_all = jnp.concatenate(enc_parts, axis=0)
    dec_all = jnp.concatenate(dec_parts, axis=0)

    blocks = jnp.arange(lat_count, dtype=jnp.int32)
    named = block_ids[:, :, None] == blocks[None, None, :]
    mask = jnp.sum(
        jnp.where(named[:, :, :, None], jump_mask[:, :, None, :], 0), axis=1
    ).astype(bf).reshape(tok, lat_count * lanes)
    mh = lat_count * lanes // 2
    a0 = jnp.concatenate([residual[:, :half], gradient[:, :half], mask[:, :mh]], axis=1)
    b0 = jnp.concatenate([residual[:, half:], gradient[:, half:], mask[:, mh:]], axis=1)
    a1 = by_y(a0)
    b1 = by_x(b0)
    a01 = jnp.concatenate([a0, a1], axis=0)
    a2 = by_x(a01)
    b2 = by_y(jnp.concatenate([b0, b1], axis=0))
    mine = jnp.concatenate(
        [
            jnp.concatenate([a01, a2], axis=0),
            jnp.concatenate([b0, b2[:tok], b1, b2[tok:]], axis=0),
        ],
        axis=1,
    )
    rows = jnp.concatenate([mine, by_core(mine)], axis=0)
    side = 2 * half + mh
    res_a, res_b = rows[:, :half], rows[:, side : side + half]
    grad_a, grad_b = rows[:, half : 2 * half], rows[:, side + half : side + 2 * half]
    mask_all = jnp.concatenate([rows[:, 2 * half : side], rows[:, side + 2 * half :]], axis=1)
    n_rows = rows.shape[0]

    def source_lane(c, zz, xx, qq):
        return (((zz - c // per) % ring) * 2 + xx) * lanes + qq * per + c % per

    width_all = lat_count * lanes
    mine_lanes = ring * per
    want = source_lane(lax.broadcasted_iota(jnp.int32, (mine_lanes, width_all), 0), z, x, q)
    pick_mask = (want == lax.broadcasted_iota(jnp.int32, (mine_lanes, width_all), 1)).astype(bf)
    mask_here = nt(mask_all, pick_mask)

    preact = (
        nt(res_a, enc_all[:, :half])
        + nt(res_b, enc_all[:, half:width])
        + nt(jnp.ones((n_rows, 128), bf), enc_all[:, width:])
    )
    codes = (preact * mask_here).astype(bf)
    projected = nt(grad_a, dec_all[:, :half]) + nt(grad_b, dec_all[:, half:])
    scores = codes.astype(f32) * projected
    recon = jnp.dot(codes, dec_all, preferred_element_type=f32).astype(bf)
    scores_b = scores.astype(bf)

    by_kind = scores.reshape(2, 2, 2, tok, mine_lanes).sum(axis=(0, 1, 3))
    sums = by_kind[:, :per]
    for k in range(1, ring):
        sums = sums + by_z(by_kind, -k)[:, per * k : per * k + per]
    other = by_y(sums[1])
    factor = (tok * lat_count * 2 * active / lat_count) ** (-0.5)
    latent_totals = (
        jnp.where(g == 0, jnp.concatenate([sums[0], other]), jnp.concatenate([other, sums[0]]))
        * factor
    )

    hr = n_rows // 2
    keep = jnp.concatenate([recon, codes, scores_b], axis=1)
    got = by_core(keep[hr:])
    summed = recon[:hr].astype(f32) + got[:, :width].astype(f32)
    code_two = jnp.concatenate([codes[:hr], got[:, width : width + mine_lanes]], axis=1)
    score_two = jnp.concatenate([scores_b[:hr], got[:, width + mine_lanes :]], axis=1)
    sum_a, sum_b = summed[:, :half], summed[:, half:]
    pa = jnp.concatenate([sum_a.astype(bf), code_two], axis=1)
    pb = jnp.concatenate([sum_b.astype(bf), score_two], axis=1).reshape(2, 2, tok, -1)
    got_a = by_x(pa[2 * tok :])
    got_b = by_y(pb[:, 1])
    sum_a = sum_a[: 2 * tok] + got_a[:, :half].astype(f32)
    sum_b = sum_b.reshape(2, 2, tok, half)[:, 0] + got_b[:, :, :half].astype(f32)
    code_four = jnp.concatenate([code_two[: 2 * tok], got_a[:, half:]], axis=1)
    score_four = jnp.concatenate([pb[:, 0, :, half:], got_b[:, :, half:]], axis=2)
    got_a = by_y(jnp.concatenate([sum_a[tok:].astype(bf), code_four[tok:]], axis=1))
    got_b = by_x(jnp.concatenate([sum_b[1].astype(bf), score_four[1]], axis=1))
    recon_home = jnp.concatenate(
        [
            sum_a[:tok] + got_a[:, :half].astype(f32),
            sum_b[0] + got_b[:, :half].astype(f32),
        ],
        axis=1,
    )
    recon_error = (residual.astype(f32) - dec_bias - recon_home).astype(bf)

    code_src = jnp.concatenate([code_four[:tok], got_a[:, half:]], axis=1)
    score_src = jnp.concatenate([score_four[0], got_b[:, half:]], axis=1)
    lane = lax.broadcasted_iota(jnp.int32, (width_all, width_all), 0)
    part, inner = lane // mine_lanes, lane % mine_lanes
    out_lane = lax.broadcasted_iota(jnp.int32, (width_all, width_all), 1)

    def spread(first, second):
        xx = x ^ first
        yy = g ^ second
        qq = 2 * (s ^ (part % 2)) + yy
        return (source_lane(inner, z, xx, qq) == out_lane).astype(bf)

    code_dense = jnp.dot(
        code_src, spread((part // 2) % 2, part // 4), preferred_element_type=f32
    ).reshape(tok, 1, lat_count, lanes)
    score_dense = jnp.dot(
        score_src, spread(part // 4, (part // 2) % 2), preferred_element_type=f32
    ).reshape(tok, 1, lat_count, lanes)
    chosen = named[:, :, :, None]
    latent_codes = jnp.sum(jnp.where(chosen, code_dense, 0.0), axis=2).astype(bf)
    attribution = jnp.sum(jnp.where(chosen, score_dense, 0.0), axis=2)
    return (latent_codes, attribution, recon_error, latent_totals)


def solution(mesh):
    sizes = dict(mesh.shape)

    def on_device(residual, gradient, block_ids, jump_mask, encoder, enc_bias, decoder, dec_bias):
        lanes = jump_mask.shape[2]
        small = (
            sizes["groups"] == 2
            and sizes["seq"] == 2
            and sizes["lat"] in (2, 4, 8, 16)
            and encoder.shape[1] == lanes
            and lanes % 64 == 0
            and residual.shape[1] % 256 == 0
        )
        body = move_weights if small else move_tokens
        return body(
            residual, gradient, block_ids, jump_mask, encoder, enc_bias, decoder, dec_bias
        )

    rows = P(("groups", "lat", "seq"), None)
    cubes = P(("groups", "lat", "seq"), None, None)
    return jax.shard_map(
        on_device,
        mesh=mesh,
        in_specs=(rows, rows, rows, cubes, P(None, "lat"), P("lat"), P("lat", None), P()),
        out_specs=(cubes, cubes, rows, P(("groups", "lat", "seq"))),
        check_vma=False,
    )
```

time: 177 us -> 119 us (0.67)
  blocking collectives: 106 us -> 0 us
  other arithmetic: 6.36 us -> 29.1 us
  waiting for transfers between devices: 35.4 us -> 52.7 us
  starting transfers between devices: 10.6 us -> 20.2 us
  local copies, waits for them, and re-layouts: 12.7 us -> 3.95 us
  matrix products: 3.48 us -> 11.7 us
    all_to_all x3 -> x0, blocking collectives: 60.1 us -> none  [the longest x1 40.6 us: on_device(): lax.all_to_all(residual_slots, 'lat', split_axis=0, concat_axis=0, tiled=...]
    ppermute x0 -> x20, waiting for transfers between devices: none -> 52.7 us  [permute(): return lax.ppermute(values, AXES, pairs)]
    unnamed x1 -> x0, blocking collectives: 45.8 us -> none
    all_to_all x3 -> x0, waiting for transfers between devices: 35.4 us -> none  [the longest x1 29.9 us: on_device(): lax.all_to_all(gradient_slots, 'lat', split_axis=0, concat_axis=0, tiled=...]
    concatenate x0 -> x15, other arithmetic: none -> 23.7 us  [the longest x1 11.7 us: move_weights(): jnp.concatenate([jnp.concatenate([a01, a2], axis=0), jnp.concatenate([b0,...]
    ppermute x0 -> x20, starting transfers between devices: none -> 20.2 us  [permute(): return lax.ppermute(values, AXES, pairs)]
    all_to_all x3 -> x0, starting transfers between devices: 10.6 us -> none  [the longest x1 3.7 us: on_device(): lax.all_to_all(gradient_slots, 'lat', split_axis=0, concat_axis=0, tiled=...]
    dot_general x4 -> x10, matrix products: 3.48 us -> 11.7 us  [the longest x7 4.51 us: nt(): lax.dot_general(a, b, (((1,), (1,)), ((), ())), preferred_element_type=jn...]
  transfers between devices with their start and end apart: 3 -> 20, of which waited for: 2 -> 16; matrix products, arithmetic and copies ran while one was open for 3% -> 18% of each run, Pallas kernels for 0% -> 0%
where the time goes in v1:
time: 119 us
  waiting for transfers between devices  52.7 us (44%)
  other arithmetic  29.1 us (24%)
  starting transfers between devices  20.2 us (17%)
  matrix products  11.7 us (10%)
  local copies, waits for them, and re-layouts  3.95 us (3%)
    ppermute x20, waiting for transfers between devices, permute(): return lax.ppermute(values, AXES, pairs)  52.7 us
    ppermute x20, starting transfers between devices, permute(): return lax.ppermute(values, AXES, pairs)  20.2 us
    concatenate x1, other arithmetic, move_weights(): jnp.concatenate([jnp.concatenate([a01, a2], axis=0), jnp.concatenate([b0,...  11.7 us
    concatenate x1, other arithmetic, move_weights(): rows = jnp.concatenate([mine, by_core(mine)], axis=0)  8.43 us
    dot_general x7, matrix products, nt(): lax.dot_general(a, b, (((1,), (1,)), ((), ())), preferred_element_type=jn...  4.51 us
    dot_general x1, matrix products, move_weights(): jnp.dot(score_src, spread(part // 4, part // 2 % 2), preferred_element_ty...  2.63 us
    dot_general x1, matrix products, move_weights(): jnp.dot(code_src, spread(part // 2 % 2, part // 4), preferred_element_typ...  2.62 us
  transfers between devices with their start and end apart: 20, of which 16 were waited for; matrix products, arithmetic and copies ran while one was open for 18% of the time, Pallas kernels for 0%

profile of v1, /device:TPU:0, one launch (start us, length us, event | category | flops | bytes accessed | tf_op | source)
XLA Modules:
  0.0 118.6 jit_solution(14645628991023372212)
XLA Ops:
  2.7 1.1 fusion.162
  3.8 3.0 %collective-permute-start.2 = (bf16[32,4096]{1,0:T(8,128)(2,1)S(1)}, bf16[32,4096]{1,0:T(8,128)(2,1)S(1)}, u32[]{:S(2)}, u32[]{:S(2)}) collective-permute-start(bf16[32,4096]{1,0:T(8,128)(2,1)S(1)} %pad_maximum_fusion.11), channel_id=1, source_target_pairs={{0,2},{1,3},{2,0},{3,1},{4,6},{5,7},{6,4},{7,5},{8,10},{9,11},{10,... | collective-permute-start | bytes 786440 | tf_op jit(solution)/shard_map/ppermute | solution.py:119
  6.9 1.6 %collective-permute-start = (bf16[32,4096]{1,0:T(8,128)(2,1)S(1)}, bf16[32,4096]{1,0:T(8,128)(2,1)S(1)}, u32[]{:S(2)}, u32[]{:S(2)}) collective-permute-start(bf16[32,4096]{1,0:T(8,128)(2,1)S(1)} %pad_maximum_fusion.10), channel_id=1, source_target_pairs={{0,16},{1,17},{2,18},{3,19},{4,20},{5,21},{6,22},{7,23},{8,24},{9,... | collective-permute-start | bytes 786440 | tf_op jit(solution)/shard_map/ppermute | solution.py:119
  9.2 1.6 %collective-permute-start.8 = (bf16[32,3584]{1,0:T(8,128)(2,1)}, bf16[32,3584]{1,0:T(8,128)(2,1)}, u32[]{:S(2)}, u32[]{:S(2)}) collective-permute-start(bf16[32,3584]{1,0:T(8,128)(2,1)} %constant_dynamic-slice_fusion), channel_id=1, source_target_pairs={{0,4},{1,5},{2,6},{3,7},{4,8},{5,9},{6,10},{7,11},{8,12},{9,13},{1... | collective-permute-start | bytes 688136 | tf_op jit(solution)/shard_map/ppermute | solution.py:119
  10.7 1.6 %convolution_convert_fusion.1 = bf16[32,3584]{1,0:T(8,128)(2,1)S(1)} fusion(bf16[3584,128]{1,0:T(8,128)(2,1)} %param.12, s32[32]{0:T(128)S(1)} %iota_add_fusion), kind=kOutput, calls=%fused_computation.26 | convolution fusion | flops 29478912 | bytes 1147008 | tf_op jit(solution)/shard_map/dot_general | solution.py:93
  13.2 1.8 %collective-permute-start.3 = (bf16[64,4096]{1,0:T(8,128)(2,1)S(1)}, bf16[64,4096]{1,0:T(8,128)(2,1)S(1)}, u32[]{:S(2)}, u32[]{:S(2)}) collective-permute-start(bf16[64,4096]{1,0:T(8,128)(2,1)S(1)} %pad_maximum_fusion.6), channel_id=1, source_target_pairs={{0,16},{1,17},{2,18},{3,19},{4,20},{5,21},{6,22},{7,23},{8,24},{9,... | collective-permute-start | bytes 1572872 | tf_op jit(solution)/shard_map/ppermute | solution.py:119
  15.2 1.6 %collective-permute-start.1 = (bf16[64,4096]{1,0:T(8,128)(2,1)S(1)}, bf16[64,4096]{1,0:T(8,128)(2,1)S(1)}, u32[]{:S(2)}, u32[]{:S(2)}) collective-permute-start(bf16[64,4096]{1,0:T(8,128)(2,1)S(1)} %pad_maximum_fusion.5), channel_id=1, source_target_pairs={{0,2},{1,3},{2,0},{3,1},{4,6},{5,7},{6,4},{7,5},{8,10},{9,11},{10,... | collective-permute-start | bytes 1572872 | tf_op jit(solution)/shard_map/ppermute | solution.py:119
  16.7 9.7 %collective-permute-done.3 = bf16[64,4096]{1,0:T(8,128)(2,1)S(1)} collective-permute-done((bf16[64,4096]{1,0:T(8,128)(2,1)S(1)}, bf16[64,4096]{1,0:T(8,128)(2,1)S(1)}, u32[]{:S(2)}, u32[]{:S(2)}) %collective-permute-start.3) | collective-permute-done | bytes 524320 | tf_op jit(solution)/shard_map/ppermute | solution.py:119
  26.4 1.3 %collective-permute-done.1 = bf16[64,4096]{1,0:T(8,128)(2,1)S(1)} collective-permute-done((bf16[64,4096]{1,0:T(8,128)(2,1)S(1)}, bf16[64,4096]{1,0:T(8,128)(2,1)S(1)}, u32[]{:S(2)}, u32[]{:S(2)}) %collective-permute-start.1) | collective-permute-done | bytes 524320 | tf_op jit(solution)/shard_map/ppermute | solution.py:119
  27.7 11.7 %maximum_maximum_fusion = bf16[128,8192]{1,0:T(8,128)(2,1)} fusion(bf16[32,4096]{1,0:T(8,128)(2,1)S(1)} %get-tuple-element.13, bf16[32,4096]{1,0:T(8,128)(2,1)S(1)} %collective-permute-done.2, bf16[32,4096]{1,0:T(8,128)(2,1)S(1)} %get-tuple-element.12, bf16[32,512]{1,0:T(8,128)(2,1)S(1)} %get-tuple-element.23, bf16[32,1792]{1,0:T(8,128)(2,1)S(1)} %get-tuple-element.31, ...), kind=kLoop, calls=%fused_computation.51 | loop fusion | flops 23068672 | bytes 4194304 | tf_op jit(solution)/shard_map/concatenate | solution.py:164
  39.6 1.7 %collective-permute-start.5 = (bf16[32,3712]{1,0:T(8,128)(2,1)S(1)}, bf16[32,3712]{1,0:T(8,128)(2,1)S(1)}, u32[]{:S(2)}, u32[]{:S(2)}) collective-permute-start(bf16[32,3712]{1,0:T(8,128)(2,1)S(1)} %pad_maximum_fusion.12), channel_id=1, source_target_pairs={{0,4},{1,5},{2,6},{3,7},{4,8},{5,9},{6,10},{7,11},{8,12},{9,13},{1... | collective-permute-start | bytes 712712 | tf_op jit(solution)/shard_map/ppermute | solution.py:119
  41.3 1.6 %collective-permute-start.9 = (bf16[32,3584]{1,0:T(8,128)(2,1)}, bf16[32,3584]{1,0:T(8,128)(2,1)}, u32[]{:S(2)}, u32[]{:S(2)}) collective-permute-start(bf16[32,3584]{1,0:T(8,128)(2,1)} %collective-permute-done.8), channel_id=1, source_target_pairs={{0,4},{1,5},{2,6},{3,7},{4,8},{5,9},{6,10},{7,11},{8,12},{9,13},{1... | collective-permute-start | bytes 688136 | tf_op jit(solution)/shard_map/ppermute | solution.py:119
  42.9 7.2 %collective-permute-done.5 = bf16[32,3712]{1,0:T(8,128)(2,1)S(1)} collective-permute-done((bf16[32,3712]{1,0:T(8,128)(2,1)S(1)}, bf16[32,3712]{1,0:T(8,128)(2,1)S(1)}, u32[]{:S(2)}, u32[]{:S(2)}) %collective-permute-start.5) | collective-permute-done | bytes 237600 | tf_op jit(solution)/shard_map/ppermute | solution.py:119
  50.1 5.0 %collective-permute-done.9 = bf16[32,3584]{1,0:T(8,128)(2,1)} collective-permute-done((bf16[32,3584]{1,0:T(8,128)(2,1)}, bf16[32,3584]{1,0:T(8,128)(2,1)}, u32[]{:S(2)}, u32[]{:S(2)}) %collective-permute-start.9) | collective-permute-done | bytes 229408 | tf_op jit(solution)/shard_map/ppermute | solution.py:119
  55.1 5.2 %collective-permute-done.6 = bf16[32,3712]{1,0:T(8,128)(2,1)} collective-permute-done((bf16[32,3712]{1,0:T(8,128)(2,1)S(1)}, bf16[32,3712]{1,0:T(8,128)(2,1)}, u32[]{:S(2)}, u32[]{:S(2)}) %collective-permute-start.6) | collective-permute-done | bytes 237600 | tf_op jit(solution)/shard_map/ppermute | solution.py:119
  60.4 5.2 %collective-permute-done.10 = bf16[32,3584]{1,0:T(8,128)(2,1)} collective-permute-done((bf16[32,3584]{1,0:T(8,128)(2,1)}, bf16[32,3584]{1,0:T(8,128)(2,1)}, u32[]{:S(2)}, u32[]{:S(2)}) %collective-permute-start.10) | collective-permute-done | bytes 229408 | tf_op jit(solution)/shard_map/ppermute | solution.py:119
  65.6 1.3 %pad_maximum_fusion.4 = bf16[128,3584]{1,0:T(8,128)(2,1)S(1)} fusion(bf16[32,3584]{1,0:T(8,128)(2,1)} %collective-permute-done.10, bf16[32,3584]{1,0:T(8,128)(2,1)} %collective-permute-done.9, bf16[32,3584]{1,0:T(8,128)(2,1)} %collective-permute-done.8, bf16[32,3584]{1,0:T(8,128)(2,1)} %constant_dynamic-slice_fusion), kind=kLoop, calls=%fused_computation.76 | loop fusion | flops 3670016 | bytes 1835008 | tf_op jit(solution)/shard_map/concatenate | solution.py:149
  67.0 2.8 %collective-permute-done.7 = bf16[32,3712]{1,0:T(8,128)(2,1)S(1)} collective-permute-done((bf16[32,3712]{1,0:T(8,128)(2,1)}, bf16[32,3712]{1,0:T(8,128)(2,1)S(1)}, u32[]{:S(2)}, u32[]{:S(2)}) %collective-permute-start.7) | collective-permute-done | bytes 237600 | tf_op jit(solution)/shard_map/ppermute | solution.py:119
  71.7 8.4 %pad_maximum_fusion = bf16[256,8192]{1,0:T(8,128)(2,1)S(1)} fusion(bf16[128,8192]{1,0:T(8,128)(2,1)} %collective-permute-done.4, bf16[32,4096]{1,0:T(8,128)(2,1)S(1)} %get-tuple-element.13, bf16[32,4096]{1,0:T(8,128)(2,1)S(1)} %collective-permute-done.2, bf16[32,4096]{1,0:T(8,128)(2,1)S(1)} %get-tuple-element.12, bf16[32,512]{1,0:T(8,128)(2,1)S(1)} %get-tuple-element.23, ...), kind=kLoop, calls=%fused_computation.42 | loop fusion | flops 50331648 | bytes 8388608 | tf_op jit(solution)/shard_map/concatenate | solution.py:171
  82.2 1.9 %convolution_convert_fusion = bf16[256,3584]{1,0:T(8,128)(2,1)S(1)} fusion(bf16[256,128]{1,0:T(8,128)(2,1)S(1)} %fusion.72, bf16[32,3584]{1,0:T(8,128)(2,1)} %collective-permute-done.10, bf16[32,3584]{1,0:T(8,128)(2,1)} %collective-permute-done.9, bf16[32,3584]{1,0:T(8,128)(2,1)} %collective-permute-done.8, bf16[32,3584]{1,0:T(8,128)(2,1)} %constant_dynamic-slice_fusion), kind=kOutput, calls=%fused_computation.25 | convolution fusion | flops 239468544 | bytes 2818048 | tf_op jit(solution)/shard_map/dot_general | solution.py:195
  85.2 1.8 %collective-permute-start.16 = (f32[2,128]{1,0:T(2,128)S(1)}, f32[2,128]{1,0:T(2,128)S(1)}, u32[]{:S(2)}, u32[]{:S(2)}) collective-permute-start(f32[2,128]{1,0:T(2,128)S(1)} %reduce_sum.39), channel_id=1, source_target_pairs={{0,12},{1,13},{2,14},{3,15},{4,0},{5,1},{6,2},{7,3},{8,4},{9,5},{1... | collective-permute-start | bytes 3080 | tf_op jit(solution)/shard_map/ppermute | solution.py:119
  88.9 2.6 %collective-permute-done.17 = f32[2,128]{1,0:T(2,128)S(1)} collective-permute-done((f32[2,128]{1,0:T(2,128)S(1)}, f32[2,128]{1,0:T(2,128)S(1)}, u32[]{:S(2)}, u32[]{:S(2)}) %collective-permute-start.17) | collective-permute-done | bytes 1056 | tf_op jit(solution)/shard_map/ppermute | solution.py:119
  92.5 1.1 collective-permute-start.19
  93.6 2.5 %collective-permute-done.19 = f32[32]{0:T(128)S(1)} collective-permute-done((f32[32]{0:T(128)S(1)}, f32[32]{0:T(128)S(1)}, u32[]{:S(2)}, u32[]{:S(2)}) %collective-permute-start.19) | collective-permute-done | bytes 160 | tf_op jit(solution)/shard_map/ppermute | solution.py:119
  96.6 1.4 %convert_add_fusion = f32[128,3584]{1,0:T(8,128)S(1)} fusion(bf16[128,3840]{1,0:T(8,128)(2,1)} %collective-permute-done.11, bf16[256,3584]{1,0:T(8,128)(2,1)S(1)} %convolution_convert_fusion), kind=kLoop, calls=%fused_computation.60 | loop fusion | flops 1376256 | bytes 3670016 | tf_op jit(solution)/shard_map/add | solution.py:212
  99.0 1.6 %collective-permute-start.12 = (bf16[64,2048]{1,0:T(8,128)(2,1)S(1)}, bf16[64,2048]{1,0:T(8,128)(2,1)S(1)}, u32[]{:S(2)}, u32[]{:S(2)}) collective-permute-start(bf16[64,2048]{1,0:T(8,128)(2,1)S(1)} %pad_maximum_fusion.8), channel_id=1, source_target_pairs={{0,2},{1,3},{2,0},{3,1},{4,6},{5,7},{6,4},{7,5},{8,10},{9,11},{10,... | collective-permute-start | bytes 786440 | tf_op jit(solution)/shard_map/ppermute | solution.py:119
  101.2 4.2 %collective-permute-done.12 = bf16[64,2048]{1,0:T(8,128)(2,1)S(1)} collective-permute-done((bf16[64,2048]{1,0:T(8,128)(2,1)S(1)}, bf16[64,2048]{1,0:T(8,128)(2,1)S(1)}, u32[]{:S(2)}, u32[]{:S(2)}) %collective-permute-start.12) | collective-permute-done | bytes 262176 | tf_op jit(solution)/shard_map/ppermute | solution.py:119
  105.5 1.1 collective-permute-start.13
  106.7 2.0 %collective-permute-done.14 = bf16[2,32,2048]{2,1,0:T(8,128)(2,1)S(1)} collective-permute-done((bf16[2,32,2048]{2,1,0:T(8,128)(2,1)S(1)}, bf16[2,32,2048]{2,1,0:T(8,128)(2,1)S(1)}, u32[]{:S(2)}, u32[]{:S(2)}) %collective-permute-start.14) | collective-permute-done | bytes 262176 | tf_op jit(solution)/shard_map/ppermute | solution.py:119
  108.9 1.8 %collective-permute-done.13 = bf16[32,2304]{1,0:T(8,128)(2,1)S(1)} collective-permute-done((bf16[32,2304]{1,0:T(8,128)(2,1)S(1)}, bf16[32,2304]{1,0:T(8,128)(2,1)S(1)}, u32[]{:S(2)}, u32[]{:S(2)}) %collective-permute-start.13) | collective-permute-done | bytes 147488 | tf_op jit(solution)/shard_map/ppermute | solution.py:119
  110.8 2.6 %fusion.34 = f32[4,8,8,128]{3,1,2,0:T(8,128)S(1)} fusion(s32[]{:T(128)S(6)} %axis_index.35, s32[]{:T(128)S(6)} %select_n.121, s32[1024]{0:T(1024)S(1)} %get-tuple-element.39, s32[1024]{0:T(1024)S(1)} %get-tuple-element.42, pred[1024]{0:T(1024)(128)(4,1)S(1)} %get-tuple-element.43, s32[]{:T(128)S(6)} %axis_index.32, s32[1024]{0:T(1024)S(1)} %get-tuple-element.40, ...), kind=kOutput, calls=%fused_computation.62 | convolution fusion | flops 156368896 | bytes 215056 | tf_op jit(solution)/shard_map/dot_general | solution.py:247
  114.0 2.6 %fusion.33 = f32[4,8,8,128]{3,1,2,0:T(8,128)S(1)} fusion(s32[]{:T(128)S(6)} %axis_index.35, s32[]{:T(128)S(6)} %select_n.121, s32[1024]{0:T(1024)S(1)} %get-tuple-element.39, s32[1024]{0:T(1024)S(1)} %get-tuple-element.42, pred[1024]{0:T(1024)(128)(4,1)S(1)} %get-tuple-element.43, s32[]{:T(128)S(6)} %axis_index.32, s32[1024]{0:T(1024)S(1)} %get-tuple-element.40, ...), kind=kOutput, calls=%fused_computation.61 | convolution fusion | flops 156368896 | bytes 215056 | tf_op jit(solution)/shard_map/dot_general | solution.py:250
  (90 shorter events, 16.9 us)
Async XLA Ops:
  0.6 7.8 %copy-start = (bf16[128,3584]{1,0:T(8,128)(2,1)S(1)}, bf16[128,3584]{1,0:T(8,128)(2,1)}, u32[]{:S(2)}) copy-start(bf16[128,3584]{1,0:T(8,128)(2,1)} %param.14) | copy-start | bytes 2752516
  0.6 14.4 %copy-start.3 = (f32[128]{0:T(128)S(1)}, f32[128]{0:T(128)}, u32[]{:S(2)}) copy-start(f32[128]{0:T(128)} %param.13) | copy-start | bytes 1540
  3.8 9.3 %collective-permute-start.2 = (bf16[32,4096]{1,0:T(8,128)(2,1)S(1)}, bf16[32,4096]{1,0:T(8,128)(2,1)S(1)}, u32[]{:S(2)}, u32[]{:S(2)}) collective-permute-start(bf16[32,4096]{1,0:T(8,128)(2,1)S(1)} %pad_maximum_fusion.11), channel_id=1, source_target_pairs={{0,2},{1,3},{2,0},{3,1},{4,6},{5,7},{6,4},{7,5},{8,10},{9,11},{10,... | collective-permute-start | bytes 786440 | tf_op jit(solution)/shard_map/ppermute | solution.py:119
  6.9 8.2 %collective-permute-start = (bf16[32,4096]{1,0:T(8,128)(2,1)S(1)}, bf16[32,4096]{1,0:T(8,128)(2,1)S(1)}, u32[]{:S(2)}, u32[]{:S(2)}) collective-permute-start(bf16[32,4096]{1,0:T(8,128)(2,1)S(1)} %pad_maximum_fusion.10), channel_id=1, source_target_pairs={{0,16},{1,17},{2,18},{3,19},{4,20},{5,21},{6,22},{7,23},{8,24},{9,... | collective-permute-start | bytes 786440 | tf_op jit(solution)/shard_map/ppermute | solution.py:119
  9.2 32.1 %collective-permute-start.8 = (bf16[32,3584]{1,0:T(8,128)(2,1)}, bf16[32,3584]{1,0:T(8,128)(2,1)}, u32[]{:S(2)}, u32[]{:S(2)}) collective-permute-start(bf16[32,3584]{1,0:T(8,128)(2,1)} %constant_dynamic-slice_fusion), channel_id=1, source_target_pairs={{0,4},{1,5},{2,6},{3,7},{4,8},{5,9},{6,10},{7,11},{8,12},{9,13},{1... | collective-permute-start | bytes 688136 | tf_op jit(solution)/shard_map/ppermute | solution.py:119
  13.2 13.2 %collective-permute-start.3 = (bf16[64,4096]{1,0:T(8,128)(2,1)S(1)}, bf16[64,4096]{1,0:T(8,128)(2,1)S(1)}, u32[]{:S(2)}, u32[]{:S(2)}) collective-permute-start(bf16[64,4096]{1,0:T(8,128)(2,1)S(1)} %pad_maximum_fusion.6), channel_id=1, source_target_pairs={{0,16},{1,17},{2,18},{3,19},{4,20},{5,21},{6,22},{7,23},{8,24},{9,... | collective-permute-start | bytes 1572872 | tf_op jit(solution)/shard_map/ppermute | solution.py:119
  15.2 12.6 %collective-permute-start.1 = (bf16[64,4096]{1,0:T(8,128)(2,1)S(1)}, bf16[64,4096]{1,0:T(8,128)(2,1)S(1)}, u32[]{:S(2)}, u32[]{:S(2)}) collective-permute-start(bf16[64,4096]{1,0:T(8,128)(2,1)S(1)} %pad_maximum_fusion.5), channel_id=1, source_target_pairs={{0,2},{1,3},{2,0},{3,1},{4,6},{5,7},{6,4},{7,5},{8,10},{9,11},{10,... | collective-permute-start | bytes 1572872 | tf_op jit(solution)/shard_map/ppermute | solution.py:119
  39.4 32.3 %collective-permute-start.4 = (bf16[128,8192]{1,0:T(8,128)(2,1)}, bf16[128,8192]{1,0:T(8,128)(2,1)}, u32[]{:S(2)}, u32[]{:S(2)}) collective-permute-start(bf16[128,8192]{1,0:T(8,128)(2,1)} %maximum_maximum_fusion), channel_id=1, source_target_pairs={{0,1},{1,0},{2,3},{3,2},{4,5},{5,4},{6,7},{7,6},{8,9},{9,8},{10,11... | collective-permute-start | bytes 6291464 | tf_op jit(solution)/shard_map/ppermute | solution.py:119
  39.6 10.5 %collective-permute-start.5 = (bf16[32,3712]{1,0:T(8,128)(2,1)S(1)}, bf16[32,3712]{1,0:T(8,128)(2,1)S(1)}, u32[]{:S(2)}, u32[]{:S(2)}) collective-permute-start(bf16[32,3712]{1,0:T(8,128)(2,1)S(1)} %pad_maximum_fusion.12), channel_id=1, source_target_pairs={{0,4},{1,5},{2,6},{3,7},{4,8},{5,9},{6,10},{7,11},{8,12},{9,13},{1... | collective-permute-start | bytes 712712 | tf_op jit(solution)/shard_map/ppermute | solution.py:119
  41.3 13.8 %collective-permute-start.9 = (bf16[32,3584]{1,0:T(8,128)(2,1)}, bf16[32,3584]{1,0:T(8,128)(2,1)}, u32[]{:S(2)}, u32[]{:S(2)}) collective-permute-start(bf16[32,3584]{1,0:T(8,128)(2,1)} %collective-permute-done.8), channel_id=1, source_target_pairs={{0,4},{1,5},{2,6},{3,7},{4,8},{5,9},{6,10},{7,11},{8,12},{9,13},{1... | collective-permute-start | bytes 688136 | tf_op jit(solution)/shard_map/ppermute | solution.py:119
  50.1 10.3 %collective-permute-start.6 = (bf16[32,3712]{1,0:T(8,128)(2,1)S(1)}, bf16[32,3712]{1,0:T(8,128)(2,1)}, u32[]{:S(2)}, u32[]{:S(2)}) collective-permute-start(bf16[32,3712]{1,0:T(8,128)(2,1)S(1)} %collective-permute-done.5), channel_id=1, source_target_pairs={{0,4},{1,5},{2,6},{3,7},{4,8},{5,9},{6,10},{7,11},{8,12},{9,13},{1... | collective-permute-start | bytes 712712 | tf_op jit(solution)/shard_map/ppermute | solution.py:119
  55.1 10.5 %collective-permute-start.10 = (bf16[32,3584]{1,0:T(8,128)(2,1)}, bf16[32,3584]{1,0:T(8,128)(2,1)}, u32[]{:S(2)}, u32[]{:S(2)}) collective-permute-start(bf16[32,3584]{1,0:T(8,128)(2,1)} %collective-permute-done.9), channel_id=1, source_target_pairs={{0,4},{1,5},{2,6},{3,7},{4,8},{5,9},{6,10},{7,11},{8,12},{9,13},{1... | collective-permute-start | bytes 688136 | tf_op jit(solution)/shard_map/ppermute | solution.py:119
  60.4 9.4 %collective-permute-start.7 = (bf16[32,3712]{1,0:T(8,128)(2,1)}, bf16[32,3712]{1,0:T(8,128)(2,1)S(1)}, u32[]{:S(2)}, u32[]{:S(2)}) collective-permute-start(bf16[32,3712]{1,0:T(8,128)(2,1)} %collective-permute-done.6), channel_id=1, source_target_pairs={{0,4},{1,5},{2,6},{3,7},{4,8},{5,9},{6,10},{7,11},{8,12},{9,13},{1... | collective-permute-start | bytes 712712 | tf_op jit(solution)/shard_map/ppermute | solution.py:119
  85.2 11.4 %collective-permute-start.11 = (bf16[128,3840]{1,0:T(8,128)(2,1)}, bf16[128,3840]{1,0:T(8,128)(2,1)}, u32[]{:S(2)}, u32[]{:S(2)}) collective-permute-start(bf16[128,3840]{1,0:T(8,128)(2,1)} %pad_maximum_fusion.1), channel_id=1, source_target_pairs={{0,1},{1,0},{2,3},{3,2},{4,5},{5,4},{6,7},{7,6},{8,9},{9,8},{10,11... | collective-permute-start | bytes 2949128 | tf_op jit(solution)/shard_map/ppermute | solution.py:119
  85.2 3.6 %collective-permute-start.16 = (f32[2,128]{1,0:T(2,128)S(1)}, f32[2,128]{1,0:T(2,128)S(1)}, u32[]{:S(2)}, u32[]{:S(2)}) collective-permute-start(f32[2,128]{1,0:T(2,128)S(1)} %reduce_sum.39), channel_id=1, source_target_pairs={{0,12},{1,13},{2,14},{3,15},{4,0},{5,1},{6,2},{7,3},{8,4},{9,5},{1... | collective-permute-start | bytes 3080 | tf_op jit(solution)/shard_map/ppermute | solution.py:119
  87.0 4.5 %collective-permute-start.17 = (f32[2,128]{1,0:T(2,128)S(1)}, f32[2,128]{1,0:T(2,128)S(1)}, u32[]{:S(2)}, u32[]{:S(2)}) collective-permute-start(f32[2,128]{1,0:T(2,128)S(1)} %reduce_sum.39), channel_id=1, source_target_pairs={{0,8},{1,9},{2,10},{3,11},{4,12},{5,13},{6,14},{7,15},{8,0},{9,1},... | collective-permute-start | bytes 3080 | tf_op jit(solution)/shard_map/ppermute | solution.py:119
  87.0 5.4 %collective-permute-start.18 = (f32[2,128]{1,0:T(2,128)S(1)}, f32[2,128]{1,0:T(2,128)S(1)}, u32[]{:S(2)}, u32[]{:S(2)}) collective-permute-start(f32[2,128]{1,0:T(2,128)S(1)} %reduce_sum.39), channel_id=1, source_target_pairs={{0,4},{1,5},{2,6},{3,7},{4,8},{5,9},{6,10},{7,11},{8,12},{9,13},{1... | collective-permute-start | bytes 3080 | tf_op jit(solution)/shard_map/ppermute | solution.py:119
  92.5 3.5 %collective-permute-start.19 = (f32[32]{0:T(128)S(1)}, f32[32]{0:T(128)S(1)}, u32[]{:S(2)}, u32[]{:S(2)}) collective-permute-start(f32[32]{0:T(128)S(1)} %get-tuple-element.25), channel_id=1, source_target_pairs={{0,16},{1,17},{2,18},{3,19},{4,20},{5,21},{6,22},{7,23},{8,24},{9,... | collective-permute-start | bytes 392 | tf_op jit(solution)/shard_map/ppermute | solution.py:119
  99.0 6.4 %collective-permute-start.12 = (bf16[64,2048]{1,0:T(8,128)(2,1)S(1)}, bf16[64,2048]{1,0:T(8,128)(2,1)S(1)}, u32[]{:S(2)}, u32[]{:S(2)}) collective-permute-start(bf16[64,2048]{1,0:T(8,128)(2,1)S(1)} %pad_maximum_fusion.8), channel_id=1, source_target_pairs={{0,2},{1,3},{2,0},{3,1},{4,6},{5,7},{6,4},{7,5},{8,10},{9,11},{10,... | collective-permute-start | bytes 786440 | tf_op jit(solution)/shard_map/ppermute | solution.py:119
  100.7 8.0 %collective-permute-start.14 = (bf16[2,32,2048]{2,1,0:T(8,128)(2,1)S(1)}, bf16[2,32,2048]{2,1,0:T(8,128)(2,1)S(1)}, u32[]{:S(2)}, u32[]{:S(2)}) collective-permute-start(bf16[2,32,2048]{2,1,0:T(8,128)(2,1)S(1)} %slice_bitcast_fusion.1), channel_id=1, source_target_pairs={{0,16},{1,17},{2,18},{3,19},{4,20},{5,21},{6,22},{7,23},{8,24},{9,... | collective-permute-start | bytes 786440 | tf_op jit(solution)/shard_map/ppermute | solution.py:119
  105.5 5.2 %collective-permute-start.13 = (bf16[32,2304]{1,0:T(8,128)(2,1)S(1)}, bf16[32,2304]{1,0:T(8,128)(2,1)S(1)}, u32[]{:S(2)}, u32[]{:S(2)}) collective-permute-start(bf16[32,2304]{1,0:T(8,128)(2,1)S(1)} %pad_maximum_fusion.13), channel_id=1, source_target_pairs={{0,16},{1,17},{2,18},{3,19},{4,20},{5,21},{6,22},{7,23},{8,24},{9,... | collective-permute-start | bytes 442376 | tf_op jit(solution)/shard_map/ppermute | solution.py:119
  108.8 5.2 %collective-permute-start.15 = (bf16[32,2304]{1,0:T(8,128)(2,1)S(1)}, bf16[32,2304]{1,0:T(8,128)(2,1)S(1)}, u32[]{:S(2)}, u32[]{:S(2)}) collective-permute-start(bf16[32,2304]{1,0:T(8,128)(2,1)S(1)} %pad_maximum_fusion.14), channel_id=1, source_target_pairs={{0,2},{1,3},{2,0},{3,1},{4,6},{5,7},{6,4},{7,5},{8,10},{9,11},{10,... | collective-permute-start | bytes 442376 | tf_op jit(solution)/shard_map/ppermute | solution.py:119
  114.0 3.8 %copy-start.1 = (bf16[32,3584]{1,0:T(8,128)(2,1)S(1)}, bf16[32,3584]{1,0:T(8,128)(2,1)}, u32[]{:S(2)}) copy-start(bf16[32,3584]{1,0:T(8,128)(2,1)} %param.8) | copy-start | bytes 688132
  114.0 3.8 %copy-start.2 = (f32[3584]{0:T(1024)S(1)}, f32[3584]{0:T(1024)}, u32[]{:S(2)}) copy-start(f32[3584]{0:T(1024)} %param.15) | copy-start | bytes 43012

commit v2 on v0

v2 whole, which is shorter than its diff:
```python
import functools

import jax
import jax.numpy as jnp
from jax import lax
from jax.experimental import pallas as pl
from jax.experimental.pallas import tpu as pltpu
from jax.sharding import PartitionSpec as P

AXES = ("groups", "lat", "seq")


def place_rows(values, source, filled, leading):
    picked = jnp.where(filled[:, None], values[source], jnp.zeros((), values.dtype))
    return picked.reshape(leading + (values.shape[-1],))


def move_tokens(residual, gradient, block_ids, jump_mask, encoder, enc_bias, decoder, dec_bias):
    tok_rows, width = residual.shape
    active = block_ids.shape[1]
    lanes = jump_mask.shape[2]
    lat_count = lax.axis_size("lat")
    seq_count = lax.axis_size("seq")
    local_blocks = encoder.shape[1] // lanes
    block_count = local_blocks * lat_count
    capacity = max(
        2, min(tok_rows, (3 * tok_rows * active + 2 * block_count - 1) // (2 * block_count))
    )
    slot_count = tok_rows * active
    flat_blocks = block_ids.reshape(slot_count)
    one_hot = (flat_blocks[:, None] == jnp.arange(block_count, dtype=jnp.int32)[None, :]).astype(
        jnp.int32
    )
    earlier = jnp.sum(jnp.cumsum(one_hot, axis=0) * one_hot, axis=1) - 1
    slot_id = flat_blocks * capacity + earlier
    owner_row = (
        jnp.zeros((block_count * capacity,), jnp.int32)
        .at[slot_id]
        .set(jnp.arange(slot_count, dtype=jnp.int32) + 1)
    )
    filled = owner_row > 0
    slot_source = jnp.maximum(owner_row - 1, 0)
    token_source = slot_source // active
    leading = (lat_count, local_blocks, capacity)
    enc_blocks = encoder.reshape(width, local_blocks, lanes)
    dec_blocks = decoder.reshape(local_blocks, lanes, width)
    bias_blocks = enc_bias.reshape(1, local_blocks, 1, lanes)
    mask_values = jump_mask.astype(jnp.float32)
    total_tokens = tok_rows * lat_count * seq_count
    factor = (total_tokens * active / block_count) ** (-0.5)

    def gather_home(slotted):
        last = slotted.shape[-1]
        return slotted.reshape(block_count * capacity, last)[slot_id].reshape(
            tok_rows, active, last
        )

    def swap(values):
        return lax.all_to_all(values, "lat", split_axis=0, concat_axis=0, tiled=True)

    residual_slots = place_rows(residual, token_source, filled, leading)
    gradient_slots = place_rows(gradient, token_source, filled, leading)
    preact = jnp.einsum(
        "sbcd,dbj->sbcj", swap(residual_slots), enc_blocks, preferred_element_type=jnp.float32
    )
    preact = swap((preact + bias_blocks).astype(jnp.bfloat16)).astype(jnp.float32)
    latent_codes = (gather_home(preact) * mask_values).astype(jnp.bfloat16)
    code_slots = place_rows(latent_codes.reshape(slot_count, lanes), slot_source, filled, leading)
    code_data = swap(code_slots)
    grad_data = swap(gradient_slots)
    score_data = code_data.astype(jnp.float32) * jnp.einsum(
        "sbcd,bjd->sbcj", grad_data, dec_blocks, preferred_element_type=jnp.float32
    )
    recon_data = jnp.einsum(
        "sbcj,bjd->sbcd", code_data, dec_blocks, preferred_element_type=jnp.float32
    )
    recon_home = gather_home(swap(recon_data.astype(jnp.bfloat16)))
    attribution = gather_home(swap(score_data))
    recon_error = (
        residual.astype(jnp.float32) - dec_bias - jnp.sum(recon_home.astype(jnp.float32), axis=1)
    ).astype(jnp.bfloat16)
    term = jnp.dot(
        one_hot.T.astype(jnp.float32),
        attribution.reshape(slot_count, lanes),
        precision=lax.Precision.HIGHEST,
    )
    latent_totals = (
        lax.psum_scatter(
            term.reshape(block_count * lanes), ("lat", "seq"), scatter_dimension=0, tiled=True
        )
        * factor
    )
    return (latent_codes, attribution, recon_error, latent_totals)


BF = jnp.bfloat16
F32 = jnp.float32


def nt(a, b):
    return lax.dot_general(a, b, (((1,), (1,)), ((), ())), preferred_element_type=F32)


def call(kernel, outs, *args, flops=0, size=1 << 20):
    whole = pl.BlockSpec(memory_space=pltpu.VMEM)
    smem = pl.BlockSpec(memory_space=pltpu.SMEM)
    return pl.pallas_call(
        kernel,
        in_specs=[smem] + [whole] * (len(args) - 1),
        out_specs=[whole] * len(outs),
        out_shape=[jax.ShapeDtypeStruct(*o) for o in outs],
        compiler_params=pltpu.CompilerParams(vmem_limit_bytes=48 << 20),
        cost_estimate=pl.CostEstimate(flops=flops, bytes_accessed=size, transcendentals=0),
    )(*args)


def weights_kernel(place, enc, dec, bias, enc_out, dec_out):
    per, lanes = enc_out.shape[0], enc.shape[1]
    half = dec_out.shape[1]
    row = lax.broadcasted_iota(jnp.int32, (per, lanes), 0)
    lane = lax.broadcasted_iota(jnp.int32, (per, lanes), 1)
    pick = (lane == row + per * place[1]).astype(BF)
    enc_out[:, :half] = nt(pick, enc[...]).astype(BF)
    b = bias[...]
    hi = b.astype(BF).astype(F32)
    mid = (b - hi).astype(BF).astype(F32)
    low = b - hi - mid
    term = lax.broadcasted_iota(jnp.int32, (lanes, lanes), 0)
    terms = jnp.where(term == 0, hi, jnp.where(term == 1, mid, jnp.where(term == 2, low, 0.0)))
    enc_out[:, half:] = nt(pick, terms.astype(BF)).astype(BF)
    dec_out[...] = dec[...]


def target_block(lane, m, place, x_rel, ring):
    turn = place[2] - 2 * m - (lane >= 64).astype(jnp.int32)
    turn = jnp.where(turn < 0, turn + ring, turn)
    return turn * 2 + (place[0] ^ x_rel)


def tokens_kernel(ring, place, res, grad, ids, jump, keep, send):
    tok, width = res.shape
    half = width // 2
    active = ids.shape[1]
    here = pl.multiple_of(place[3] * half, 128)
    there = pl.multiple_of((1 - place[3]) * half, 128)
    keep[:, :half] = res[:, pl.ds(here, half)]
    keep[:, half:width] = grad[:, pl.ds(here, half)]
    send[:, :half] = res[:, pl.ds(there, half)]
    send[:, half:width] = grad[:, pl.ds(there, half)]
    lane = lax.broadcasted_iota(jnp.int32, (tok, 128), 1)
    low = lane < 64
    plain = [jump[:, k, :] for k in range(active)]
    moved = [pltpu.roll(v, 64, 1) for v in plain]
    for dest in range(4):
        x_rel, y_rel = dest % 2, dest // 2
        first = (place[1] ^ y_rel) == 0
        for m in range(ring // 2):
            tgt = target_block(lane, m, place, x_rel, ring)
            total = jnp.zeros((tok, 128), jnp.int32)
            for k in range(active):
                value = jnp.where(low == first, plain[k], moved[k])
                total = total + jnp.where(ids[:, k : k + 1] == tgt, value, 0)
            at = width + (dest * (ring // 2) + m) * 128
            out = total.astype(F32).astype(BF)
            keep[:, at : at + 128] = out
            send[:, at : at + 128] = out


def rows_kernel(place, keep, got, *outs):
    tok = keep.shape[0]
    width = outs[0].shape[1]
    names = (keep.shape[1] - width) // 3
    width = width - names
    for dest, out in enumerate(outs):
        at = width + (dest + 1) * names
        for i, src in enumerate((keep, got)):
            out[i * tok : (i + 1) * tok, :width] = src[:, :width]
            out[i * tok : (i + 1) * tok, width:] = src[:, at : at + names]


def preact_kernel(ring, half, place, keep, got, from_x, from_y, from_d, *refs):
    parts, out = refs[:ring], refs[ring]
    tok = keep.shape[0]
    per = parts[0].shape[0]
    weights = jnp.concatenate([p[:, :half] for p in parts], axis=0)
    extra = jnp.concatenate([p[:, half:] for p in parts], axis=0)
    ones = jnp.where(place[3] == 0, 1.0, 0.0) * jnp.ones((8, 128), F32)
    bias = nt(ones.astype(BF), extra)[:1]
    at = 0
    for src in (keep, got, from_x, from_y, from_d):
        n = src.shape[0]
        out[at : at + n] = nt(src[:, :half], weights) + bias
        at += n


def codes_kernel(place, mine, other, keep, got, from_x, from_y, from_d, out):
    tok = keep.shape[0]
    names = out.shape[1]
    base = keep.shape[1] - 4 * names
    for chip, src in enumerate((None, from_x, from_y, from_d)):
        for i in range(2):
            at = (2 * chip + i) * tok
            swapped = (2 * chip + 1 - i) * tok
            if chip == 0:
                mask = (keep, got)[i][:, base : base + names]
            else:
                mask = src[i * tok : (i + 1) * tok, base:]
            total = mine[at : at + tok] + other[swapped : swapped + tok]
            out[at : at + tok] = (total * mask.astype(F32)).astype(BF)


def recon_kernel(ring, half, place, codes, keep, got, from_x, from_y, from_d, *refs):
    parts = refs[:ring]
    own_recon, own_proj, sums = refs[ring : ring + 3]
    sends = refs[ring + 3 :]
    tok = keep.shape[0]
    names = codes.shape[1]
    weights = jnp.concatenate([p[...] for p in parts], axis=0)
    totals = []
    for chip, src in enumerate((None, from_x, from_y, from_d)):
        at = chip * 2 * tok
        code = codes[at : at + 2 * tok]
        recon = jnp.dot(code, weights, preferred_element_type=F32)
        if chip == 0:
            proj = jnp.concatenate(
                [nt(v[:, half : 2 * half], weights) for v in (keep, got)], axis=0
            )
            own_recon[...] = recon
            own_proj[...] = proj
        else:
            proj = nt(src[:, half : 2 * half], weights)
            out = sends[chip - 1]
            out[:, :half] = recon.astype(BF)
            out[:, half : half + names] = proj.astype(BF)
            out[:tok, half + names :] = code[:tok, : names // 2]
            out[tok:, half + names :] = code[:tok, names // 2 :]
        totals.append(jnp.sum(code.astype(F32) * proj, axis=0, keepdims=True))
    sums[...] = jnp.concatenate(
        [totals[0] + totals[1], totals[2] + totals[3], jnp.zeros((6, names), F32)], axis=0
    )


def home_kernel(half, names, place, own_recon, own_proj, from_x, from_y, from_d, kept, send):
    tok = kept.shape[0]
    others = (from_x, from_y, from_d)
    total = own_recon[...]
    for src in others:
        total = total + src[:, :half].astype(F32)
    kept[...] = total[:tok]
    send[:, :half] = total[tok:].astype(BF)
    send[:, half : half + names] = own_proj[tok:].astype(BF)
    for i, src in enumerate(others):
        at = half + (i + 1) * names
        send[:, at : at + names] = src[tok:, half : half + names]


def final_kernel(
    ring, half, names, place, kept, got, own_proj, codes, from_x, from_y, from_d, res, dec_bias, ids,
    out_codes, out_scores, out_error,
):
    tok = kept.shape[0]
    active = ids.shape[1]
    here = pl.multiple_of(place[3] * half, 128)
    there = pl.multiple_of((1 - place[3]) * half, 128)
    for at, recon in ((here, kept[...]), (there, got[:, :half].astype(F32))):
        cols = pl.ds(at, half)
        out_error[:, cols] = (res[:, cols].astype(F32) - dec_bias[:, cols] - recon).astype(BF)
    code_src, proj_src = [codes[:tok].astype(F32)], [own_proj[:tok]]
    for src in (from_x, from_y, from_d):
        code_src.append(
            jnp.concatenate([src[:tok, half + names :], src[tok:, half + names :]], axis=1).astype(F32)
        )
        proj_src.append(src[:tok, half : half + names].astype(F32))
    proj_src = [
        v + got[:, half + i * names : half + (i + 1) * names].astype(F32)
        for i, v in enumerate(proj_src)
    ]
    lane = lax.broadcasted_iota(jnp.int32, (tok, 128), 1)
    low = lane < 64
    y = place[1]
    code_out = [jnp.zeros((tok, 128), F32)] * active
    proj_out = [jnp.zeros((tok, 128), F32)] * active
    for x_rel in range(2):
        for kk in range(ring):
            cols = slice(128 * (kk // 2), 128 * (kk // 2) + 128)
            turn = place[2] - kk
            turn = jnp.where(turn < 0, turn + ring, turn)
            block = turn * 2 + (place[0] ^ x_rel)
            pair = []
            for src in (code_src, proj_src):
                near, far = src[x_rel][:, cols], src[2 + x_rel][:, cols]
                first = jnp.where(y == 0, near, far)
                second = jnp.where(y == 0, far, near)
                if kk % 2 == 0:
                    pair.append(jnp.where(low, first, pltpu.roll(second, 64, 1)))
                else:
                    pair.append(jnp.where(low, pltpu.roll(first, 64, 1), second))
            for k in range(active):
                hit = ids[:, k : k + 1] == block
                code_out[k] = code_out[k] + jnp.where(hit, pair[0], 0.0)
                proj_out[k] = proj_out[k] + jnp.where(hit, pair[1], 0.0)
    for k in range(active):
        out_codes[:, k, :] = code_out[k].astype(BF)
        out_scores[:, k, :] = code_out[k] * proj_out[k]


def move_weights(residual, gradient, block_ids, jump_mask, encoder, enc_bias, decoder, dec_bias):
    tok, width = residual.shape
    active = block_ids.shape[1]
    lanes = jump_mask.shape[2]
    lat_count = lax.axis_size("lat")
    ring = lat_count // 2
    per = lanes // 2
    half = width // 2
    names = ring * per
    y = lax.axis_index("groups")
    lat = lax.axis_index("lat")
    s = lax.axis_index("seq")
    z, x = lat // 2, lat % 2
    place = jnp.stack([x, y, z, s]).astype(jnp.int32)

    def permute(values, to):
        pairs = []
        for gg in range(2):
            for ll in range(lat_count):
                for ss in range(2):
                    a, b, c = to(gg, ll, ss)
                    pairs.append(((gg * lat_count + ll) * 2 + ss, (a * lat_count + b) * 2 + c))
        return lax.ppermute(values, AXES, pairs)

    def by_x(v):
        return permute(v, lambda gg, ll, ss: (gg, ll ^ 1, ss))

    def by_y(v):
        return permute(v, lambda gg, ll, ss: (1 - gg, ll, ss))

    def by_xy(v):
        return permute(v, lambda gg, ll, ss: (1 - gg, ll ^ 1, ss))

    def by_core(v):
        return permute(v, lambda gg, ll, ss: (gg, ll, 1 - ss))

    def by_z(v, k):
        return permute(v, lambda gg, ll, ss: (gg, (ll + 2 * k) % lat_count, ss))

    enc_q, dec_q = pl.pallas_call(
        weights_kernel,
        grid_spec=pltpu.PrefetchScalarGridSpec(
            num_scalar_prefetch=1,
            grid=(1,),
            in_specs=[
                pl.BlockSpec((half, lanes), lambda i, p: (p[3], 0)),
                pl.BlockSpec((per, half), lambda i, p: (p[1], p[3])),
                pl.BlockSpec((1, lanes), lambda i, p: (0, 0)),
            ],
            out_specs=[
                pl.BlockSpec((per, half + 128), lambda i, p: (0, 0)),
                pl.BlockSpec((per, half), lambda i, p: (0, 0)),
            ],
        ),
        out_shape=[
            jax.ShapeDtypeStruct((per, half + 128), BF),
            jax.ShapeDtypeStruct((per, half), BF),
        ],
        compiler_params=pltpu.CompilerParams(vmem_limit_bytes=32 << 20),
    )(place, encoder, decoder, enc_bias.reshape(1, lanes))
    enc_parts, dec_parts = [enc_q], [dec_q]
    for _ in range(ring - 1):
        enc_parts.append(by_z(enc_parts[-1], 1))
        dec_parts.append(by_z(dec_parts[-1], 1))

    lead = width + 4 * names
    keep, send = call(
        functools.partial(tokens_kernel, ring),
        [((tok, lead), BF)] * 2,
        place, residual, gradient, block_ids, jump_mask,
    )
    got = by_core(send)
    to_x, to_y, to_d = call(
        rows_kernel, [((2 * tok, width + names), BF)] * 3, place, keep, got
    )
    rows = (keep, got, by_x(to_x), by_y(to_y), by_xy(to_d))

    (part,) = call(
        functools.partial(preact_kernel, ring, half),
        [((8 * tok, names), F32)], place, *rows, *enc_parts,
    )
    (codes,) = call(codes_kernel, [((8 * tok, names), BF)], place, part, by_core(part), *rows)
    out_lanes = half + names + names // 2
    own_recon, own_proj, sums, to_x, to_y, to_d = call(
        functools.partial(recon_kernel, ring, half),
        [((2 * tok, half), F32), ((2 * tok, names), F32), ((8, names), F32)]
        + [((2 * tok, out_lanes), BF)] * 3,
        place, codes, *rows, *dec_parts,
    )
    from_d = by_xy(to_d)
    from_x = by_x(to_x)
    from_y = by_y(to_y)

    total = sums[:2, :per]
    for k in range(1, ring):
        total = total + by_z(sums, -k)[:2, per * k : per * k + per]
    other = by_y(total[1])
    both = jnp.where(
        y == 0, jnp.concatenate([total[0], other]), jnp.concatenate([other, total[0]])
    ).reshape(2, per)
    mine = jnp.where(s == 0, both[0], both[1])
    theirs = jnp.where(s == 0, both[1], both[0])
    factor = (tok * lat_count * 2 * active / lat_count) ** (-0.5)
    latent_totals = (mine + by_core(theirs)) * factor

    kept, send = call(
        functools.partial(home_kernel, half, names),
        [((tok, half), F32), ((tok, half + 4 * names), BF)],
        place, own_recon, own_proj, from_x, from_y, from_d,
    )
    latent_codes, attribution, recon_error = call(
        functools.partial(final_kernel, ring, half, names),
        [((tok, active, lanes), BF), ((tok, active, lanes), F32), ((tok, width), BF)],
        place, kept, by_core(send), own_proj, codes, from_x, from_y, from_d,
        residual, dec_bias.reshape(1, width), block_ids,
    )
    return (latent_codes, attribution, recon_error, latent_totals)


def solution(mesh):
    sizes = dict(mesh.shape)

    def on_device(residual, gradient, block_ids, jump_mask, encoder, enc_bias, decoder, dec_bias):
        lanes = jump_mask.shape[2]
        small = (
            sizes["groups"] == 2
            and sizes["seq"] == 2
            and sizes["lat"] in (4, 8, 16)
            and encoder.shape[1] == lanes
            and lanes == 128
            and residual.shape[0] % 16 == 0
            and residual.shape[1] % 256 == 0
        )
        body = move_weights if small else move_tokens
        return body(
            residual, gradient, block_ids, jump_mask, encoder, enc_bias, decoder, dec_bias
        )

    rows = P(("groups", "lat", "seq"), None)
    cubes = P(("groups", "lat", "seq"), None, None)
    return jax.shard_map(
        on_device,
        mesh=mesh,
        in_specs=(rows, rows, rows, cubes, P(None, "lat"), P("lat"), P("lat", None), P()),
        out_specs=(cubes, cubes, rows, P(("groups", "lat", "seq"))),
        check_vma=False,
    )
```

time: 177 us -> 84.2 us (0.48)
  blocking collectives: 106 us -> 0 us
  waiting for transfers between devices: 35.4 us -> 50.2 us
  Pallas kernels: 0 us -> 9.82 us
  local copies, waits for them, and re-layouts: 12.7 us -> 5.19 us
  starting transfers between devices: 10.6 us -> 17 us
  other arithmetic: 6.36 us -> 0.89 us
  matrix products: 3.48 us -> 0 us
    all_to_all x3 -> x0, blocking collectives: 60.1 us -> none  [the longest x1 40.6 us: on_device(): lax.all_to_all(residual_slots, 'lat', split_axis=0, concat_axis=0, tiled=...]
    ppermute x0 -> x20, waiting for transfers between devices: none -> 50.2 us  [permute(): return lax.ppermute(values, AXES, pairs)]
    unnamed x1 -> x0, blocking collectives: 45.8 us -> none
    all_to_all x3 -> x0, waiting for transfers between devices: 35.4 us -> none  [the longest x1 29.9 us: on_device(): lax.all_to_all(gradient_slots, 'lat', split_axis=0, concat_axis=0, tiled=...]
    ppermute x0 -> x20, starting transfers between devices: none -> 17 us  [permute(): return lax.ppermute(values, AXES, pairs)]
    all_to_all x3 -> x0, starting transfers between devices: 10.6 us -> none  [the longest x1 3.7 us: on_device(): lax.all_to_all(gradient_slots, 'lat', split_axis=0, concat_axis=0, tiled=...]
    pallas_call x0 -> x8, Pallas kernels: none -> 9.82 us  [the longest x7 8.98 us: call(): pl.pallas_call(kernel, in_specs=[smem] + [whole] * (len(args) - 1), out_s...]
    gather x6 -> x0, local copies, waits for them, and re-layouts: 8.09 us -> none  [the longest x3 4.73 us: place_rows(): values[source]]
  transfers between devices with their start and end apart: 3 -> 20, of which waited for: 2 -> 13; matrix products, arithmetic and copies ran while one was open for 3% -> 1% of each run, Pallas kernels for 0% -> 6%
where the time goes in v2:
time: 84.2 us; the launch traced here: 83.9 us
  waiting for transfers between devices  50.2 us (60%)
  starting transfers between devices  17 us (20%)
  Pallas kernels  9.82 us (12%)
  local copies, waits for them, and re-layouts  5.19 us (6%)
  other arithmetic  0.89 us (1%)
    ppermute x20, waiting for transfers between devices, permute(): return lax.ppermute(values, AXES, pairs)  50.2 us
    ppermute x20, starting transfers between devices, permute(): return lax.ppermute(values, AXES, pairs)  17 us
    pallas_call x7, Pallas kernels, call(): pl.pallas_call(kernel, in_specs=[smem] + [whole] * (len(args) - 1), out_s...  8.98 us
    unnamed x17, local copies, waits for them, and re-layouts  5.17 us
  transfers between devices with their start and end apart: 20, of which 13 were waited for; matrix products, arithmetic and copies ran while one was open for 1% of the time, Pallas kernels for 6%

profile of v2, /device:TPU:0, one launch (start us, length us, event | category | flops | bytes accessed | tf_op | source)
XLA Modules:
  0.0 83.9 jit_solution(11963931972711416214)
XLA Ops:
  0.7 0.8 copy.12.ids
  1.5 0.9 %copy-done = bf16[32,3584]{1,0:T(8,128)(2,1)S(1)} copy-done((bf16[32,3584]{1,0:T(8,128)(2,1)S(1)}, bf16[32,3584]{1,0:T(8,128)(2,1)}, u32[]{:S(2)}) %copy-start) | copy-done | bytes 229400
  2.5 0.9 %copy-done.4 = bf16[32,3584]{1,0:T(8,128)(2,1)S(1)} copy-done((bf16[32,3584]{1,0:T(8,128)(2,1)S(1)}, bf16[32,3584]{1,0:T(8,128)(2,1)}, u32[]{:S(2)}) %copy-start.4) | copy-done | bytes 229400
  3.4 0.8 shard_map.111
  4.9 1.2 %copy-done.2 = bf16[3584,128]{1,0:T(8,128)(2,1)S(1)} copy-done((bf16[3584,128]{1,0:T(8,128)(2,1)S(1)}, bf16[3584,128]{1,0:T(8,128)(2,1)}, u32[]{:S(2)}) %copy-start.2) | copy-done | bytes 917528
  6.1 1.2 %copy-done.3 = bf16[128,3584]{1,0:T(8,128)(2,1)S(1)} copy-done((bf16[128,3584]{1,0:T(8,128)(2,1)S(1)}, bf16[128,3584]{1,0:T(8,128)(2,1)}, u32[]{:S(2)}) %copy-start.3) | copy-done | bytes 917528
  7.3 0.8 %shard_map.113 = (bf16[64,1920]{1,0:T(8,128)(2,1)S(1)}, bf16[64,1792]{1,0:T(8,128)(2,1)S(1)}) custom-call(s32[4]{0:T(128)S(1)} %pad_add_fusion.place, bf16[3584,128]{1,0:T(8,128)(2,1)S(1)} %copy-done.2, bf16[128,3584]{1,0:T(8,128)(2,1)S(1)} %copy-done.3, f32[1,128]{1,0:T(1,128)S(1)} %bitcast.9), custom_call_target="tpu_custom_call" | custom-call | tf_op jit(solution)/shard_map/pallas_call | solution.py:346
  8.1 3.1 %collective-permute-start.4 = (bf16[64,1920]{1,0:T(8,128)(2,1)S(1)}, bf16[64,1920]{1,0:T(8,128)(2,1)S(1)}, u32[]{:S(2)}, u32[]{:S(2)}) collective-permute-start(bf16[64,1920]{1,0:T(8,128)(2,1)S(1)} %get-tuple-element.27.refs_0_), channel_id=1, source_target_pairs={{0,4},{1,5},{2,6},{3,7},{4,8},{5,9},{6,10},{7,11},{8,12},{9,13},{1... | collective-permute-start | bytes 737288 | tf_op jit(solution)/shard_map/ppermute | solution.py:329
  11.2 8.1 %collective-permute-done.4.refs_1_ = bf16[64,1920]{1,0:T(8,128)(2,1)S(1)} collective-permute-done((bf16[64,1920]{1,0:T(8,128)(2,1)S(1)}, bf16[64,1920]{1,0:T(8,128)(2,1)S(1)}, u32[]{:S(2)}, u32[]{:S(2)}) %collective-permute-start.4) | collective-permute-done | bytes 245792 | tf_op jit(solution)/shard_map/ppermute | solution.py:329
  19.9 1.6 %collective-permute-start.1 = (bf16[64,3840]{1,0:T(8,128)(2,1)S(1)}, bf16[64,3840]{1,0:T(8,128)(2,1)S(1)}, u32[]{:S(2)}, u32[]{:S(2)}) collective-permute-start(bf16[64,3840]{1,0:T(8,128)(2,1)S(1)} %get-tuple-element.24), channel_id=1, source_target_pairs={{0,2},{1,3},{2,0},{3,1},{4,6},{5,7},{6,4},{7,5},{8,10},{9,11},{10,... | collective-permute-start | bytes 1474568 | tf_op jit(solution)/shard_map/ppermute | solution.py:329
  21.5 1.5 %collective-permute-start.2 = (bf16[64,3840]{1,0:T(8,128)(2,1)S(1)}, bf16[64,3840]{1,0:T(8,128)(2,1)S(1)}, u32[]{:S(2)}, u32[]{:S(2)}) collective-permute-start(bf16[64,3840]{1,0:T(8,128)(2,1)S(1)} %get-tuple-element.25), channel_id=1, source_target_pairs={{0,16},{1,17},{2,18},{3,19},{4,20},{5,21},{6,22},{7,23},{8,24},{9,... | collective-permute-start | bytes 1474568 | tf_op jit(solution)/shard_map/ppermute | solution.py:329
  23.5 1.3 %collective-permute-start.8 = (bf16[64,1792]{1,0:T(8,128)(2,1)S(1)}, bf16[64,1792]{1,0:T(8,128)(2,1)S(1)}, u32[]{:S(2)}, u32[]{:S(2)}) collective-permute-start(bf16[64,1792]{1,0:T(8,128)(2,1)S(1)} %get-tuple-element.28.refs_0_), channel_id=1, source_target_pairs={{0,4},{1,5},{2,6},{3,7},{4,8},{5,9},{6,10},{7,11},{8,12},{9,13},{1... | collective-permute-start | bytes 688136 | tf_op jit(solution)/shard_map/ppermute | solution.py:329
  24.8 5.2 %collective-permute-done.5.refs_2_ = bf16[64,1920]{1,0:T(8,128)(2,1)S(1)} collective-permute-done((bf16[64,1920]{1,0:T(8,128)(2,1)S(1)}, bf16[64,1920]{1,0:T(8,128)(2,1)S(1)}, u32[]{:S(2)}, u32[]{:S(2)}) %collective-permute-start.5) | collective-permute-done | bytes 245792 | tf_op jit(solution)/shard_map/ppermute | solution.py:329
  30.0 4.9 %collective-permute-done.8.refs_1_ = bf16[64,1792]{1,0:T(8,128)(2,1)S(1)} collective-permute-done((bf16[64,1792]{1,0:T(8,128)(2,1)S(1)}, bf16[64,1792]{1,0:T(8,128)(2,1)S(1)}, u32[]{:S(2)}, u32[]{:S(2)}) %collective-permute-start.8) | collective-permute-done | bytes 229408 | tf_op jit(solution)/shard_map/ppermute | solution.py:329
  34.9 5.8 %collective-permute-done.6.refs_3_ = bf16[64,1920]{1,0:T(8,128)(2,1)S(1)} collective-permute-done((bf16[64,1920]{1,0:T(8,128)(2,1)S(1)}, bf16[64,1920]{1,0:T(8,128)(2,1)S(1)}, u32[]{:S(2)}, u32[]{:S(2)}) %collective-permute-start.6) | collective-permute-done | bytes 245792 | tf_op jit(solution)/shard_map/ppermute | solution.py:329
  40.7 3.3 %collective-permute-done.2.from_y = bf16[64,3840]{1,0:T(8,128)(2,1)S(1)} collective-permute-done((bf16[64,3840]{1,0:T(8,128)(2,1)S(1)}, bf16[64,3840]{1,0:T(8,128)(2,1)S(1)}, u32[]{:S(2)}, u32[]{:S(2)}) %collective-permute-start.2) | collective-permute-done | bytes 491552 | tf_op jit(solution)/shard_map/ppermute | solution.py:329
  44.0 1.9 %shard_map.114.mine = f32[256,256]{1,0:T(8,128)S(1)} custom-call(s32[4]{0:T(128)S(1)} %pad_add_fusion.place, bf16[32,4608]{1,0:T(8,128)(2,1)S(1)} %get-tuple-element.22.keep, bf16[32,4608]{1,0:T(8,128)(2,1)S(1)} %collective-permute-done.got, bf16[64,3840]{1,0:T(8,128)(2,1)S(1)} %collective-permute-done.1.from_x, ...), custom_call_target="tpu_custom_call" | custom-call | bytes 1048576 | tf_op jit(solution)/shard_map/pallas_call | solution.py:107
  46.0 1.0 %collective-permute-start.10 = (bf16[64,1792]{1,0:T(8,128)(2,1)S(1)}, bf16[64,1792]{1,0:T(8,128)(2,1)S(1)}, u32[]{:S(2)}, u32[]{:S(2)}) collective-permute-start(bf16[64,1792]{1,0:T(8,128)(2,1)S(1)} %collective-permute-done.9.refs_2_), channel_id=1, source_target_pairs={{0,4},{1,5},{2,6},{3,7},{4,8},{5,9},{6,10},{7,11},{8,12},{9,13},{1... | collective-permute-start | bytes 688136 | tf_op jit(solution)/shard_map/ppermute | solution.py:329
  48.1 7.7 %collective-permute-done.10.refs_3_ = bf16[64,1792]{1,0:T(8,128)(2,1)S(1)} collective-permute-done((bf16[64,1792]{1,0:T(8,128)(2,1)S(1)}, bf16[64,1792]{1,0:T(8,128)(2,1)S(1)}, u32[]{:S(2)}, u32[]{:S(2)}) %collective-permute-start.10) | collective-permute-done | bytes 229408 | tf_op jit(solution)/shard_map/ppermute | solution.py:329
  55.8 2.6 %shard_map.116 = (f32[64,1792]{1,0:T(8,128)S(1)}, f32[64,256]{1,0:T(8,128)S(1)}, f32[8,256]{1,0:T(8,128)S(1)}, bf16[64,2176]{1,0:T(8,128)(2,1)S(1)}, bf16[64,217...) custom-call(s32[4]{0:T(128)S(1)} %pad_add_fusion.place, bf16[256,256]{1,0:T(8,128)(2,1)S(1)} %shard_map.115.codes, ...), custom_call_target="tpu_custom_call" | custom-call | bytes 1048576 | tf_op jit(solution)/shard_map/pallas_call | solution.py:107
  58.5 1.8 %collective-permute-start.15 = (f32[8,256]{1,0:T(8,128)S(1)}, f32[8,256]{1,0:T(8,128)S(1)}, u32[]{:S(2)}, u32[]{:S(2)}) collective-permute-start(f32[8,256]{1,0:T(8,128)S(1)} %get-tuple-element.39), channel_id=1, source_target_pairs={{0,12},{1,13},{2,14},{3,15},{4,0},{5,1},{6,2},{7,3},{8,4},{9,5},{1... | collective-permute-start | bytes 24584 | tf_op jit(solution)/shard_map/ppermute | solution.py:329
  60.9 1.3 %collective-permute-done.15 = f32[8,256]{1,0:T(8,128)S(1)} collective-permute-done((f32[8,256]{1,0:T(8,128)S(1)}, f32[8,256]{1,0:T(8,128)S(1)}, u32[]{:S(2)}, u32[]{:S(2)}) %collective-permute-start.15) | collective-permute-done | bytes 8224 | tf_op jit(solution)/shard_map/ppermute | solution.py:329
  62.2 2.6 %collective-permute-done.16 = f32[8,256]{1,0:T(8,128)S(1)} collective-permute-done((f32[8,256]{1,0:T(8,128)S(1)}, f32[8,256]{1,0:T(8,128)S(1)}, u32[]{:S(2)}, u32[]{:S(2)}) %collective-permute-start.16) | collective-permute-done | bytes 8224 | tf_op jit(solution)/shard_map/ppermute | solution.py:329
  64.8 0.9 %collective-permute-done.17 = f32[8,256]{1,0:T(8,128)S(1)} collective-permute-done((f32[8,256]{1,0:T(8,128)S(1)}, f32[8,256]{1,0:T(8,128)S(1)}, u32[]{:S(2)}, u32[]{:S(2)}) %collective-permute-start.17) | collective-permute-done | bytes 8224 | tf_op jit(solution)/shard_map/ppermute | solution.py:329
  65.8 1.5 %collective-permute-start.18 = (f32[64]{0:T(128)S(1)}, f32[64]{0:T(128)S(1)}, u32[]{:S(2)}, u32[]{:S(2)}) collective-permute-start(f32[64]{0:T(128)S(1)} %get-tuple-element.41), channel_id=1, source_target_pairs={{0,16},{1,17},{2,18},{3,19},{4,20},{5,21},{6,22},{7,23},{8,24},{9,... | collective-permute-start | bytes 776 | tf_op jit(solution)/shard_map/ppermute | solution.py:329
  67.9 1.2 %collective-permute-start.12 = (bf16[64,2176]{1,0:T(8,128)(2,1)S(1)}, bf16[64,2176]{1,0:T(8,128)(2,1)S(1)}, u32[]{:S(2)}, u32[]{:S(2)}) collective-permute-start(bf16[64,2176]{1,0:T(8,128)(2,1)S(1)} %get-tuple-element.32), channel_id=1, source_target_pairs={{0,16},{1,17},{2,18},{3,19},{4,20},{5,21},{6,22},{7,23},{8,24},{9,... | collective-permute-start | bytes 835592 | tf_op jit(solution)/shard_map/ppermute | solution.py:329
  69.1 1.7 %collective-permute-start.13 = (bf16[64,2176]{1,0:T(8,128)(2,1)S(1)}, bf16[64,2176]{1,0:T(8,128)(2,1)S(1)}, u32[]{:S(2)}, u32[]{:S(2)}) collective-permute-start(bf16[64,2176]{1,0:T(8,128)(2,1)S(1)} %get-tuple-element.33), channel_id=1, source_target_pairs={{0,18},{1,19},{2,16},{3,17},{4,22},{5,23},{6,20},{7,21},{8,26},{9,... | collective-permute-start | bytes 835592 | tf_op jit(solution)/shard_map/ppermute | solution.py:329
  71.0 5.8 %collective-permute-done.11.from_x = bf16[64,2176]{1,0:T(8,128)(2,1)S(1)} collective-permute-done((bf16[64,2176]{1,0:T(8,128)(2,1)S(1)}, bf16[64,2176]{1,0:T(8,128)(2,1)S(1)}, u32[]{:S(2)}, u32[]{:S(2)}) %collective-permute-start.11) | collective-permute-done | bytes 278560 | tf_op jit(solution)/shard_map/ppermute | solution.py:329
  76.8 3.2 %collective-permute-done.12.from_y = bf16[64,2176]{1,0:T(8,128)(2,1)S(1)} collective-permute-done((bf16[64,2176]{1,0:T(8,128)(2,1)S(1)}, bf16[64,2176]{1,0:T(8,128)(2,1)S(1)}, u32[]{:S(2)}, u32[]{:S(2)}) %collective-permute-start.12) | collective-permute-done | bytes 278560 | tf_op jit(solution)/shard_map/ppermute | solution.py:329
  80.0 0.7 shard_map.117
  81.4 0.8 collective-permute-done.14.got
  82.2 1.7 %shard_map.118 = (bf16[32,4,128]{2,1,0:T(4,128)(2,1)}, f32[32,4,128]{2,1,0:T(4,128)}, bf16[32,3584]{1,0:T(8,128)(2,1)}) custom-call(s32[4]{0:T(128)S(1)} %pad_add_fusion.place, f32[32,1792]{1,0:T(8,128)S(1)} %get-tuple-element.34.kept, bf16[32,2816]{1,0:T(8,128)(2,1)S(1)} %collective-permute-done.14.got, f32[64,256]{1,0:T(8,128)S(1)} %get-tuple-element.30.own_proj, ...), custom_call_target="tpu_custom_call" | custom-call | bytes 1048576 | tf_op jit(solution)/shard_map/pallas_call | solution.py:107
  (40 shorter events, 5.1 us)
Async XLA Ops:
  0.6 0.9 %copy-start.5 = (s32[32,4,128]{2,1,0:T(4,128)S(1)}, s32[32,4,128]{2,1,0:T(4,128)}, u32[]{:S(2)}) copy-start(s32[32,4,128]{2,1,0:T(4,128)} %jump.1) | copy-start | bytes 196612
  1.5 0.9 %copy-start = (bf16[32,3584]{1,0:T(8,128)(2,1)S(1)}, bf16[32,3584]{1,0:T(8,128)(2,1)}, u32[]{:S(2)}) copy-start(bf16[32,3584]{1,0:T(8,128)(2,1)} %res.3) | copy-start | bytes 688132
  2.5 0.9 %copy-start.4 = (bf16[32,3584]{1,0:T(8,128)(2,1)S(1)}, bf16[32,3584]{1,0:T(8,128)(2,1)}, u32[]{:S(2)}) copy-start(bf16[32,3584]{1,0:T(8,128)(2,1)} %grad.1) | copy-start | bytes 688132
  4.2 0.7 copy-start.6
  4.3 15.0 %collective-permute-start = (bf16[32,4608]{1,0:T(8,128)(2,1)S(1)}, bf16[32,4608]{1,0:T(8,128)(2,1)S(1)}, u32[]{:S(2)}, u32[]{:S(2)}) collective-permute-start(bf16[32,4608]{1,0:T(8,128)(2,1)S(1)} %get-tuple-element.23), channel_id=1, source_target_pairs={{0,1},{1,0},{2,3},{3,2},{4,5},{5,4},{6,7},{7,6},{8,9},{9,8},{10,11... | collective-permute-start | bytes 884744 | tf_op jit(solution)/shard_map/ppermute | solution.py:329
  4.9 1.2 %copy-start.2 = (bf16[3584,128]{1,0:T(8,128)(2,1)S(1)}, bf16[3584,128]{1,0:T(8,128)(2,1)}, u32[]{:S(2)}) copy-start(bf16[3584,128]{1,0:T(8,128)(2,1)} %enc.1) | copy-start | bytes 2752516
  6.1 1.2 %copy-start.3 = (bf16[128,3584]{1,0:T(8,128)(2,1)S(1)}, bf16[128,3584]{1,0:T(8,128)(2,1)}, u32[]{:S(2)}) copy-start(bf16[128,3584]{1,0:T(8,128)(2,1)} %dec.1) | copy-start | bytes 2752516
  8.1 11.2 %collective-permute-start.4 = (bf16[64,1920]{1,0:T(8,128)(2,1)S(1)}, bf16[64,1920]{1,0:T(8,128)(2,1)S(1)}, u32[]{:S(2)}, u32[]{:S(2)}) collective-permute-start(bf16[64,1920]{1,0:T(8,128)(2,1)S(1)} %get-tuple-element.27.refs_0_), channel_id=1, source_target_pairs={{0,4},{1,5},{2,6},{3,7},{4,8},{5,9},{6,10},{7,11},{8,12},{9,13},{1... | collective-permute-start | bytes 737288 | tf_op jit(solution)/shard_map/ppermute | solution.py:329
  19.3 10.7 %collective-permute-start.5 = (bf16[64,1920]{1,0:T(8,128)(2,1)S(1)}, bf16[64,1920]{1,0:T(8,128)(2,1)S(1)}, u32[]{:S(2)}, u32[]{:S(2)}) collective-permute-start(bf16[64,1920]{1,0:T(8,128)(2,1)S(1)} %collective-permute-done.4.refs_1_), channel_id=1, source_target_pairs={{0,4},{1,5},{2,6},{3,7},{4,8},{5,9},{6,10},{7,11},{8,12},{9,13},{1... | collective-permute-start | bytes 737288 | tf_op jit(solution)/shard_map/ppermute | solution.py:329
  19.9 20.7 %collective-permute-start.1 = (bf16[64,3840]{1,0:T(8,128)(2,1)S(1)}, bf16[64,3840]{1,0:T(8,128)(2,1)S(1)}, u32[]{:S(2)}, u32[]{:S(2)}) collective-permute-start(bf16[64,3840]{1,0:T(8,128)(2,1)S(1)} %get-tuple-element.24), channel_id=1, source_target_pairs={{0,2},{1,3},{2,0},{3,1},{4,6},{5,7},{6,4},{7,5},{8,10},{9,11},{10,... | collective-permute-start | bytes 1474568 | tf_op jit(solution)/shard_map/ppermute | solution.py:329
  21.5 22.5 %collective-permute-start.2 = (bf16[64,3840]{1,0:T(8,128)(2,1)S(1)}, bf16[64,3840]{1,0:T(8,128)(2,1)S(1)}, u32[]{:S(2)}, u32[]{:S(2)}) collective-permute-start(bf16[64,3840]{1,0:T(8,128)(2,1)S(1)} %get-tuple-element.25), channel_id=1, source_target_pairs={{0,16},{1,17},{2,18},{3,19},{4,20},{5,21},{6,22},{7,23},{8,24},{9,... | collective-permute-start | bytes 1474568 | tf_op jit(solution)/shard_map/ppermute | solution.py:329
  23.0 21.0 %collective-permute-start.3 = (bf16[64,3840]{1,0:T(8,128)(2,1)S(1)}, bf16[64,3840]{1,0:T(8,128)(2,1)S(1)}, u32[]{:S(2)}, u32[]{:S(2)}) collective-permute-start(bf16[64,3840]{1,0:T(8,128)(2,1)S(1)} %get-tuple-element.26), channel_id=1, source_target_pairs={{0,18},{1,19},{2,16},{3,17},{4,22},{5,23},{6,20},{7,21},{8,26},{9,... | collective-permute-start | bytes 1474568 | tf_op jit(solution)/shard_map/ppermute | solution.py:329
  23.5 11.4 %collective-permute-start.8 = (bf16[64,1792]{1,0:T(8,128)(2,1)S(1)}, bf16[64,1792]{1,0:T(8,128)(2,1)S(1)}, u32[]{:S(2)}, u32[]{:S(2)}) collective-permute-start(bf16[64,1792]{1,0:T(8,128)(2,1)S(1)} %get-tuple-element.28.refs_0_), channel_id=1, source_target_pairs={{0,4},{1,5},{2,6},{3,7},{4,8},{5,9},{6,10},{7,11},{8,12},{9,13},{1... | collective-permute-start | bytes 688136 | tf_op jit(solution)/shard_map/ppermute | solution.py:329
  30.0 10.7 %collective-permute-start.6 = (bf16[64,1920]{1,0:T(8,128)(2,1)S(1)}, bf16[64,1920]{1,0:T(8,128)(2,1)S(1)}, u32[]{:S(2)}, u32[]{:S(2)}) collective-permute-start(bf16[64,1920]{1,0:T(8,128)(2,1)S(1)} %collective-permute-done.5.refs_2_), channel_id=1, source_target_pairs={{0,4},{1,5},{2,6},{3,7},{4,8},{5,9},{6,10},{7,11},{8,12},{9,13},{1... | collective-permute-start | bytes 737288 | tf_op jit(solution)/shard_map/ppermute | solution.py:329
  34.9 11.1 %collective-permute-start.9 = (bf16[64,1792]{1,0:T(8,128)(2,1)S(1)}, bf16[64,1792]{1,0:T(8,128)(2,1)S(1)}, u32[]{:S(2)}, u32[]{:S(2)}) collective-permute-start(bf16[64,1792]{1,0:T(8,128)(2,1)S(1)} %collective-permute-done.8.refs_1_), channel_id=1, source_target_pairs={{0,4},{1,5},{2,6},{3,7},{4,8},{5,9},{6,10},{7,11},{8,12},{9,13},{1... | collective-permute-start | bytes 688136 | tf_op jit(solution)/shard_map/ppermute | solution.py:329
  45.9 1.6 %collective-permute-start.7 = (f32[256,256]{1,0:T(8,128)S(1)}, f32[256,256]{1,0:T(8,128)S(1)}, u32[]{:S(2)}, u32[]{:S(2)}) collective-permute-start(f32[256,256]{1,0:T(8,128)S(1)} %shard_map.114.mine), channel_id=1, source_target_pairs={{0,1},{1,0},{2,3},{3,2},{4,5},{5,4},{6,7},{7,6},{8,9},{9,8},{10,11... | collective-permute-start | bytes 786440 | tf_op jit(solution)/shard_map/ppermute | solution.py:329
  46.0 9.8 %collective-permute-start.10 = (bf16[64,1792]{1,0:T(8,128)(2,1)S(1)}, bf16[64,1792]{1,0:T(8,128)(2,1)S(1)}, u32[]{:S(2)}, u32[]{:S(2)}) collective-permute-start(bf16[64,1792]{1,0:T(8,128)(2,1)S(1)} %collective-permute-done.9.refs_2_), channel_id=1, source_target_pairs={{0,4},{1,5},{2,6},{3,7},{4,8},{5,9},{6,10},{7,11},{8,12},{9,13},{1... | collective-permute-start | bytes 688136 | tf_op jit(solution)/shard_map/ppermute | solution.py:329
  55.8 5.1 %copy-start.7 = (f32[3584]{0:T(1024)S(1)}, f32[3584]{0:T(1024)}, u32[]{:S(2)}) copy-start(f32[3584]{0:T(1024)} %param.15) | copy-start | bytes 43012
  58.5 3.7 %collective-permute-start.15 = (f32[8,256]{1,0:T(8,128)S(1)}, f32[8,256]{1,0:T(8,128)S(1)}, u32[]{:S(2)}, u32[]{:S(2)}) collective-permute-start(f32[8,256]{1,0:T(8,128)S(1)} %get-tuple-element.39), channel_id=1, source_target_pairs={{0,12},{1,13},{2,14},{3,15},{4,0},{5,1},{6,2},{7,3},{8,4},{9,5},{1... | collective-permute-start | bytes 24584 | tf_op jit(solution)/shard_map/ppermute | solution.py:329
  60.3 4.5 %collective-permute-start.16 = (f32[8,256]{1,0:T(8,128)S(1)}, f32[8,256]{1,0:T(8,128)S(1)}, u32[]{:S(2)}, u32[]{:S(2)}) collective-permute-start(f32[8,256]{1,0:T(8,128)S(1)} %get-tuple-element.39), channel_id=1, source_target_pairs={{0,8},{1,9},{2,10},{3,11},{4,12},{5,13},{6,14},{7,15},{8,0},{9,1},... | collective-permute-start | bytes 24584 | tf_op jit(solution)/shard_map/ppermute | solution.py:329
  60.3 5.4 %collective-permute-start.17 = (f32[8,256]{1,0:T(8,128)S(1)}, f32[8,256]{1,0:T(8,128)S(1)}, u32[]{:S(2)}, u32[]{:S(2)}) collective-permute-start(f32[8,256]{1,0:T(8,128)S(1)} %get-tuple-element.39), channel_id=1, source_target_pairs={{0,4},{1,5},{2,6},{3,7},{4,8},{5,9},{6,10},{7,11},{8,12},{9,13},{1... | collective-permute-start | bytes 24584 | tf_op jit(solution)/shard_map/ppermute | solution.py:329
  65.8 5.0 %collective-permute-start.18 = (f32[64]{0:T(128)S(1)}, f32[64]{0:T(128)S(1)}, u32[]{:S(2)}, u32[]{:S(2)}) collective-permute-start(f32[64]{0:T(128)S(1)} %get-tuple-element.41), channel_id=1, source_target_pairs={{0,16},{1,17},{2,18},{3,19},{4,20},{5,21},{6,22},{7,23},{8,24},{9,... | collective-permute-start | bytes 776 | tf_op jit(solution)/shard_map/ppermute | solution.py:329
  67.3 9.5 %collective-permute-start.11 = (bf16[64,2176]{1,0:T(8,128)(2,1)S(1)}, bf16[64,2176]{1,0:T(8,128)(2,1)S(1)}, u32[]{:S(2)}, u32[]{:S(2)}) collective-permute-start(bf16[64,2176]{1,0:T(8,128)(2,1)S(1)} %get-tuple-element.31), channel_id=1, source_target_pairs={{0,2},{1,3},{2,0},{3,1},{4,6},{5,7},{6,4},{7,5},{8,10},{9,11},{10,... | collective-permute-start | bytes 835592 | tf_op jit(solution)/shard_map/ppermute | solution.py:329
  67.9 12.2 %collective-permute-start.12 = (bf16[64,2176]{1,0:T(8,128)(2,1)S(1)}, bf16[64,2176]{1,0:T(8,128)(2,1)S(1)}, u32[]{:S(2)}, u32[]{:S(2)}) collective-permute-start(bf16[64,2176]{1,0:T(8,128)(2,1)S(1)} %get-tuple-element.32), channel_id=1, source_target_pairs={{0,16},{1,17},{2,18},{3,19},{4,20},{5,21},{6,22},{7,23},{8,24},{9,... | collective-permute-start | bytes 835592 | tf_op jit(solution)/shard_map/ppermute | solution.py:329
  69.1 11.0 %collective-permute-start.13 = (bf16[64,2176]{1,0:T(8,128)(2,1)S(1)}, bf16[64,2176]{1,0:T(8,128)(2,1)S(1)}, u32[]{:S(2)}, u32[]{:S(2)}) collective-permute-start(bf16[64,2176]{1,0:T(8,128)(2,1)S(1)} %get-tuple-element.33), channel_id=1, source_target_pairs={{0,18},{1,19},{2,16},{3,17},{4,22},{5,23},{6,20},{7,21},{8,26},{9,... | collective-permute-start | bytes 835592 | tf_op jit(solution)/shard_map/ppermute | solution.py:329
  71.0 9.8 %collective-permute-start.19 = (f32[64]{0:T(128)S(1)}, f32[64]{0:T(128)S(1)}, u32[]{:S(2)}, u32[]{:S(2)}) collective-permute-start(f32[64]{0:T(128)S(1)} %broadcast_select_fusion.1), channel_id=1, source_target_pairs={{0,1},{1,0},{2,3},{3,2},{4,5},{5,4},{6,7},{7,6},{8,9},{9,8},{10,11... | collective-permute-start | bytes 776 | tf_op jit(solution)/shard_map/ppermute | solution.py:329
  80.0 2.1 %copy-start.1 = (bf16[32,3584]{1,0:T(8,128)(2,1)S(1)}, bf16[32,3584]{1,0:T(8,128)(2,1)}, u32[]{:S(2)}) copy-start(bf16[32,3584]{1,0:T(8,128)(2,1)} %res.3) | copy-start | bytes 688132
  80.7 1.5 %collective-permute-start.14 = (bf16[32,2816]{1,0:T(8,128)(2,1)S(1)}, bf16[32,2816]{1,0:T(8,128)(2,1)S(1)}, u32[]{:S(2)}, u32[]{:S(2)}) collective-permute-start(bf16[32,2816]{1,0:T(8,128)(2,1)S(1)} %get-tuple-element.35), channel_id=1, source_target_pairs={{0,1},{1,0},{2,3},{3,2},{4,5},{5,4},{6,7},{7,6},{8,9},{9,8},{10,11... | collective-permute-start | bytes 540680 | tf_op jit(solution)/shard_map/ppermute | solution.py:329

commit v3 on v2

--- a/solution.py
+++ b/solution.py
@@ -101,34 +101,56 @@
     return lax.dot_general(a, b, (((1,), (1,)), ((), ())), preferred_element_type=F32)
 
 
-def call(kernel, outs, *args, flops=0, size=1 << 20):
-    whole = pl.BlockSpec(memory_space=pltpu.VMEM)
-    smem = pl.BlockSpec(memory_space=pltpu.SMEM)
+def call(kernel, outs, *args, far=(), scratch=(), vmem=48, flops=0, size=1 << 20):
+    specs = [pl.BlockSpec(memory_space=pltpu.SMEM)]
+    for i in range(1, len(args)):
+        specs.append(pl.BlockSpec(memory_space=pl.ANY if i in far else pltpu.VMEM))
     return pl.pallas_call(
         kernel,
-        in_specs=[smem] + [whole] * (len(args) - 1),
-        out_specs=[whole] * len(outs),
+        in_specs=specs,
+        out_specs=[pl.BlockSpec(memory_space=pltpu.VMEM)] * len(outs),
         out_shape=[jax.ShapeDtypeStruct(*o) for o in outs],
-        compiler_params=pltpu.CompilerParams(vmem_limit_bytes=48 << 20),
+        scratch_shapes=list(scratch),
+        compiler_params=pltpu.CompilerParams(vmem_limit_bytes=vmem << 20),
         cost_estimate=pl.CostEstimate(flops=flops, bytes_accessed=size, transcendentals=0),
     )(*args)
 
 
-def weights_kernel(place, enc, dec, bias, enc_out, dec_out):
-    per, lanes = enc_out.shape[0], enc.shape[1]
-    half = dec_out.shape[1]
+def weights_kernel(place, enc, dec, bias, out, enc_half, sem):
+    lanes = enc.shape[1]
+    half = enc_half.shape[0]
+    per = out.shape[0]
+    cols = pl.ds(pl.multiple_of(place[3] * half, 128), half)
+    get_enc = pltpu.make_async_copy(enc.at[cols, :], enc_half, sem.at[0])
+    get_dec = pltpu.make_async_copy(
+        dec.at[pl.ds(pl.multiple_of(place[1] * per, 16), per), cols],
+        out.at[:, pl.ds(half + 128, half)],
+        sem.at[1],
+    )
+    get_enc.start()
+    get_dec.start()
     row = lax.broadcasted_iota(jnp.int32, (per, lanes), 0)
     lane = lax.broadcasted_iota(jnp.int32, (per, lanes), 1)
     pick = (lane == row + per * place[1]).astype(BF)
-    enc_out[:, :half] = nt(pick, enc[...]).astype(BF)
     b = bias[...]
     hi = b.astype(BF).astype(F32)
     mid = (b - hi).astype(BF).astype(F32)
     low = b - hi - mid
     term = lax.broadcasted_iota(jnp.int32, (lanes, lanes), 0)
     terms = jnp.where(term == 0, hi, jnp.where(term == 1, mid, jnp.where(term == 2, low, 0.0)))
-    enc_out[:, half:] = nt(pick, terms.astype(BF)).astype(BF)
-    dec_out[...] = dec[...]
+    out[:, half : half + 128] = nt(pick, terms.astype(BF)).astype(BF)
+    get_enc.wait()
+    out[:, :half] = nt(pick, enc_half[...]).astype(BF)
+    get_dec.wait()
+
+
+def split_kernel(place, both, enc_out, dec_out):
+    enc_out[...] = both[:, : enc_out.shape[1]]
+    dec_out[...] = both[:, enc_out.shape[1] :]
+
+
+def after_kernel(place, values, waited, out):
+    out[...] = values[...]
 
 
 def target_block(lane, m, place, x_rel, ring):
@@ -137,16 +159,24 @@
     return turn * 2 + (place[0] ^ x_rel)
 
 
-def tokens_kernel(ring, place, res, grad, ids, jump, keep, send):
+def tokens_kernel(ring, place, res, grad, ids, jump, keep, send, sem):
     tok, width = res.shape
     half = width // 2
-    active = ids.shape[1]
-    here = pl.multiple_of(place[3] * half, 128)
-    there = pl.multiple_of((1 - place[3]) * half, 128)
-    keep[:, :half] = res[:, pl.ds(here, half)]
-    keep[:, half:width] = grad[:, pl.ds(here, half)]
-    send[:, :half] = res[:, pl.ds(there, half)]
-    send[:, half:width] = grad[:, pl.ds(there, half)]
+    active = ids.shape[0]
+    copies = []
+    for i, src in enumerate((res, grad)):
+        for j, out in enumerate((keep, send)):
+            side = place[3] if j == 0 else 1 - place[3]
+            copies.append(
+                pltpu.make_async_copy(
+                    src.at[:, pl.ds(pl.multiple_of(side * half, 128), half)],
+                    out.at[:, pl.ds(i * half, half)],
+                    sem.at[2 * i + j],
+                )
+            )
+    for copy in copies:
+        copy.start()
+    names = ids[...].T
     lane = lax.broadcasted_iota(jnp.int32, (tok, 128), 1)
     low = lane < 64
     plain = [jump[:, k, :] for k in range(active)]
@@ -159,11 +189,13 @@
             total = jnp.zeros((tok, 128), jnp.int32)
             for k in range(active):
                 value = jnp.where(low == first, plain[k], moved[k])
-                total = total + jnp.where(ids[:, k : k + 1] == tgt, value, 0)
+                total = total + jnp.where(names[:, k : k + 1] == tgt, value, 0)
             at = width + (dest * (ring // 2) + m) * 128
             out = total.astype(F32).astype(BF)
             keep[:, at : at + 128] = out
             send[:, at : at + 128] = out
+    for copy in copies:
+        copy.wait()
 
 
 def rows_kernel(place, keep, got, *outs):
@@ -183,7 +215,7 @@
     tok = keep.shape[0]
     per = parts[0].shape[0]
     weights = jnp.concatenate([p[:, :half] for p in parts], axis=0)
-    extra = jnp.concatenate([p[:, half:] for p in parts], axis=0)
+    extra = jnp.concatenate([p[:, half : half + 128] for p in parts], axis=0)
     ones = jnp.where(place[3] == 0, 1.0, 0.0) * jnp.ones((8, 128), F32)
     bias = nt(ones.astype(BF), extra)[:1]
     at = 0
@@ -215,7 +247,7 @@
     sends = refs[ring + 3 :]
     tok = keep.shape[0]
     names = codes.shape[1]
-    weights = jnp.concatenate([p[...] for p in parts], axis=0)
+    weights = jnp.concatenate([p[:, p.shape[1] - half :] for p in parts], axis=0)
     totals = []
     for chip, src in enumerate((None, from_x, from_y, from_d)):
         at = chip * 2 * tok
@@ -259,7 +291,8 @@
     out_codes, out_scores, out_error,
 ):
     tok = kept.shape[0]
-    active = ids.shape[1]
+    active = ids.shape[0]
+    named = ids[...].T
     here = pl.multiple_of(place[3] * half, 128)
     there = pl.multiple_of((1 - place[3]) * half, 128)
     for at, recon in ((here, kept[...]), (there, got[:, :half].astype(F32))):
@@ -296,7 +329,7 @@
                 else:
                     pair.append(jnp.where(low, pltpu.roll(first, 64, 1), second))
             for k in range(active):
-                hit = ids[:, k : k + 1] == block
+                hit = named[:, k : k + 1] == block
                 code_out[k] = code_out[k] + jnp.where(hit, pair[0], 0.0)
                 proj_out[k] = proj_out[k] + jnp.where(hit, pair[1], 0.0)
     for k in range(active):
@@ -343,37 +376,32 @@
     def by_z(v, k):
         return permute(v, lambda gg, ll, ss: (gg, (ll + 2 * k) % lat_count, ss))
 
-    enc_q, dec_q = pl.pallas_call(
+    (own,) = call(
         weights_kernel,
-        grid_spec=pltpu.PrefetchScalarGridSpec(
-            num_scalar_prefetch=1,
-            grid=(1,),
-            in_specs=[
-                pl.BlockSpec((half, lanes), lambda i, p: (p[3], 0)),
-                pl.BlockSpec((per, half), lambda i, p: (p[1], p[3])),
-                pl.BlockSpec((1, lanes), lambda i, p: (0, 0)),
-            ],
-            out_specs=[
-                pl.BlockSpec((per, half + 128), lambda i, p: (0, 0)),
-                pl.BlockSpec((per, half), lambda i, p: (0, 0)),
-            ],
-        ),
-        out_shape=[
-            jax.ShapeDtypeStruct((per, half + 128), BF),
-            jax.ShapeDtypeStruct((per, half), BF),
-        ],
-        compiler_params=pltpu.CompilerParams(vmem_limit_bytes=32 << 20),
-    )(place, encoder, decoder, enc_bias.reshape(1, lanes))
-    enc_parts, dec_parts = [enc_q], [dec_q]
-    for _ in range(ring - 1):
-        enc_parts.append(by_z(enc_parts[-1], 1))
-        dec_parts.append(by_z(dec_parts[-1], 1))
+        [((per, 2 * half + 128), BF)],
+        place, encoder, decoder, enc_bias.reshape(1, lanes),
+        far=(1, 2),
+        scratch=[pltpu.VMEM((half, lanes), BF), pltpu.SemaphoreType.DMA((2,))],
+        vmem=56,
+    )
+    first = by_z(own, 1)
+    enc_next, dec_next = call(
+        split_kernel, [((per, half + 128), BF), ((per, half), BF)], place, first
+    )
+    enc_parts, dec_parts = [own, first], [own, first]
+    for _ in range(ring - 2):
+        enc_next, dec_next = by_z(enc_next, 1), by_z(dec_next, 1)
+        enc_parts.append(enc_next)
+        dec_parts.append(dec_next)
 
     lead = width + 4 * names
     keep, send = call(
         functools.partial(tokens_kernel, ring),
         [((tok, lead), BF)] * 2,
-        place, residual, gradient, block_ids, jump_mask,
+        place, residual, gradient, block_ids.T, jump_mask,
+        far=(1, 2),
+        scratch=[pltpu.SemaphoreType.DMA((4,))],
+        vmem=56,
     )
     got = by_core(send)
     to_x, to_y, to_d = call(
@@ -397,17 +425,17 @@
     from_x = by_x(to_x)
     from_y = by_y(to_y)
 
+    (sums,) = call(after_kernel, [(sums.shape, F32)], place, sums, from_x, far=(2,))
     total = sums[:2, :per]
     for k in range(1, ring):
         total = total + by_z(sums, -k)[:2, per * k : per * k + per]
-    other = by_y(total[1])
-    both = jnp.where(
-        y == 0, jnp.concatenate([total[0], other]), jnp.concatenate([other, total[0]])
-    ).reshape(2, per)
-    mine = jnp.where(s == 0, both[0], both[1])
-    theirs = jnp.where(s == 0, both[1], both[0])
+    row = jnp.where(y == s, total[0], total[1])
+    rest = jnp.where(y == s, total[1], total[0])
     factor = (tok * lat_count * 2 * active / lat_count) ** (-0.5)
-    latent_totals = (mine + by_core(theirs)) * factor
+    latent_totals = (
+        permute(row, lambda gg, ll, ss: (ss, ll, gg))
+        + permute(rest, lambda gg, ll, ss: (1 - ss, ll, gg))
+    ) * factor
 
     kept, send = call(
         functools.partial(home_kernel, half, names),
@@ -418,7 +446,7 @@
         functools.partial(final_kernel, ring, half, names),
         [((tok, active, lanes), BF), ((tok, active, lanes), F32), ((tok, width), BF)],
         place, kept, by_core(send), own_proj, codes, from_x, from_y, from_d,
-        residual, dec_bias.reshape(1, width), block_ids,
+        residual, dec_bias.reshape(1, width), block_ids.T,
     )
     return (latent_codes, attribution, recon_error, latent_totals)
 

time: 84.2 us -> 81.9 us (0.973)
  Pallas kernels: 9.82 us -> 15 us
  local copies, waits for them, and re-layouts: 5.19 us -> 1 us
  waiting for transfers between devices: 50.2 us -> 48.1 us
  starting transfers between devices: 17 us -> 15.5 us
    pallas_call x8 -> x10, Pallas kernels: 9.82 us -> 15 us  [call(): pl.pallas_call(kernel, in_specs=specs, out_specs=[pl.BlockSpec(memory_spa...]
    unnamed x17 -> x14, local copies, waits for them, and re-layouts: 5.17 us -> 0.99 us
    ppermute x20 -> x19, waiting for transfers between devices: 50.2 us -> 48.1 us  [permute(): return lax.ppermute(values, AXES, pairs)]
    ppermute x20 -> x19, starting transfers between devices: 17 us -> 15.5 us  [permute(): return lax.ppermute(values, AXES, pairs)]
  transfers between devices with their start and end apart: 20 -> 19, of which waited for: 13 -> 13; matrix products, arithmetic and copies ran while one was open for 1% -> 1% of each run, Pallas kernels for 6% -> 9%
where the time goes in v3:
time: 81.9 us; the launch traced here: 81.6 us
  waiting for transfers between devices  48.1 us (59%)
  starting transfers between devices  15.5 us (19%)
  Pallas kernels  15 us (18%)
  other arithmetic  1.21 us (1%)
  local copies, waits for them, and re-layouts  1 us (1%)
  between operations  0.83 us (1%)
    ppermute x19, waiting for transfers between devices, permute(): return lax.ppermute(values, AXES, pairs)  48.1 us
    ppermute x19, starting transfers between devices, permute(): return lax.ppermute(values, AXES, pairs)  15.5 us
    pallas_call x10, Pallas kernels, call(): pl.pallas_call(kernel, in_specs=specs, out_specs=[pl.BlockSpec(memory_spa...  15 us
  transfers between devices with their start and end apart: 19, of which 13 were waited for; matrix products, arithmetic and copies ran while one was open for 1% of the time, Pallas kernels for 9%

profile of v3, /device:TPU:0, one launch (start us, length us, event | category | flops | bytes accessed | tf_op | source)
XLA Modules:
  0.0 81.6 jit_solution(13666950479315451180)
XLA Ops:
  0.7 0.6 pad_add_fusion.place
  1.3 2.8 %shard_map.113.refs_0_ = bf16[64,3712]{1,0:T(8,128)(2,1)} custom-call(s32[4]{0:T(128)} %pad_add_fusion.place, bf16[3584,128]{1,0:T(8,128)(2,1)} %enc.1, bf16[128,3584]{1,0:T(8,128)(2,1)} %dec.1, f32[1,128]{1,0:T(1,128)} %bitcast.12), custom_call_target="tpu_custom_call" | custom-call | bytes 1048576 | tf_op jit(solution)/shard_map/pallas_call | solution.py:108
  4.1 3.1 %collective-permute-start.4 = (bf16[64,3712]{1,0:T(8,128)(2,1)}, bf16[64,3712]{1,0:T(8,128)(2,1)S(1)}, u32[]{:S(2)}, u32[]{:S(2)}) collective-permute-start(bf16[64,3712]{1,0:T(8,128)(2,1)} %shard_map.113.refs_0_), channel_id=1, source_target_pairs={{0,4},{1,5},{2,6},{3,7},{4,8},{5,9},{6,10},{7,11},{8,12},{9,13},{1... | collective-permute-start | bytes 1425416 | tf_op jit(solution)/shard_map/ppermute | solution.py:362
  7.1 2.8 %shard_map.111 = (bf16[32,4608]{1,0:T(8,128)(2,1)}, bf16[32,4608]{1,0:T(8,128)(2,1)}) custom-call(s32[4]{0:T(128)} %pad_add_fusion.place, bf16[32,3584]{1,0:T(8,128)(2,1)} %res.3, bf16[32,3584]{1,0:T(8,128)(2,1)} %grad.1, s32[4,32]{1,0:T(4,128)} %bitcast.10, s32[32,4,128]{2,1,0:T(4,128)} %jump.1), custom_call_target="tpu_custom_call" | custom-call | bytes 1048576 | tf_op jit(solution)/shard_map/pallas_call | solution.py:108
  10.1 1.8 %collective-permute-done.got = bf16[32,4608]{1,0:T(8,128)(2,1)S(1)} collective-permute-done((bf16[32,4608]{1,0:T(8,128)(2,1)}, bf16[32,4608]{1,0:T(8,128)(2,1)S(1)}, u32[]{:S(2)}, u32[]{:S(2)}) %collective-permute-start) | collective-permute-done | bytes 294944 | tf_op jit(solution)/shard_map/ppermute | solution.py:362
  11.8 1.0 %copy-done = bf16[32,4608]{1,0:T(8,128)(2,1)S(1)} copy-done((bf16[32,4608]{1,0:T(8,128)(2,1)S(1)}, bf16[32,4608]{1,0:T(8,128)(2,1)}, u32[]{:S(2)}) %copy-start) | copy-done | bytes 294936
  12.8 0.6 shard_map.112
  13.5 1.6 %collective-permute-start.1 = (bf16[64,3840]{1,0:T(8,128)(2,1)S(1)}, bf16[64,3840]{1,0:T(8,128)(2,1)S(1)}, u32[]{:S(2)}, u32[]{:S(2)}) collective-permute-start(bf16[64,3840]{1,0:T(8,128)(2,1)S(1)} %get-tuple-element.24), channel_id=1, source_target_pairs={{0,2},{1,3},{2,0},{3,1},{4,6},{5,7},{6,4},{7,5},{8,10},{9,11},{10,... | collective-permute-start | bytes 1474568 | tf_op jit(solution)/shard_map/ppermute | solution.py:362
  15.0 1.5 %collective-permute-start.2 = (bf16[64,3840]{1,0:T(8,128)(2,1)S(1)}, bf16[64,3840]{1,0:T(8,128)(2,1)S(1)}, u32[]{:S(2)}, u32[]{:S(2)}) collective-permute-start(bf16[64,3840]{1,0:T(8,128)(2,1)S(1)} %get-tuple-element.25), channel_id=1, source_target_pairs={{0,16},{1,17},{2,18},{3,19},{4,20},{5,21},{6,22},{7,23},{8,24},{9,... | collective-permute-start | bytes 1474568 | tf_op jit(solution)/shard_map/ppermute | solution.py:362
  17.0 3.2 %collective-permute-done.4.both.refs_1_ = bf16[64,3712]{1,0:T(8,128)(2,1)S(1)} collective-permute-done((bf16[64,3712]{1,0:T(8,128)(2,1)}, bf16[64,3712]{1,0:T(8,128)(2,1)S(1)}, u32[]{:S(2)}, u32[]{:S(2)}) %collective-permute-start.4) | collective-permute-done | bytes 475168 | tf_op jit(solution)/shard_map/ppermute | solution.py:362
  20.2 0.6 shard_map.114
  20.9 8.9 %collective-permute-done.5.refs_2_ = bf16[64,1920]{1,0:T(8,128)(2,1)S(1)} collective-permute-done((bf16[64,1920]{1,0:T(8,128)(2,1)S(1)}, bf16[64,1920]{1,0:T(8,128)(2,1)S(1)}, u32[]{:S(2)}, u32[]{:S(2)}) %collective-permute-start.5) | collective-permute-done | bytes 245792 | tf_op jit(solution)/shard_map/ppermute | solution.py:362
  29.8 8.7 %collective-permute-done.2.from_y = bf16[64,3840]{1,0:T(8,128)(2,1)S(1)} collective-permute-done((bf16[64,3840]{1,0:T(8,128)(2,1)S(1)}, bf16[64,3840]{1,0:T(8,128)(2,1)S(1)}, u32[]{:S(2)}, u32[]{:S(2)}) %collective-permute-start.2) | collective-permute-done | bytes 491552 | tf_op jit(solution)/shard_map/ppermute | solution.py:362
  38.5 1.8 %collective-permute-done.6.refs_3_ = bf16[64,1920]{1,0:T(8,128)(2,1)S(1)} collective-permute-done((bf16[64,1920]{1,0:T(8,128)(2,1)S(1)}, bf16[64,1920]{1,0:T(8,128)(2,1)S(1)}, u32[]{:S(2)}, u32[]{:S(2)}) %collective-permute-start.6) | collective-permute-done | bytes 245792 | tf_op jit(solution)/shard_map/ppermute | solution.py:362
  40.3 1.9 %shard_map.115.mine = f32[256,256]{1,0:T(8,128)S(1)} custom-call(s32[4]{0:T(128)S(1)} %copy-done.4, bf16[32,4608]{1,0:T(8,128)(2,1)S(1)} %copy-done.1, bf16[32,4608]{1,0:T(8,128)(2,1)S(1)} %collective-permute-done.got, bf16[64,3840]{1,0:T(8,128)(2,1)S(1)} %collective-permute-done.1.from_x, bf16[64,3840]{1,0:T(8,128)(2,1)S(1)} %collective-permute-done.2.from_y, ...), custom_call_target="tpu_custom_call" | custom-call | bytes 1048576 | tf_op jit(solution)/shard_map/pallas_call | solution.py:108
  42.8 1.1 %collective-permute-done.7.other = f32[256,256]{1,0:T(8,128)S(1)} collective-permute-done((f32[256,256]{1,0:T(8,128)S(1)}, f32[256,256]{1,0:T(8,128)S(1)}, u32[]{:S(2)}, u32[]{:S(2)}) %collective-permute-start.7) | collective-permute-done | bytes 262176 | tf_op jit(solution)/shard_map/ppermute | solution.py:362
  43.8 0.6 shard_map.116.codes
  44.4 7.7 %collective-permute-done.9.refs_3_ = bf16[64,1792]{1,0:T(8,128)(2,1)S(1)} collective-permute-done((bf16[64,1792]{1,0:T(8,128)(2,1)S(1)}, bf16[64,1792]{1,0:T(8,128)(2,1)S(1)}, u32[]{:S(2)}, u32[]{:S(2)}) %collective-permute-start.9) | collective-permute-done | bytes 229408 | tf_op jit(solution)/shard_map/ppermute | solution.py:362
  52.1 2.6 %shard_map.117 = (f32[64,1792]{1,0:T(8,128)S(1)}, f32[64,256]{1,0:T(8,128)S(1)}, f32[8,256]{1,0:T(8,128)S(1)}, bf16[64,2176]{1,0:T(8,128)(2,1)S(1)}, bf16[64,217...) custom-call(s32[4]{0:T(128)S(1)} %copy-done.4, bf16[256,256]{1,0:T(8,128)(2,1)S(1)} %shard_map.116.codes, ...), custom_call_target="tpu_custom_call" | custom-call | bytes 1048576 | tf_op jit(solution)/shard_map/pallas_call | solution.py:108
  54.8 1.1 %collective-permute-start.10 = (bf16[64,2176]{1,0:T(8,128)(2,1)S(1)}, bf16[64,2176]{1,0:T(8,128)(2,1)S(1)}, u32[]{:S(2)}, u32[]{:S(2)}) collective-permute-start(bf16[64,2176]{1,0:T(8,128)(2,1)S(1)} %get-tuple-element.31), channel_id=1, source_target_pairs={{0,2},{1,3},{2,0},{3,1},{4,6},{5,7},{6,4},{7,5},{8,10},{9,11},{10,... | collective-permute-start | bytes 835592 | tf_op jit(solution)/shard_map/ppermute | solution.py:362
  55.8 6.8 %collective-permute-done.10.from_x.waited = bf16[64,2176]{1,0:T(8,128)(2,1)S(1)} collective-permute-done((bf16[64,2176]{1,0:T(8,128)(2,1)S(1)}, bf16[64,2176]{1,0:T(8,128)(2,1)S(1)}, u32[]{:S(2)}, u32[]{:S(2)}) %collective-permute-start.10) | collective-permute-done | bytes 278560 | tf_op jit(solution)/shard_map/ppermute | solution.py:362
  62.6 0.5 shard_map.120
  63.5 1.8 %collective-permute-start.16 = (f32[8,256]{1,0:T(8,128)S(1)}, f32[8,256]{1,0:T(8,128)S(1)}, u32[]{:S(2)}, u32[]{:S(2)}) collective-permute-start(f32[8,256]{1,0:T(8,128)S(1)} %shard_map.120), channel_id=1, source_target_pairs={{0,4},{1,5},{2,6},{3,7},{4,8},{5,9},{6,10},{7,11},{8,12},{9,13},{1... | collective-permute-start | bytes 24584 | tf_op jit(solution)/shard_map/ppermute | solution.py:362
  65.3 1.1 %collective-permute-start.11 = (bf16[64,2176]{1,0:T(8,128)(2,1)S(1)}, bf16[64,2176]{1,0:T(8,128)(2,1)S(1)}, u32[]{:S(2)}, u32[]{:S(2)}) collective-permute-start(bf16[64,2176]{1,0:T(8,128)(2,1)S(1)} %get-tuple-element.32), channel_id=1, source_target_pairs={{0,16},{1,17},{2,18},{3,19},{4,20},{5,21},{6,22},{7,23},{8,24},{9,... | collective-permute-start | bytes 835592 | tf_op jit(solution)/shard_map/ppermute | solution.py:362
  66.4 1.4 %collective-permute-start.12 = (bf16[64,2176]{1,0:T(8,128)(2,1)S(1)}, bf16[64,2176]{1,0:T(8,128)(2,1)S(1)}, u32[]{:S(2)}, u32[]{:S(2)}) collective-permute-start(bf16[64,2176]{1,0:T(8,128)(2,1)S(1)} %get-tuple-element.33), channel_id=1, source_target_pairs={{0,18},{1,19},{2,16},{3,17},{4,22},{5,23},{6,20},{7,21},{8,26},{9,... | collective-permute-start | bytes 835592 | tf_op jit(solution)/shard_map/ppermute | solution.py:362
  67.9 1.5 %collective-permute-done.16 = f32[8,256]{1,0:T(8,128)S(1)} collective-permute-done((f32[8,256]{1,0:T(8,128)S(1)}, f32[8,256]{1,0:T(8,128)S(1)}, u32[]{:S(2)}, u32[]{:S(2)}) %collective-permute-start.16) | collective-permute-done | bytes 8224 | tf_op jit(solution)/shard_map/ppermute | solution.py:362
  69.4 0.7 collective-permute-start.17
  70.1 2.3 %collective-permute-start.18 = (f32[64]{0:T(128)S(1)}, f32[64]{0:T(128)S(1)}, u32[]{:S(2)}, u32[]{:S(2)}) collective-permute-start(f32[64]{0:T(128)S(1)} %get-tuple-element.40), channel_id=1, source_target_pairs={{0,16},{1,0},{2,18},{3,2},{4,20},{5,4},{6,22},{7,6},{8,24},{9,8},{... | collective-permute-start | bytes 776 | tf_op jit(solution)/shard_map/ppermute | solution.py:362
  72.4 5.3 %collective-permute-done.11.from_y = bf16[64,2176]{1,0:T(8,128)(2,1)S(1)} collective-permute-done((bf16[64,2176]{1,0:T(8,128)(2,1)S(1)}, bf16[64,2176]{1,0:T(8,128)(2,1)S(1)}, u32[]{:S(2)}, u32[]{:S(2)}) %collective-permute-start.11) | collective-permute-done | bytes 278560 | tf_op jit(solution)/shard_map/ppermute | solution.py:362
  77.6 0.7 shard_map.118
  78.9 0.9 %collective-permute-done.13.got = bf16[32,2816]{1,0:T(8,128)(2,1)S(1)} collective-permute-done((bf16[32,2816]{1,0:T(8,128)(2,1)S(1)}, bf16[32,2816]{1,0:T(8,128)(2,1)S(1)}, u32[]{:S(2)}, u32[]{:S(2)}) %collective-permute-start.13) | collective-permute-done | bytes 180256 | tf_op jit(solution)/shard_map/ppermute | solution.py:362
  79.8 1.8 %shard_map.119 = (bf16[32,4,128]{2,1,0:T(4,128)(2,1)}, f32[32,4,128]{2,1,0:T(4,128)}, bf16[32,3584]{1,0:T(8,128)(2,1)}) custom-call(s32[4]{0:T(128)S(1)} %copy-done.4, f32[32,1792]{1,0:T(8,128)S(1)} %get-tuple-element.34.kept, bf16[32,2816]{1,0:T(8,128)(2,1)S(1)} %collective-permute-done.13.got, f32[64,256]{1,0:T(8,128)S(1)} %get-tuple-element.30.own_proj, ...), custom_call_target="tpu_custom_call" | custom-call | bytes 1048576 | tf_op jit(solution)/shard_map/pallas_call | solution.py:108
  (35 shorter events, 2.2 us)
Async XLA Ops:
  4.1 16.2 %collective-permute-start.4 = (bf16[64,3712]{1,0:T(8,128)(2,1)}, bf16[64,3712]{1,0:T(8,128)(2,1)S(1)}, u32[]{:S(2)}, u32[]{:S(2)}) collective-permute-start(bf16[64,3712]{1,0:T(8,128)(2,1)} %shard_map.113.refs_0_), channel_id=1, source_target_pairs={{0,4},{1,5},{2,6},{3,7},{4,8},{5,9},{6,10},{7,11},{8,12},{9,13},{1... | collective-permute-start | bytes 1425416 | tf_op jit(solution)/shard_map/ppermute | solution.py:362
  10.0 1.9 %copy-start.4 = (s32[4]{0:T(128)S(1)}, s32[4]{0:T(128)}, u32[]{:S(2)}) copy-start(s32[4]{0:T(128)} %pad_add_fusion.place) | copy-start | bytes 52
  10.0 1.9 %collective-permute-start = (bf16[32,4608]{1,0:T(8,128)(2,1)}, bf16[32,4608]{1,0:T(8,128)(2,1)S(1)}, u32[]{:S(2)}, u32[]{:S(2)}) collective-permute-start(bf16[32,4608]{1,0:T(8,128)(2,1)} %get-tuple-element.23), channel_id=1, source_target_pairs={{0,1},{1,0},{2,3},{3,2},{4,5},{5,4},{6,7},{7,6},{8,9},{9,8},{10,11... | collective-permute-start | bytes 884744 | tf_op jit(solution)/shard_map/ppermute | solution.py:362
  11.8 1.0 %copy-start = (bf16[32,4608]{1,0:T(8,128)(2,1)S(1)}, bf16[32,4608]{1,0:T(8,128)(2,1)}, u32[]{:S(2)}) copy-start(bf16[32,4608]{1,0:T(8,128)(2,1)} %get-tuple-element.22.keep) | copy-start | bytes 884740
  12.8 27.5 %copy-start.2 = (bf16[64,3712]{1,0:T(8,128)(2,1)S(1)}, bf16[64,3712]{1,0:T(8,128)(2,1)}, u32[]{:S(2)}) copy-start(bf16[64,3712]{1,0:T(8,128)(2,1)} %shard_map.113.refs_0_) | copy-start | bytes 1425412
  13.5 26.8 %copy-start.1 = (bf16[32,4608]{1,0:T(8,128)(2,1)S(1)}, bf16[32,4608]{1,0:T(8,128)(2,1)}, u32[]{:S(2)}) copy-start(bf16[32,4608]{1,0:T(8,128)(2,1)} %get-tuple-element.22.keep) | copy-start | bytes 884740
  13.5 16.4 %collective-permute-start.1 = (bf16[64,3840]{1,0:T(8,128)(2,1)S(1)}, bf16[64,3840]{1,0:T(8,128)(2,1)S(1)}, u32[]{:S(2)}, u32[]{:S(2)}) collective-permute-start(bf16[64,3840]{1,0:T(8,128)(2,1)S(1)} %get-tuple-element.24), channel_id=1, source_target_pairs={{0,2},{1,3},{2,0},{3,1},{4,6},{5,7},{6,4},{7,5},{8,10},{9,11},{10,... | collective-permute-start | bytes 1474568 | tf_op jit(solution)/shard_map/ppermute | solution.py:362
  15.0 23.5 %collective-permute-start.2 = (bf16[64,3840]{1,0:T(8,128)(2,1)S(1)}, bf16[64,3840]{1,0:T(8,128)(2,1)S(1)}, u32[]{:S(2)}, u32[]{:S(2)}) collective-permute-start(bf16[64,3840]{1,0:T(8,128)(2,1)S(1)} %get-tuple-element.25), channel_id=1, source_target_pairs={{0,16},{1,17},{2,18},{3,19},{4,20},{5,21},{6,22},{7,23},{8,24},{9,... | collective-permute-start | bytes 1474568 | tf_op jit(solution)/shard_map/ppermute | solution.py:362
  16.5 22.0 %collective-permute-start.3 = (bf16[64,3840]{1,0:T(8,128)(2,1)S(1)}, bf16[64,3840]{1,0:T(8,128)(2,1)S(1)}, u32[]{:S(2)}, u32[]{:S(2)}) collective-permute-start(bf16[64,3840]{1,0:T(8,128)(2,1)S(1)} %get-tuple-element.26), channel_id=1, source_target_pairs={{0,18},{1,19},{2,16},{3,17},{4,22},{5,23},{6,20},{7,21},{8,26},{9,... | collective-permute-start | bytes 1474568 | tf_op jit(solution)/shard_map/ppermute | solution.py:362
  20.8 9.0 %collective-permute-start.5 = (bf16[64,1920]{1,0:T(8,128)(2,1)S(1)}, bf16[64,1920]{1,0:T(8,128)(2,1)S(1)}, u32[]{:S(2)}, u32[]{:S(2)}) collective-permute-start(bf16[64,1920]{1,0:T(8,128)(2,1)S(1)} %get-tuple-element.27), channel_id=1, source_target_pairs={{0,4},{1,5},{2,6},{3,7},{4,8},{5,9},{6,10},{7,11},{8,12},{9,13},{1... | collective-permute-start | bytes 737288 | tf_op jit(solution)/shard_map/ppermute | solution.py:362
  29.8 10.5 %collective-permute-start.6 = (bf16[64,1920]{1,0:T(8,128)(2,1)S(1)}, bf16[64,1920]{1,0:T(8,128)(2,1)S(1)}, u32[]{:S(2)}, u32[]{:S(2)}) collective-permute-start(bf16[64,1920]{1,0:T(8,128)(2,1)S(1)} %collective-permute-done.5.refs_2_), channel_id=1, source_target_pairs={{0,4},{1,5},{2,6},{3,7},{4,8},{5,9},{6,10},{7,11},{8,12},{9,13},{1... | collective-permute-start | bytes 737288 | tf_op jit(solution)/shard_map/ppermute | solution.py:362
  29.8 12.9 %collective-permute-start.8 = (bf16[64,1792]{1,0:T(8,128)(2,1)S(1)}, bf16[64,1792]{1,0:T(8,128)(2,1)S(1)}, u32[]{:S(2)}, u32[]{:S(2)}) collective-permute-start(bf16[64,1792]{1,0:T(8,128)(2,1)S(1)} %get-tuple-element.28), channel_id=1, source_target_pairs={{0,4},{1,5},{2,6},{3,7},{4,8},{5,9},{6,10},{7,11},{8,12},{9,13},{1... | collective-permute-start | bytes 688136 | tf_op jit(solution)/shard_map/ppermute | solution.py:362
  42.2 1.6 %collective-permute-start.7 = (f32[256,256]{1,0:T(8,128)S(1)}, f32[256,256]{1,0:T(8,128)S(1)}, u32[]{:S(2)}, u32[]{:S(2)}) collective-permute-start(f32[256,256]{1,0:T(8,128)S(1)} %shard_map.115.mine), channel_id=1, source_target_pairs={{0,1},{1,0},{2,3},{3,2},{4,5},{5,4},{6,7},{7,6},{8,9},{9,8},{10,11... | collective-permute-start | bytes 786440 | tf_op jit(solution)/shard_map/ppermute | solution.py:362
  42.7 9.4 %collective-permute-start.9 = (bf16[64,1792]{1,0:T(8,128)(2,1)S(1)}, bf16[64,1792]{1,0:T(8,128)(2,1)S(1)}, u32[]{:S(2)}, u32[]{:S(2)}) collective-permute-start(bf16[64,1792]{1,0:T(8,128)(2,1)S(1)} %collective-permute-done.8.refs_2_), channel_id=1, source_target_pairs={{0,4},{1,5},{2,6},{3,7},{4,8},{5,9},{6,10},{7,11},{8,12},{9,13},{1... | collective-permute-start | bytes 688136 | tf_op jit(solution)/shard_map/ppermute | solution.py:362
  54.8 7.9 %collective-permute-start.10 = (bf16[64,2176]{1,0:T(8,128)(2,1)S(1)}, bf16[64,2176]{1,0:T(8,128)(2,1)S(1)}, u32[]{:S(2)}, u32[]{:S(2)}) collective-permute-start(bf16[64,2176]{1,0:T(8,128)(2,1)S(1)} %get-tuple-element.31), channel_id=1, source_target_pairs={{0,2},{1,3},{2,0},{3,1},{4,6},{5,7},{6,4},{7,5},{8,10},{9,11},{10,... | collective-permute-start | bytes 835592 | tf_op jit(solution)/shard_map/ppermute | solution.py:362
  62.6 2.6 %copy-start.6 = (f32[3584]{0:T(1024)S(1)}, f32[3584]{0:T(1024)}, u32[]{:S(2)}) copy-start(f32[3584]{0:T(1024)} %param.15) | copy-start | bytes 43012
  63.2 4.6 %collective-permute-start.14 = (f32[8,256]{1,0:T(8,128)S(1)}, f32[8,256]{1,0:T(8,128)S(1)}, u32[]{:S(2)}, u32[]{:S(2)}) collective-permute-start(f32[8,256]{1,0:T(8,128)S(1)} %shard_map.120), channel_id=1, source_target_pairs={{0,12},{1,13},{2,14},{3,15},{4,0},{5,1},{6,2},{7,3},{8,4},{9,5},{1... | collective-permute-start | bytes 24584 | tf_op jit(solution)/shard_map/ppermute | solution.py:362
  63.2 4.6 %collective-permute-start.15 = (f32[8,256]{1,0:T(8,128)S(1)}, f32[8,256]{1,0:T(8,128)S(1)}, u32[]{:S(2)}, u32[]{:S(2)}) collective-permute-start(f32[8,256]{1,0:T(8,128)S(1)} %shard_map.120), channel_id=1, source_target_pairs={{0,8},{1,9},{2,10},{3,11},{4,12},{5,13},{6,14},{7,15},{8,0},{9,1},... | collective-permute-start | bytes 24584 | tf_op jit(solution)/shard_map/ppermute | solution.py:362
  63.5 5.8 %collective-permute-start.16 = (f32[8,256]{1,0:T(8,128)S(1)}, f32[8,256]{1,0:T(8,128)S(1)}, u32[]{:S(2)}, u32[]{:S(2)}) collective-permute-start(f32[8,256]{1,0:T(8,128)S(1)} %shard_map.120), channel_id=1, source_target_pairs={{0,4},{1,5},{2,6},{3,7},{4,8},{5,9},{6,10},{7,11},{8,12},{9,13},{1... | collective-permute-start | bytes 24584 | tf_op jit(solution)/shard_map/ppermute | solution.py:362
  65.3 12.4 %collective-permute-start.11 = (bf16[64,2176]{1,0:T(8,128)(2,1)S(1)}, bf16[64,2176]{1,0:T(8,128)(2,1)S(1)}, u32[]{:S(2)}, u32[]{:S(2)}) collective-permute-start(bf16[64,2176]{1,0:T(8,128)(2,1)S(1)} %get-tuple-element.32), channel_id=1, source_target_pairs={{0,16},{1,17},{2,18},{3,19},{4,20},{5,21},{6,22},{7,23},{8,24},{9,... | collective-permute-start | bytes 835592 | tf_op jit(solution)/shard_map/ppermute | solution.py:362
  66.4 11.3 %collective-permute-start.12 = (bf16[64,2176]{1,0:T(8,128)(2,1)S(1)}, bf16[64,2176]{1,0:T(8,128)(2,1)S(1)}, u32[]{:S(2)}, u32[]{:S(2)}) collective-permute-start(bf16[64,2176]{1,0:T(8,128)(2,1)S(1)} %get-tuple-element.33), channel_id=1, source_target_pairs={{0,18},{1,19},{2,16},{3,17},{4,22},{5,23},{6,20},{7,21},{8,26},{9,... | collective-permute-start | bytes 835592 | tf_op jit(solution)/shard_map/ppermute | solution.py:362
  69.4 9.0 %collective-permute-start.17 = (f32[64]{0:T(128)S(1)}, f32[64]{0:T(128)S(1)}, u32[]{:S(2)}, u32[]{:S(2)}) collective-permute-start(f32[64]{0:T(128)S(1)} %get-tuple-element.41), channel_id=1, source_target_pairs={{0,0},{1,16},{2,2},{3,18},{4,4},{5,20},{6,6},{7,22},{8,8},{9,24},{... | collective-permute-start | bytes 776 | tf_op jit(solution)/shard_map/ppermute | solution.py:362
  70.1 8.3 %collective-permute-start.18 = (f32[64]{0:T(128)S(1)}, f32[64]{0:T(128)S(1)}, u32[]{:S(2)}, u32[]{:S(2)}) collective-permute-start(f32[64]{0:T(128)S(1)} %get-tuple-element.40), channel_id=1, source_target_pairs={{0,16},{1,0},{2,18},{3,2},{4,20},{5,4},{6,22},{7,6},{8,24},{9,8},{... | collective-permute-start | bytes 776 | tf_op jit(solution)/shard_map/ppermute | solution.py:362
  77.6 2.2 %copy-start.3 = (bf16[32,3584]{1,0:T(8,128)(2,1)S(1)}, bf16[32,3584]{1,0:T(8,128)(2,1)}, u32[]{:S(2)}) copy-start(bf16[32,3584]{1,0:T(8,128)(2,1)} %res.3) | copy-start | bytes 688132
  78.3 1.5 %copy-start.5 = (s32[32,4]{0,1:T(4,128)S(1)}, s32[32,4]{0,1:T(4,128)}, u32[]{:S(2)}) copy-start(s32[32,4]{0,1:T(4,128)} %param.10) | copy-start | bytes 1540
  78.3 1.5 %collective-permute-start.13 = (bf16[32,2816]{1,0:T(8,128)(2,1)S(1)}, bf16[32,2816]{1,0:T(8,128)(2,1)S(1)}, u32[]{:S(2)}, u32[]{:S(2)}) collective-permute-start(bf16[32,2816]{1,0:T(8,128)(2,1)S(1)} %get-tuple-element.35), channel_id=1, source_target_pairs={{0,1},{1,0},{2,3},{3,2},{4,5},{5,4},{6,7},{7,6},{8,9},{9,8},{10,11... | collective-permute-start | bytes 540680 | tf_op jit(solution)/shard_map/ppermute | solution.py:362

commit v4 on v0

v4 whole, which is shorter than its diff:
```python
import functools

import jax
import jax.numpy as jnp
from jax import lax
from jax.experimental import pallas as pl
from jax.experimental.pallas import tpu as pltpu
from jax.sharding import PartitionSpec as P

AXES = ("groups", "lat", "seq")


def place_rows(values, source, filled, leading):
    picked = jnp.where(filled[:, None], values[source], jnp.zeros((), values.dtype))
    return picked.reshape(leading + (values.shape[-1],))


def move_tokens(residual, gradient, block_ids, jump_mask, encoder, enc_bias, decoder, dec_bias):
    tok_rows, width = residual.shape
    active = block_ids.shape[1]
    lanes = jump_mask.shape[2]
    lat_count = lax.axis_size("lat")
    seq_count = lax.axis_size("seq")
    local_blocks = encoder.shape[1] // lanes
    block_count = local_blocks * lat_count
    capacity = max(
        2, min(tok_rows, (3 * tok_rows * active + 2 * block_count - 1) // (2 * block_count))
    )
    slot_count = tok_rows * active
    flat_blocks = block_ids.reshape(slot_count)
    one_hot = (flat_blocks[:, None] == jnp.arange(block_count, dtype=jnp.int32)[None, :]).astype(
        jnp.int32
    )
    earlier = jnp.sum(jnp.cumsum(one_hot, axis=0) * one_hot, axis=1) - 1
    slot_id = flat_blocks * capacity + earlier
    owner_row = (
        jnp.zeros((block_count * capacity,), jnp.int32)
        .at[slot_id]
        .set(jnp.arange(slot_count, dtype=jnp.int32) + 1)
    )
    filled = owner_row > 0
    slot_source = jnp.maximum(owner_row - 1, 0)
    token_source = slot_source // active
    leading = (lat_count, local_blocks, capacity)
    enc_blocks = encoder.reshape(width, local_blocks, lanes)
    dec_blocks = decoder.reshape(local_blocks, lanes, width)
    bias_blocks = enc_bias.reshape(1, local_blocks, 1, lanes)
    mask_values = jump_mask.astype(jnp.float32)
    total_tokens = tok_rows * lat_count * seq_count
    factor = (total_tokens * active / block_count) ** (-0.5)

    def gather_home(slotted):
        last = slotted.shape[-1]
        return slotted.reshape(block_count * capacity, last)[slot_id].reshape(
            tok_rows, active, last
        )

    def swap(values):
        return lax.all_to_all(values, "lat", split_axis=0, concat_axis=0, tiled=True)

    residual_slots = place_rows(residual, token_source, filled, leading)
    gradient_slots = place_rows(gradient, token_source, filled, leading)
    preact = jnp.einsum(
        "sbcd,dbj->sbcj", swap(residual_slots), enc_blocks, preferred_element_type=jnp.float32
    )
    preact = swap((preact + bias_blocks).astype(jnp.bfloat16)).astype(jnp.float32)
    latent_codes = (gather_home(preact) * mask_values).astype(jnp.bfloat16)
    code_slots = place_rows(latent_codes.reshape(slot_count, lanes), slot_source, filled, leading)
    code_data = swap(code_slots)
    grad_data = swap(gradient_slots)
    score_data = code_data.astype(jnp.float32) * jnp.einsum(
        "sbcd,bjd->sbcj", grad_data, dec_blocks, preferred_element_type=jnp.float32
    )
    recon_data = jnp.einsum(
        "sbcj,bjd->sbcd", code_data, dec_blocks, preferred_element_type=jnp.float32
    )
    recon_home = gather_home(swap(recon_data.astype(jnp.bfloat16)))
    attribution = gather_home(swap(score_data))
    recon_error = (
        residual.astype(jnp.float32) - dec_bias - jnp.sum(recon_home.astype(jnp.float32), axis=1)
    ).astype(jnp.bfloat16)
    term = jnp.dot(
        one_hot.T.astype(jnp.float32),
        attribution.reshape(slot_count, lanes),
        precision=lax.Precision.HIGHEST,
    )
    latent_totals = (
        lax.psum_scatter(
            term.reshape(block_count * lanes), ("lat", "seq"), scatter_dimension=0, tiled=True
        )
        * factor
    )
    return (latent_codes, attribution, recon_error, latent_totals)


BF = jnp.bfloat16
F32 = jnp.float32


def nt(a, b):
    return lax.dot_general(a, b, (((1,), (1,)), ((), ())), preferred_element_type=F32)


def place_here():
    lat = lax.axis_index("lat")
    return lax.rem(lat, 2), lax.axis_index("groups"), lax.div(lat, 2), lax.axis_index("seq")


def call(kernel, outs, *args, far=(), scratch=(), vmem=24):
    return pl.pallas_call(
        kernel,
        in_specs=[
            pl.BlockSpec(memory_space=pl.ANY if i in far else pltpu.VMEM) for i in range(len(args))
        ],
        out_specs=[pl.BlockSpec(memory_space=pltpu.VMEM)] * len(outs),
        out_shape=[jax.ShapeDtypeStruct(*o) for o in outs],
        scratch_shapes=list(scratch),
        compiler_params=pltpu.CompilerParams(vmem_limit_bytes=vmem << 20),
    )(*args)


def pick_latents(per, lanes, y):
    row = lax.broadcasted_iota(jnp.int32, (per, lanes), 0)
    lane = lax.broadcasted_iota(jnp.int32, (per, lanes), 1)
    return (lane == row + per * y).astype(BF)


def weights_kernel(enc, dec, bias, out, enc_half, sem):
    _, y, _, s = place_here()
    lanes = enc.shape[1]
    half = enc_half.shape[0]
    per = out.shape[0]
    cols = pl.ds(pl.multiple_of(s * half, 128), half)
    get_enc = pltpu.make_async_copy(enc.at[cols, :], enc_half, sem.at[0])
    get_dec = pltpu.make_async_copy(
        dec.at[pl.ds(pl.multiple_of(y * per, 16), per), cols],
        out.at[:, pl.ds(half + 128, half)],
        sem.at[1],
    )
    get_enc.start()
    get_dec.start()
    pick = pick_latents(per, lanes, y)
    b = bias[...]
    hi = b.astype(BF).astype(F32)
    mid = (b - hi).astype(BF).astype(F32)
    low = b - hi - mid
    term = lax.broadcasted_iota(jnp.int32, (lanes, lanes), 0)
    terms = jnp.where(term == 0, hi, jnp.where(term == 1, mid, jnp.where(term == 2, low, 0.0)))
    out[:, half : half + 128] = nt(pick, terms.astype(BF)).astype(BF)
    get_enc.wait()
    out[:, :half] = nt(pick, enc_half[...]).astype(BF)
    get_dec.wait()


def totals_kernel(per, early, one, two, three, row, rest):
    _, y, _, s = place_here()
    total = early[:2, :per] + one[:2, per : 2 * per] + two[:2, :per] + three[:2, 3 * per :]
    row[...] = jnp.where(y == s, total[:1], total[1:])
    rest[...] = jnp.where(y == s, total[1:], total[:1])


def target_block(lane, m, x, z, ring):
    turn = z - 2 * m - (lane >= 64).astype(jnp.int32)
    turn = jnp.where(turn < 0, turn + ring, turn)
    return turn * 2 + x


def tokens_kernel(ring, res, grad, ids, jump, _, to_x, to_y, to_d, own_mask, sem):
    x, y, z, _ = place_here()
    tok, width = res.shape
    active = ids.shape[0]
    outs = (to_x, to_y, to_d)
    copies = []
    for i, src in enumerate((res, grad)):
        for j, out in enumerate(outs):
            copies.append(
                pltpu.make_async_copy(src, out.at[:, pl.ds(i * width, width)], sem.at[3 * i + j])
            )
    for copy in copies:
        copy.start()
    names = ids[...].T
    names = [jnp.broadcast_to(names[:, k : k + 1], (tok, 128)) for k in range(active)]
    lane = lax.broadcasted_iota(jnp.int32, (tok, 128), 1)
    low = lane < 64
    plain = [jump[:, k, :] for k in range(active)]
    moved = [pltpu.roll(v, 64, 1) for v in plain]
    for dest in range(4):
        x_rel, y_rel = dest % 2, dest // 2
        first = (y ^ y_rel) == 0
        for m in range(ring // 2):
            tgt = target_block(lane, m, x ^ x_rel, z, ring)
            total = jnp.zeros((tok, 128), jnp.int32)
            for k in range(active):
                value = jnp.where(low == first, plain[k], moved[k])
                total = total + jnp.where(names[k] == tgt, value, 0)
            out = total.astype(F32).astype(BF)
            if dest == 0:
                own_mask[:, m * 128 : m * 128 + 128] = out
            else:
                at = 2 * width + m * 128
                outs[dest - 1][:, at : at + 128] = out
    for copy in copies:
        copy.wait()


def group_sums(scores):
    half = scores.shape[0] // 2
    near = jnp.sum(scores[:half], axis=0, keepdims=True)
    far = jnp.sum(scores[half:], axis=0, keepdims=True)
    return jnp.concatenate([near, far, jnp.zeros((6, scores.shape[1]), F32)], axis=0)


def early_kernel(
    own, own_mask, from_x, from_y, from_d, enc, dec, mine_0, mine_1, other_1, mine_3, other_3,
    rows, mask, recon, codes, scores, sums, enc_half, other_0, sem,
):
    _, y, _, s = place_here()
    tok = own.shape[0]
    per, lanes = mine_0.shape[0], enc.shape[1]
    half = enc_half.shape[0]
    width = 2 * half
    far = pl.ds(pl.multiple_of((1 - s) * half, 128), half)
    get_enc = pltpu.make_async_copy(enc.at[far, :], enc_half, sem.at[0])
    get_dec = pltpu.make_async_copy(
        dec.at[pl.ds(pl.multiple_of(y * per, 16), per), far],
        other_0.at[:, pl.ds(half + 128, half)],
        sem.at[1],
    )
    get_enc.start()
    get_dec.start()
    for i, src in enumerate((own, from_x, from_y, from_d)):
        at = slice(i * tok, (i + 1) * tok)
        mask[at] = own_mask[...] if i == 0 else src[:, 2 * width :]
        for j in range(4):
            side = s if j % 2 == 0 else 1 - s
            cols = pl.ds(pl.multiple_of(width * (j // 2) + side * half, 128), half)
            rows[at, j * half : (j + 1) * half] = src[:, cols]
    get_enc.wait()
    other_0[:, :half] = nt(pick_latents(per, lanes, y), enc_half[...]).astype(BF)
    get_dec.wait()
    blank = jnp.zeros((per, half), BF)
    sides = ((mine_0, mine_1, mine_3), (other_0, other_1, other_3))

    def stack(parts, at, n):
        return jnp.concatenate(
            [parts[0][:, at : at + n], parts[1][:, at : at + n], blank[:, :n], parts[2][:, at : at + n]],
            axis=0,
        )

    preact = nt(jnp.ones((8, 128), BF), stack(sides[0], half, 128))[:1]
    for j, parts in enumerate(sides):
        preact = preact + nt(rows[:, j * half : (j + 1) * half], stack(parts, 0, half))
    code = (preact * mask[...].astype(F32)).astype(BF)
    codes[...] = code
    proj = jnp.zeros(code.shape, F32)
    for j, parts in enumerate(sides):
        weights = stack(parts, half + 128, half)
        proj = proj + nt(rows[:, (2 + j) * half : (3 + j) * half], weights)
        recon[:, j * half : (j + 1) * half] = jnp.dot(code, weights, preferred_element_type=F32)
    score = code.astype(F32) * proj
    scores[...] = score
    sums[...] = group_sums(score)


def late_kernel(
    rows, mask, recon, codes, scores, mine_2, other_2,
    own_recon, own_codes, own_scores, to_x, to_y, to_d, sums,
):
    _, _, _, s = place_here()
    per = mine_2.shape[0]
    tok = own_codes.shape[0]
    width = own_recon.shape[1]
    half = width // 2
    names = codes.shape[1]
    blank = jnp.zeros((per, half), BF)
    sides = (mine_2, other_2)

    def stack(part, at, n):
        return jnp.concatenate([part[:, at : at + n], blank[:, :n]], axis=0)

    preact = nt(jnp.ones((8, 128), BF), stack(mine_2, half, 128))[:1]
    for j, part in enumerate(sides):
        preact = preact + nt(rows[:, j * half : (j + 1) * half], stack(part, 0, half))
    code = (preact * mask[:, 2 * per :].astype(F32)).astype(BF)
    proj = jnp.zeros(code.shape, F32)
    outs = (own_recon, to_x, to_y, to_d)
    for j, part in enumerate(sides):
        weights = stack(part, half + 128, half)
        proj = proj + nt(rows[:, (2 + j) * half : (3 + j) * half], weights)
        total = recon[:, j * half : (j + 1) * half] + jnp.dot(
            code, weights, preferred_element_type=F32
        )
        cols = pl.ds(pl.multiple_of((s if j == 0 else 1 - s) * half, 128), half)
        for i, out in enumerate(outs):
            out[:, cols] = total[i * tok : (i + 1) * tok].astype(out.dtype)
    score = code.astype(F32) * proj
    sums[...] = group_sums(score)
    all_codes = jnp.concatenate([codes[:, : 2 * per], code + codes[:, 2 * per :]], axis=1)
    all_scores = jnp.concatenate([scores[:, : 2 * per], score + scores[:, 2 * per :]], axis=1)
    own_codes[...] = all_codes[:tok]
    own_scores[...] = all_scores[:tok]
    for i, out in enumerate((to_x, to_y, to_d)):
        at = slice((i + 1) * tok, (i + 2) * tok)
        out[:, width : width + names] = all_codes[at]
        out[:, width + names :] = all_scores[at].astype(BF)


def final_kernel(
    ring, factor, own_recon, own_codes, own_scores, from_x, from_y, from_d, own, dec_bias, ids, row, rest,
    out_codes, out_scores, out_error, out_totals,
):
    x, y, z, _ = place_here()
    out_totals[...] = (row[...] + rest[...]) * factor
    tok, width = own_recon.shape
    names = own_codes.shape[1]
    active = ids.shape[0]
    named = ids[...].T
    named = [jnp.broadcast_to(named[:, k : k + 1], (tok, 128)) for k in range(active)]
    others = (from_x, from_y, from_d)
    recon = own_recon[...]
    for src in others:
        recon = recon + src[:, :width].astype(F32)
    out_error[...] = (own[:, :width].astype(F32) - dec_bias[...] - recon).astype(BF)
    code_src = [own_codes[...].astype(F32)]
    score_src = [own_scores[...]]
    for src in others:
        code_src.append(src[:, width : width + names].astype(F32))
        score_src.append(src[:, width + names :].astype(F32))
    lane = lax.broadcasted_iota(jnp.int32, (tok, 128), 1)
    low = lane < 64
    code_out = [jnp.zeros((tok, 128), F32)] * active
    score_out = [jnp.zeros((tok, 128), F32)] * active
    for x_rel in range(2):
        for kk in range(ring):
            cols = slice(128 * (kk // 2), 128 * (kk // 2) + 128)
            turn = z - kk
            turn = jnp.where(turn < 0, turn + ring, turn)
            block = turn * 2 + (x ^ x_rel)
            pair = []
            for src in (code_src, score_src):
                near, far = src[x_rel][:, cols], src[2 + x_rel][:, cols]
                first = jnp.where(y == 0, near, far)
                second = jnp.where(y == 0, far, near)
                if kk % 2 == 0:
                    pair.append(jnp.where(low, first, pltpu.roll(second, 64, 1)))
                else:
                    pair.append(jnp.where(low, pltpu.roll(first, 64, 1), second))
            for k in range(active):
                hit = named[k] == block
                code_out[k] = code_out[k] + jnp.where(hit, pair[0], 0.0)
                score_out[k] = score_out[k] + jnp.where(hit, pair[1], 0.0)
    for k in range(active):
        out_codes[:, k, :] = code_out[k].astype(BF)
        out_scores[:, k, :] = score_out[k]


def move_weights(residual, gradient, block_ids, jump_mask, encoder, enc_bias, decoder, dec_bias):
    tok, width = residual.shape
    active = block_ids.shape[1]
    lanes = jump_mask.shape[2]
    lat_count = lax.axis_size("lat")
    ring = lat_count // 2
    per = lanes // 2
    half = width // 2
    names = ring * per

    def permute(values, to):
        pairs = []
        for gg in range(2):
            for ll in range(lat_count):
                for ss in range(2):
                    a, b, c = to(gg, ll, ss)
                    pairs.append(((gg * lat_count + ll) * 2 + ss, (a * lat_count + b) * 2 + c))
        return lax.ppermute(values, AXES, pairs)

    def by_x(v):
        return permute(v, lambda gg, ll, ss: (gg, ll ^ 1, ss))

    def by_y(v):
        return permute(v, lambda gg, ll, ss: (1 - gg, ll, ss))

    def by_xy(v):
        return permute(v, lambda gg, ll, ss: (1 - gg, ll ^ 1, ss))

    def by_core(v):
        return permute(v, lambda gg, ll, ss: (gg, ll, 1 - ss))

    def by_z(v, k):
        return permute(v, lambda gg, ll, ss: (gg, (ll + 2 * k) % lat_count, ss))

    (own,) = call(
        weights_kernel,
        [((per, 2 * half + 128), BF)],
        encoder, decoder, enc_bias.reshape(1, lanes),
        far=(0, 1),
        scratch=[pltpu.VMEM((half, lanes), BF), pltpu.SemaphoreType.DMA((2,))],
    )
    part_1 = by_z(own, 1)
    part_3 = by_z(own, -1)
    part_2 = by_z(part_1, 1)

    to_x, to_y, to_d, own_mask = call(
        functools.partial(tokens_kernel, ring),
        [((tok, 2 * width + names), BF)] * 3 + [((tok, names), BF)],
        residual, gradient, block_ids.T, jump_mask, own,
        far=(0, 1, 4),
        scratch=[pltpu.SemaphoreType.DMA((6,))],
    )
    own_rows = to_x
    rows, mask, recon, codes, scores, sums = call(
        early_kernel,
        [
            ((4 * tok, 2 * width), BF),
            ((4 * tok, names), BF),
            ((4 * tok, width), F32),
            ((4 * tok, names), BF),
            ((4 * tok, names), F32),
            ((8, names), F32),
        ],
        own_rows, own_mask, by_x(to_x), by_y(to_y), by_xy(to_d), encoder, decoder,
        own, part_1, by_core(part_1), part_3, by_core(part_3),
        far=(5, 6),
        scratch=[
            pltpu.VMEM((half, lanes), BF),
            pltpu.VMEM((per, 2 * half + 128), BF),
            pltpu.SemaphoreType.DMA((2,)),
        ],
    )
    own_recon, own_codes, own_scores, to_x, to_y, to_d, sums_2 = call(
        late_kernel,
        [((tok, width), F32), ((tok, names), BF), ((tok, names), F32)]
        + [((tok, width + 2 * names), BF)] * 3
        + [((8, 2 * per), F32)],
        rows, mask, recon, codes, scores, part_2, by_core(part_2),
    )
    from_d = by_xy(to_d)
    from_x = by_x(to_x)
    from_y = by_y(to_y)

    row, rest = call(
        functools.partial(totals_kernel, per),
        [((1, per), F32)] * 2,
        sums, by_z(sums, -1), by_z(sums_2, -2), by_z(sums, 1),
    )
    factor = (tok * lat_count * 2 * active / lat_count) ** (-0.5)
    latent_codes, attribution, recon_error, latent_totals = call(
        functools.partial(final_kernel, ring, factor),
        [
            ((tok, active, lanes), BF),
            ((tok, active, lanes), F32),
            ((tok, width), BF),
            ((1, per), F32),
        ],
        own_recon, own_codes, own_scores, from_x, from_y, from_d,
        own_rows, dec_bias.reshape(1, width), block_ids.T,
        permute(row, lambda gg, ll, ss: (ss, ll, gg)),
        permute(rest, lambda gg, ll, ss: (1 - ss, ll, gg)),
    )
    return (latent_codes, attribution, recon_error, latent_totals.reshape(per))


def solution(mesh):
    sizes = dict(mesh.shape)

    def on_device(residual, gradient, block_ids, jump_mask, encoder, enc_bias, decoder, dec_bias):
        lanes = jump_mask.shape[2]
        small = (
            sizes["groups"] == 2
            and sizes["seq"] == 2
            and sizes["lat"] == 8
            and encoder.shape[1] == lanes
            and lanes == 128
            and residual.shape[0] % 16 == 0
            and residual.shape[1] % 256 == 0
        )
        body = move_weights if small else move_tokens
        return body(
            residual, gradient, block_ids, jump_mask, encoder, enc_bias, decoder, dec_bias
        )

    rows = P(("groups", "lat", "seq"), None)
    cubes = P(("groups", "lat", "seq"), None, None)
    return jax.shard_map(
        on_device,
        mesh=mesh,
        in_specs=(rows, rows, rows, cubes, P(None, "lat"), P("lat"), P("lat", None), P()),
        out_specs=(cubes, cubes, rows, P(("groups", "lat", "seq"))),
        check_vma=False,
    )
```

time: 177 us -> 67.3 us (0.38)
  blocking collectives: 106 us -> 0 us
  starting transfers between devices: 10.6 us -> 22.1 us
  local copies, waits for them, and re-layouts: 12.7 us -> 3.88 us
  Pallas kernels: 0 us -> 7.47 us
  other arithmetic: 6.36 us -> 0 us
  matrix products: 3.48 us -> 0 us
  waiting for transfers between devices: 35.4 us -> 32.1 us
    all_to_all x3 -> x0, blocking collectives: 60.1 us -> none  [the longest x1 40.6 us: on_device(): lax.all_to_all(residual_slots, 'lat', split_axis=0, concat_axis=0, tiled=...]
    unnamed x1 -> x0, blocking collectives: 45.8 us -> none
    all_to_all x3 -> x0, waiting for transfers between devices: 35.4 us -> none  [the longest x1 29.9 us: on_device(): lax.all_to_all(gradient_slots, 'lat', split_axis=0, concat_axis=0, tiled=...]
    ppermute x0 -> x17, waiting for transfers between devices: none -> 32.1 us  [permute(): return lax.ppermute(values, AXES, pairs)]
    ppermute x0 -> x17, starting transfers between devices: none -> 22.1 us  [permute(): return lax.ppermute(values, AXES, pairs)]
    all_to_all x3 -> x0, starting transfers between devices: 10.6 us -> none  [the longest x1 3.7 us: on_device(): lax.all_to_all(gradient_slots, 'lat', split_axis=0, concat_axis=0, tiled=...]
    gather x6 -> x0, local copies, waits for them, and re-layouts: 8.09 us -> none  [the longest x3 4.73 us: place_rows(): values[source]]
    pallas_call x0 -> x6, Pallas kernels: none -> 7.47 us  [call(): pl.pallas_call(kernel, in_specs=[pl.BlockSpec(memory_space=pl.ANY if i in...]
  transfers between devices with their start and end apart: 3 -> 17, of which waited for: 2 -> 8; matrix products, arithmetic and copies ran while one was open for 3% -> 0% of each run, Pallas kernels for 0% -> 6%
where the time goes in v4:
time: 67.3 us; the launch traced here: 66.3 us
  waiting for transfers between devices  32.1 us (48%)
  starting transfers between devices  22.1 us (33%)
  Pallas kernels  7.47 us (11%)
  local copies, waits for them, and re-layouts  3.88 us (6%)
  between operations  0.77 us (1%)
    ppermute x17, waiting for transfers between devices, permute(): return lax.ppermute(values, AXES, pairs)  32.1 us
    ppermute x17, starting transfers between devices, permute(): return lax.ppermute(values, AXES, pairs)  22.1 us
    pallas_call x6, Pallas kernels, call(): pl.pallas_call(kernel, in_specs=[pl.BlockSpec(memory_space=pl.ANY if i in...  7.47 us
    unnamed x20, local copies, waits for them, and re-layouts  3.87 us
  transfers between devices with their start and end apart: 17, of which 8 were waited for; matrix products, arithmetic and copies ran while one was open for 0% of the time, Pallas kernels for 6%

profile of v4, /device:TPU:0, one launch (start us, length us, event | category | flops | bytes accessed | tf_op | source)
XLA Modules:
  0.0 66.3 jit_solution(18153832452902238266)
XLA Ops:
  0.6 1.2 %copy-done = bf16[3584,128]{1,0:T(8,128)(2,1)S(1)} copy-done((bf16[3584,128]{1,0:T(8,128)(2,1)S(1)}, bf16[3584,128]{1,0:T(8,128)(2,1)}, u32[]{:S(2)}) %copy-start) | copy-done | bytes 917528
  1.8 1.2 %copy-done.2 = bf16[128,3584]{1,0:T(8,128)(2,1)S(1)} copy-done((bf16[128,3584]{1,0:T(8,128)(2,1)S(1)}, bf16[128,3584]{1,0:T(8,128)(2,1)}, u32[]{:S(2)}) %copy-start.2) | copy-done | bytes 917528
  3.0 0.7 copy-done.8
  3.7 0.8 %shard_map.111._.mine_0 = bf16[64,3712]{1,0:T(8,128)(2,1)S(1)} custom-call(bf16[3584,128]{1,0:T(8,128)(2,1)S(1)} %copy-done, bf16[128,3584]{1,0:T(8,128)(2,1)S(1)} %copy-done.2, f32[1,128]{1,0:T(1,128)S(1)} %bitcast.5), custom_call_target="tpu_custom_call" | custom-call | tf_op jit(solution)/shard_map/pallas_call | solution.py:110
  4.4 3.1 %collective-permute-start.3 = (bf16[64,3712]{1,0:T(8,128)(2,1)S(1)}, bf16[64,3712]{1,0:T(8,128)(2,1)S(1)}, u32[]{:S(2)}, u32[]{:S(2)}) collective-permute-start(bf16[64,3712]{1,0:T(8,128)(2,1)S(1)} %shard_map.111._.mine_0), channel_id=1, source_target_pairs={{0,4},{1,5},{2,6},{3,7},{4,8},{5,9},{6,10},{7,11},{8,12},{9,13},{1... | collective-permute-start | bytes 1425416 | tf_op jit(solution)/shard_map/ppermute | solution.py:374
  7.5 0.8 %copy-done.6 = s32[32,4,128]{2,1,0:T(4,128)S(1)} copy-done((s32[32,4,128]{2,1,0:T(4,128)S(1)}, s32[32,4,128]{2,1,0:T(4,128)}, u32[]{:S(2)}) %copy-start.6) | copy-done | bytes 65560
  8.4 0.7 %shard_map.112 = (bf16[32,7424]{1,0:T(8,128)(2,1)S(1)}, bf16[32,7424]{1,0:T(8,128)(2,1)S(1)}, bf16[32,7424]{1,0:T(8,128)(2,1)S(1)}, bf16[32,256]{1,0:T(8,128)(2,1)S(1)}) custom-call(bf16[32,3584]{1,0:T(8,128)(2,1)S(1)} %copy-done.4, bf16[32,3584]{1,0:T(8,128)(2,1)S(1)} %copy-done.5, s32[4,32]{1,0:T(4,128)S(1)} %bitcast.3, s32[32,4,128]{2,1,0:T(4,128)S(1)} %copy-done.6, ...), custom_call_target="tpu_custom_call" | custom-call | tf_op jit(solution)/shard_map/pallas_call | solution.py:110
  9.0 1.6 %collective-permute-start = (bf16[32,7424]{1,0:T(8,128)(2,1)S(1)}, bf16[32,7424]{1,0:T(8,128)(2,1)S(1)}, u32[]{:S(2)}, u32[]{:S(2)}) collective-permute-start(bf16[32,7424]{1,0:T(8,128)(2,1)S(1)} %get-tuple-element.27.own), channel_id=1, source_target_pairs={{0,2},{1,3},{2,0},{3,1},{4,6},{5,7},{6,4},{7,5},{8,10},{9,11},{10,... | collective-permute-start | bytes 1425416 | tf_op jit(solution)/shard_map/ppermute | solution.py:374
  10.6 2.2 %collective-permute-start.5 = (bf16[64,3712]{1,0:T(8,128)(2,1)S(1)}, bf16[64,3712]{1,0:T(8,128)(2,1)S(1)}, u32[]{:S(2)}, u32[]{:S(2)}) collective-permute-start(bf16[64,3712]{1,0:T(8,128)(2,1)S(1)} %shard_map.111._.mine_0), channel_id=1, source_target_pairs={{0,12},{1,13},{2,14},{3,15},{4,0},{5,1},{6,2},{7,3},{8,4},{9,5},{1... | collective-permute-start | bytes 1425416 | tf_op jit(solution)/shard_map/ppermute | solution.py:374
  12.9 8.4 %collective-permute-done.3.mine_1 = bf16[64,3712]{1,0:T(8,128)(2,1)S(1)} collective-permute-done((bf16[64,3712]{1,0:T(8,128)(2,1)S(1)}, bf16[64,3712]{1,0:T(8,128)(2,1)S(1)}, u32[]{:S(2)}, u32[]{:S(2)}) %collective-permute-start.3) | collective-permute-done | bytes 475168 | tf_op jit(solution)/shard_map/ppermute | solution.py:374
  21.3 1.8 %collective-permute-start.1 = (bf16[32,7424]{1,0:T(8,128)(2,1)S(1)}, bf16[32,7424]{1,0:T(8,128)(2,1)S(1)}, u32[]{:S(2)}, u32[]{:S(2)}) collective-permute-start(bf16[32,7424]{1,0:T(8,128)(2,1)S(1)} %get-tuple-element.29), channel_id=1, source_target_pairs={{0,16},{1,17},{2,18},{3,19},{4,20},{5,21},{6,22},{7,23},{8,24},{9,... | collective-permute-start | bytes 1425416 | tf_op jit(solution)/shard_map/ppermute | solution.py:374
  23.1 1.4 %collective-permute-start.2 = (bf16[32,7424]{1,0:T(8,128)(2,1)S(1)}, bf16[32,7424]{1,0:T(8,128)(2,1)S(1)}, u32[]{:S(2)}, u32[]{:S(2)}) collective-permute-start(bf16[32,7424]{1,0:T(8,128)(2,1)S(1)} %get-tuple-element.30), channel_id=1, source_target_pairs={{0,18},{1,19},{2,16},{3,17},{4,22},{5,23},{6,20},{7,21},{8,26},{9,... | collective-permute-start | bytes 1425416 | tf_op jit(solution)/shard_map/ppermute | solution.py:374
  24.5 0.0 collective-permute-done.from_x
  24.5 6.9 %collective-permute-done.5.mine_3 = bf16[64,3712]{1,0:T(8,128)(2,1)S(1)} collective-permute-done((bf16[64,3712]{1,0:T(8,128)(2,1)S(1)}, bf16[64,3712]{1,0:T(8,128)(2,1)S(1)}, u32[]{:S(2)}, u32[]{:S(2)}) %collective-permute-start.5) | collective-permute-done | bytes 475168 | tf_op jit(solution)/shard_map/ppermute | solution.py:374
  31.4 9.4 %collective-permute-done.7.mine_2 = bf16[64,3712]{1,0:T(8,128)(2,1)S(1)} collective-permute-done((bf16[64,3712]{1,0:T(8,128)(2,1)S(1)}, bf16[64,3712]{1,0:T(8,128)(2,1)S(1)}, u32[]{:S(2)}, u32[]{:S(2)}) %collective-permute-start.7) | collective-permute-done | bytes 475168 | tf_op jit(solution)/shard_map/ppermute | solution.py:374
  40.8 1.9 %collective-permute-done.1.from_y = bf16[32,7424]{1,0:T(8,128)(2,1)S(1)} collective-permute-done((bf16[32,7424]{1,0:T(8,128)(2,1)S(1)}, bf16[32,7424]{1,0:T(8,128)(2,1)S(1)}, u32[]{:S(2)}, u32[]{:S(2)}) %collective-permute-start.1) | collective-permute-done | bytes 475168 | tf_op jit(solution)/shard_map/ppermute | solution.py:374
  42.7 3.2 %shard_map.113 = (bf16[128,7168]{1,0:T(8,128)(2,1)S(1)}, bf16[128,256]{1,0:T(8,128)(2,1)S(1)}, f32[128,3584]{1,0:T(8,128)S(1)}, bf16[128,256]{1,0:T(8,128)(2,1)S...) custom-call(bf16[32,7424]{1,0:T(8,128)(2,1)S(1)} %get-tuple-element.27.own, ...), custom_call_target="tpu_custom_call" | custom-call | tf_op jit(solution)/shard_map/pallas_call | solution.py:110
  46.0 0.0 copy-start.9
  46.0 1.4 %shard_map.114 = (f32[32,3584]{1,0:T(8,128)S(1)}, bf16[32,256]{1,0:T(8,128)(2,1)S(1)}, f32[32,256]{1,0:T(8,128)S(1)}, bf16[32,4096]{1,0:T(8,128)(2,1)S(1)}, bf16...) custom-call(bf16[128,7168]{1,0:T(8,128)(2,1)S(1)} %get-tuple-element.31.rows, ...), custom_call_target="tpu_custom_call" | custom-call | tf_op jit(solution)/shard_map/pallas_call | solution.py:110
  47.4 1.3 %collective-permute-start.10 = (bf16[32,4096]{1,0:T(8,128)(2,1)S(1)}, bf16[32,4096]{1,0:T(8,128)(2,1)S(1)}, u32[]{:S(2)}, u32[]{:S(2)}) collective-permute-start(bf16[32,4096]{1,0:T(8,128)(2,1)S(1)} %get-tuple-element.40), channel_id=1, source_target_pairs={{0,16},{1,17},{2,18},{3,19},{4,20},{5,21},{6,22},{7,23},{8,24},{9,... | collective-permute-start | bytes 786440 | tf_op jit(solution)/shard_map/ppermute | solution.py:374
  48.8 1.4 %collective-permute-start.11 = (bf16[32,4096]{1,0:T(8,128)(2,1)S(1)}, bf16[32,4096]{1,0:T(8,128)(2,1)S(1)}, u32[]{:S(2)}, u32[]{:S(2)}) collective-permute-start(bf16[32,4096]{1,0:T(8,128)(2,1)S(1)} %get-tuple-element.41), channel_id=1, source_target_pairs={{0,18},{1,19},{2,16},{3,17},{4,22},{5,23},{6,20},{7,21},{8,26},{9,... | collective-permute-start | bytes 786440 | tf_op jit(solution)/shard_map/ppermute | solution.py:374
  50.2 0.8 %collective-permute-start.9 = (bf16[32,4096]{1,0:T(8,128)(2,1)S(1)}, bf16[32,4096]{1,0:T(8,128)(2,1)S(1)}, u32[]{:S(2)}, u32[]{:S(2)}) collective-permute-start(bf16[32,4096]{1,0:T(8,128)(2,1)S(1)} %get-tuple-element.39), channel_id=1, source_target_pairs={{0,2},{1,3},{2,0},{3,1},{4,6},{5,7},{6,4},{7,5},{8,10},{9,11},{10,... | collective-permute-start | bytes 786440 | tf_op jit(solution)/shard_map/ppermute | solution.py:374
  51.0 3.5 %collective-permute-start.12 = (f32[8,256]{1,0:T(8,128)S(1)}, f32[8,256]{1,0:T(8,128)S(1)}, u32[]{:S(2)}, u32[]{:S(2)}) collective-permute-start(f32[8,256]{1,0:T(8,128)S(1)} %get-tuple-element.42.early), channel_id=1, source_target_pairs={{0,12},{1,13},{2,14},{3,15},{4,0},{5,1},{6,2},{7,3},{8,4},{9,5},{1... | collective-permute-start | bytes 24584 | tf_op jit(solution)/shard_map/ppermute | solution.py:374
  54.5 1.4 %collective-permute-done.12.one = f32[8,256]{1,0:T(8,128)S(1)} collective-permute-done((f32[8,256]{1,0:T(8,128)S(1)}, f32[8,256]{1,0:T(8,128)S(1)}, u32[]{:S(2)}, u32[]{:S(2)}) %collective-permute-start.12) | collective-permute-done | bytes 8224 | tf_op jit(solution)/shard_map/ppermute | solution.py:374
  55.9 1.7 %collective-permute-start.13 = (f32[8,128]{1,0:T(8,128)S(1)}, f32[8,128]{1,0:T(8,128)S(1)}, u32[]{:S(2)}, u32[]{:S(2)}) collective-permute-start(f32[8,128]{1,0:T(8,128)S(1)} %get-tuple-element.43), channel_id=1, source_target_pairs={{0,8},{1,9},{2,10},{3,11},{4,12},{5,13},{6,14},{7,15},{8,0},{9,1},... | collective-permute-start | bytes 12296 | tf_op jit(solution)/shard_map/ppermute | solution.py:374
  57.6 2.4 %collective-permute-done.14.three = f32[8,256]{1,0:T(8,128)S(1)} collective-permute-done((f32[8,256]{1,0:T(8,128)S(1)}, f32[8,256]{1,0:T(8,128)S(1)}, u32[]{:S(2)}, u32[]{:S(2)}) %collective-permute-start.14) | collective-permute-done | bytes 8224 | tf_op jit(solution)/shard_map/ppermute | solution.py:374
  60.0 0.4 collective-permute-done.13.two
  60.4 0.1 shard_map.115
  60.5 0.7 collective-permute-start.15
  61.1 2.5 %collective-permute-start.16 = (f32[1,64]{1,0:T(1,128)S(1)}, f32[1,64]{1,0:T(1,128)S(1)}, u32[]{:S(2)}, u32[]{:S(2)}) collective-permute-start(f32[1,64]{1,0:T(1,128)S(1)} %get-tuple-element.45), channel_id=1, source_target_pairs={{0,16},{1,0},{2,18},{3,2},{4,20},{5,4},{6,22},{7,6},{8,24},{9,8},{... | collective-permute-start | bytes 776 | tf_op jit(solution)/shard_map/ppermute | solution.py:374
  63.7 1.3 %collective-permute-done.16.rest = f32[1,64]{1,0:T(1,128)S(1)} collective-permute-done((f32[1,64]{1,0:T(1,128)S(1)}, f32[1,64]{1,0:T(1,128)S(1)}, u32[]{:S(2)}, u32[]{:S(2)}) %collective-permute-start.16) | collective-permute-done | bytes 288 | tf_op jit(solution)/shard_map/ppermute | solution.py:374
  65.0 1.3 %shard_map.116 = (bf16[32,4,128]{2,1,0:T(4,128)(2,1)}, f32[32,4,128]{2,1,0:T(4,128)}, bf16[32,3584]{1,0:T(8,128)(2,1)}, f32[1,64]{1,0:T(1,128)}) custom-call(f32[32,3584]{1,0:T(8,128)S(1)} %get-tuple-element.36.own_recon, bf16[32,256]{1,0:T(8,128)(2,1)S(1)} %get-tuple-element.37.own_codes, f32[32,256]{1,0:T(8,128)S(1)} %get-tuple-element.38.own_scores, ...), custom_call_target="tpu_custom_call" | custom-call | tf_op jit(solution)/shard_map/pallas_call | solution.py:110
  (29 shorter events, 0.1 us)
Async XLA Ops:
  0.6 1.2 %copy-start = (bf16[3584,128]{1,0:T(8,128)(2,1)S(1)}, bf16[3584,128]{1,0:T(8,128)(2,1)}, u32[]{:S(2)}) copy-start(bf16[3584,128]{1,0:T(8,128)(2,1)} %enc.3) | copy-start | bytes 2752516
  1.8 1.2 %copy-start.2 = (bf16[128,3584]{1,0:T(8,128)(2,1)S(1)}, bf16[128,3584]{1,0:T(8,128)(2,1)}, u32[]{:S(2)}) copy-start(bf16[128,3584]{1,0:T(8,128)(2,1)} %dec.3) | copy-start | bytes 2752516
  3.0 0.7 copy-start.8
  3.6 3.9 %copy-start.4 = (bf16[32,3584]{1,0:T(8,128)(2,1)S(1)}, bf16[32,3584]{1,0:T(8,128)(2,1)}, u32[]{:S(2)}) copy-start(bf16[32,3584]{1,0:T(8,128)(2,1)} %res.1) | copy-start | bytes 688132
  3.6 3.9 %copy-start.5 = (bf16[32,3584]{1,0:T(8,128)(2,1)S(1)}, bf16[32,3584]{1,0:T(8,128)(2,1)}, u32[]{:S(2)}) copy-start(bf16[32,3584]{1,0:T(8,128)(2,1)} %grad.1) | copy-start | bytes 688132
  3.7 3.9 %copy-start.7 = (s32[32,4]{0,1:T(4,128)S(1)}, s32[32,4]{0,1:T(4,128)}, u32[]{:S(2)}) copy-start(s32[32,4]{0,1:T(4,128)} %param.10) | copy-start | bytes 1540
  3.7 39.1 %copy-start.1 = (bf16[3584,128]{1,0:T(8,128)(2,1)S(1)}, bf16[3584,128]{1,0:T(8,128)(2,1)}, u32[]{:S(2)}) copy-start(bf16[3584,128]{1,0:T(8,128)(2,1)} %enc.3) | copy-start | bytes 2752516
  3.7 39.1 %copy-start.3 = (bf16[128,3584]{1,0:T(8,128)(2,1)S(1)}, bf16[128,3584]{1,0:T(8,128)(2,1)}, u32[]{:S(2)}) copy-start(bf16[128,3584]{1,0:T(8,128)(2,1)} %dec.3) | copy-start | bytes 2752516
  4.4 16.8 %collective-permute-start.3 = (bf16[64,3712]{1,0:T(8,128)(2,1)S(1)}, bf16[64,3712]{1,0:T(8,128)(2,1)S(1)}, u32[]{:S(2)}, u32[]{:S(2)}) collective-permute-start(bf16[64,3712]{1,0:T(8,128)(2,1)S(1)} %shard_map.111._.mine_0), channel_id=1, source_target_pairs={{0,4},{1,5},{2,6},{3,7},{4,8},{5,9},{6,10},{7,11},{8,12},{9,13},{1... | collective-permute-start | bytes 1425416 | tf_op jit(solution)/shard_map/ppermute | solution.py:374
  7.5 0.8 %copy-start.6 = (s32[32,4,128]{2,1,0:T(4,128)S(1)}, s32[32,4,128]{2,1,0:T(4,128)}, u32[]{:S(2)}) copy-start(s32[32,4,128]{2,1,0:T(4,128)} %jump.1) | copy-start | bytes 196612
  9.0 15.5 %collective-permute-start = (bf16[32,7424]{1,0:T(8,128)(2,1)S(1)}, bf16[32,7424]{1,0:T(8,128)(2,1)S(1)}, u32[]{:S(2)}, u32[]{:S(2)}) collective-permute-start(bf16[32,7424]{1,0:T(8,128)(2,1)S(1)} %get-tuple-element.27.own), channel_id=1, source_target_pairs={{0,2},{1,3},{2,0},{3,1},{4,6},{5,7},{6,4},{7,5},{8,10},{9,11},{10,... | collective-permute-start | bytes 1425416 | tf_op jit(solution)/shard_map/ppermute | solution.py:374
  10.6 20.8 %collective-permute-start.5 = (bf16[64,3712]{1,0:T(8,128)(2,1)S(1)}, bf16[64,3712]{1,0:T(8,128)(2,1)S(1)}, u32[]{:S(2)}, u32[]{:S(2)}) collective-permute-start(bf16[64,3712]{1,0:T(8,128)(2,1)S(1)} %shard_map.111._.mine_0), channel_id=1, source_target_pairs={{0,12},{1,13},{2,14},{3,15},{4,0},{5,1},{6,2},{7,3},{8,4},{9,5},{1... | collective-permute-start | bytes 1425416 | tf_op jit(solution)/shard_map/ppermute | solution.py:374
  21.3 19.5 %collective-permute-start.7 = (bf16[64,3712]{1,0:T(8,128)(2,1)S(1)}, bf16[64,3712]{1,0:T(8,128)(2,1)S(1)}, u32[]{:S(2)}, u32[]{:S(2)}) collective-permute-start(bf16[64,3712]{1,0:T(8,128)(2,1)S(1)} %collective-permute-done.3.mine_1), channel_id=1, source_target_pairs={{0,4},{1,5},{2,6},{3,7},{4,8},{5,9},{6,10},{7,11},{8,12},{9,13},{1... | collective-permute-start | bytes 1425416 | tf_op jit(solution)/shard_map/ppermute | solution.py:374
  21.3 21.4 %collective-permute-start.1 = (bf16[32,7424]{1,0:T(8,128)(2,1)S(1)}, bf16[32,7424]{1,0:T(8,128)(2,1)S(1)}, u32[]{:S(2)}, u32[]{:S(2)}) collective-permute-start(bf16[32,7424]{1,0:T(8,128)(2,1)S(1)} %get-tuple-element.29), channel_id=1, source_target_pairs={{0,16},{1,17},{2,18},{3,19},{4,20},{5,21},{6,22},{7,23},{8,24},{9,... | collective-permute-start | bytes 1425416 | tf_op jit(solution)/shard_map/ppermute | solution.py:374
  23.1 19.6 %collective-permute-start.2 = (bf16[32,7424]{1,0:T(8,128)(2,1)S(1)}, bf16[32,7424]{1,0:T(8,128)(2,1)S(1)}, u32[]{:S(2)}, u32[]{:S(2)}) collective-permute-start(bf16[32,7424]{1,0:T(8,128)(2,1)S(1)} %get-tuple-element.30), channel_id=1, source_target_pairs={{0,18},{1,19},{2,16},{3,17},{4,22},{5,23},{6,20},{7,21},{8,26},{9,... | collective-permute-start | bytes 1425416 | tf_op jit(solution)/shard_map/ppermute | solution.py:374
  24.5 18.2 %collective-permute-start.4 = (bf16[64,3712]{1,0:T(8,128)(2,1)S(1)}, bf16[64,3712]{1,0:T(8,128)(2,1)S(1)}, u32[]{:S(2)}, u32[]{:S(2)}) collective-permute-start(bf16[64,3712]{1,0:T(8,128)(2,1)S(1)} %collective-permute-done.3.mine_1), channel_id=1, source_target_pairs={{0,1},{1,0},{2,3},{3,2},{4,5},{5,4},{6,7},{7,6},{8,9},{9,8},{10,11... | collective-permute-start | bytes 1425416 | tf_op jit(solution)/shard_map/ppermute | solution.py:374
  31.4 11.3 %collective-permute-start.6 = (bf16[64,3712]{1,0:T(8,128)(2,1)S(1)}, bf16[64,3712]{1,0:T(8,128)(2,1)S(1)}, u32[]{:S(2)}, u32[]{:S(2)}) collective-permute-start(bf16[64,3712]{1,0:T(8,128)(2,1)S(1)} %collective-permute-done.5.mine_3), channel_id=1, source_target_pairs={{0,1},{1,0},{2,3},{3,2},{4,5},{5,4},{6,7},{7,6},{8,9},{9,8},{10,11... | collective-permute-start | bytes 1425416 | tf_op jit(solution)/shard_map/ppermute | solution.py:374
  40.8 5.1 %collective-permute-start.8 = (bf16[64,3712]{1,0:T(8,128)(2,1)S(1)}, bf16[64,3712]{1,0:T(8,128)(2,1)S(1)}, u32[]{:S(2)}, u32[]{:S(2)}) collective-permute-start(bf16[64,3712]{1,0:T(8,128)(2,1)S(1)} %collective-permute-done.7.mine_2), channel_id=1, source_target_pairs={{0,1},{1,0},{2,3},{3,2},{4,5},{5,4},{6,7},{7,6},{8,9},{9,8},{10,11... | collective-permute-start | bytes 1425416 | tf_op jit(solution)/shard_map/ppermute | solution.py:374
  46.0 17.7 %copy-start.9 = (f32[3584]{0:T(1024)S(1)}, f32[3584]{0:T(1024)}, u32[]{:S(2)}) copy-start(f32[3584]{0:T(1024)} %param.15) | copy-start | bytes 43012
  47.4 17.6 %collective-permute-start.10 = (bf16[32,4096]{1,0:T(8,128)(2,1)S(1)}, bf16[32,4096]{1,0:T(8,128)(2,1)S(1)}, u32[]{:S(2)}, u32[]{:S(2)}) collective-permute-start(bf16[32,4096]{1,0:T(8,128)(2,1)S(1)} %get-tuple-element.40), channel_id=1, source_target_pairs={{0,16},{1,17},{2,18},{3,19},{4,20},{5,21},{6,22},{7,23},{8,24},{9,... | collective-permute-start | bytes 786440 | tf_op jit(solution)/shard_map/ppermute | solution.py:374
  48.8 16.2 %collective-permute-start.11 = (bf16[32,4096]{1,0:T(8,128)(2,1)S(1)}, bf16[32,4096]{1,0:T(8,128)(2,1)S(1)}, u32[]{:S(2)}, u32[]{:S(2)}) collective-permute-start(bf16[32,4096]{1,0:T(8,128)(2,1)S(1)} %get-tuple-element.41), channel_id=1, source_target_pairs={{0,18},{1,19},{2,16},{3,17},{4,22},{5,23},{6,20},{7,21},{8,26},{9,... | collective-permute-start | bytes 786440 | tf_op jit(solution)/shard_map/ppermute | solution.py:374
  50.2 14.8 %collective-permute-start.9 = (bf16[32,4096]{1,0:T(8,128)(2,1)S(1)}, bf16[32,4096]{1,0:T(8,128)(2,1)S(1)}, u32[]{:S(2)}, u32[]{:S(2)}) collective-permute-start(bf16[32,4096]{1,0:T(8,128)(2,1)S(1)} %get-tuple-element.39), channel_id=1, source_target_pairs={{0,2},{1,3},{2,0},{3,1},{4,6},{5,7},{6,4},{7,5},{8,10},{9,11},{10,... | collective-permute-start | bytes 786440 | tf_op jit(solution)/shard_map/ppermute | solution.py:374
  51.0 4.9 %collective-permute-start.12 = (f32[8,256]{1,0:T(8,128)S(1)}, f32[8,256]{1,0:T(8,128)S(1)}, u32[]{:S(2)}, u32[]{:S(2)}) collective-permute-start(f32[8,256]{1,0:T(8,128)S(1)} %get-tuple-element.42.early), channel_id=1, source_target_pairs={{0,12},{1,13},{2,14},{3,15},{4,0},{5,1},{6,2},{7,3},{8,4},{9,5},{1... | collective-permute-start | bytes 24584 | tf_op jit(solution)/shard_map/ppermute | solution.py:374
  54.5 5.4 %collective-permute-start.14 = (f32[8,256]{1,0:T(8,128)S(1)}, f32[8,256]{1,0:T(8,128)S(1)}, u32[]{:S(2)}, u32[]{:S(2)}) collective-permute-start(f32[8,256]{1,0:T(8,128)S(1)} %get-tuple-element.42.early), channel_id=1, source_target_pairs={{0,4},{1,5},{2,6},{3,7},{4,8},{5,9},{6,10},{7,11},{8,12},{9,13},{1... | collective-permute-start | bytes 24584 | tf_op jit(solution)/shard_map/ppermute | solution.py:374
  55.9 4.5 %collective-permute-start.13 = (f32[8,128]{1,0:T(8,128)S(1)}, f32[8,128]{1,0:T(8,128)S(1)}, u32[]{:S(2)}, u32[]{:S(2)}) collective-permute-start(f32[8,128]{1,0:T(8,128)S(1)} %get-tuple-element.43), channel_id=1, source_target_pairs={{0,8},{1,9},{2,10},{3,11},{4,12},{5,13},{6,14},{7,15},{8,0},{9,1},... | collective-permute-start | bytes 12296 | tf_op jit(solution)/shard_map/ppermute | solution.py:374
  60.5 3.2 %collective-permute-start.15 = (f32[1,64]{1,0:T(1,128)S(1)}, f32[1,64]{1,0:T(1,128)S(1)}, u32[]{:S(2)}, u32[]{:S(2)}) collective-permute-start(f32[1,64]{1,0:T(1,128)S(1)} %get-tuple-element.44), channel_id=1, source_target_pairs={{0,0},{1,16},{2,2},{3,18},{4,4},{5,20},{6,6},{7,22},{8,8},{9,24},{... | collective-permute-start | bytes 776 | tf_op jit(solution)/shard_map/ppermute | solution.py:374
  61.1 3.8 %collective-permute-start.16 = (f32[1,64]{1,0:T(1,128)S(1)}, f32[1,64]{1,0:T(1,128)S(1)}, u32[]{:S(2)}, u32[]{:S(2)}) collective-permute-start(f32[1,64]{1,0:T(1,128)S(1)} %get-tuple-element.45), channel_id=1, source_target_pairs={{0,16},{1,0},{2,18},{3,2},{4,20},{5,4},{6,22},{7,6},{8,24},{9,8},{... | collective-permute-start | bytes 776 | tf_op jit(solution)/shard_map/ppermute | solution.py:374

commit v5 on v4

--- a/solution.py
+++ b/solution.py
@@ -125,38 +125,63 @@
     return (lane == row + per * y).astype(BF)
 
 
-def weights_kernel(enc, dec, bias, out, enc_half, sem):
+def weights_kernel(enc, dec, bias, out, enc_half, bias_here, sem):
     _, y, _, s = place_here()
     lanes = enc.shape[1]
     half = enc_half.shape[0]
     per = out.shape[0]
-    cols = pl.ds(pl.multiple_of(s * half, 128), half)
-    get_enc = pltpu.make_async_copy(enc.at[cols, :], enc_half, sem.at[0])
-    get_dec = pltpu.make_async_copy(
-        dec.at[pl.ds(pl.multiple_of(y * per, 16), per), cols],
-        out.at[:, pl.ds(half + 128, half)],
-        sem.at[1],
-    )
-    get_enc.start()
-    get_dec.start()
+    chunks = 4
+    n = half // chunks
+    side = s * half
+    copies = [pltpu.make_async_copy(bias, bias_here, sem.at[2 * chunks])]
+    for i in range(chunks):
+        copies.append(
+            pltpu.make_async_copy(
+                enc.at[pl.ds(pl.multiple_of(side + i * n, 64), n), :],
+                enc_half.at[pl.ds(i * n, n), :],
+                sem.at[i],
+            )
+        )
+    m = per // chunks
+    for i in range(chunks):
+        copies.append(
+            pltpu.make_async_copy(
+                dec.at[
+                    pl.ds(pl.multiple_of(y * per + i * m, 16), m),
+                    pl.ds(pl.multiple_of(side, 128), half),
+                ],
+                out.at[pl.ds(i * m, m), pl.ds(half + 128, half)],
+                sem.at[chunks + i],
+            )
+        )
+    for copy in copies:
+        copy.start()
     pick = pick_latents(per, lanes, y)
-    b = bias[...]
+    copies[0].wait()
+    b = bias_here[...]
     hi = b.astype(BF).astype(F32)
     mid = (b - hi).astype(BF).astype(F32)
     low = b - hi - mid
     term = lax.broadcasted_iota(jnp.int32, (lanes, lanes), 0)
     terms = jnp.where(term == 0, hi, jnp.where(term == 1, mid, jnp.where(term == 2, low, 0.0)))
     out[:, half : half + 128] = nt(pick, terms.astype(BF)).astype(BF)
-    get_enc.wait()
+    for copy in copies[1 : chunks + 1]:
+        copy.wait()
     out[:, :half] = nt(pick, enc_half[...]).astype(BF)
-    get_dec.wait()
-
-
-def totals_kernel(per, early, one, two, three, row, rest):
+    for copy in copies[chunks + 1 :]:
+        copy.wait()
+
+
+def totals_kernel(early, two, three, row, rest):
     _, y, _, s = place_here()
-    total = early[:2, :per] + one[:2, per : 2 * per] + two[:2, :per] + three[:2, 3 * per :]
-    row[...] = jnp.where(y == s, total[:1], total[1:])
-    rest[...] = jnp.where(y == s, total[1:], total[:1])
+    per = row.shape[1]
+    total = early[:2] + two[:2] + pltpu.roll(three[...], per, 1)[:2]
+    row[...] = jnp.where(y == s, total[:1, :per], total[1:, :per])
+    rest[...] = jnp.where(y == s, total[1:, :per], total[:1, :per])
+
+
+def after_kernel(values, _, out):
+    out[...] = values[...]
 
 
 def target_block(lane, m, x, z, ring):
@@ -210,13 +235,29 @@
     return jnp.concatenate([near, far, jnp.zeros((6, scores.shape[1]), F32)], axis=0)
 
 
+def blocks(rows, mask, sides, half):
+    bias = jnp.concatenate([p[:, half : half + 128] for p in sides[0]], axis=0)
+    preact = nt(jnp.ones((8, 128), BF), bias)[:1]
+    for j, parts in enumerate(sides):
+        weights = jnp.concatenate([p[:, :half] for p in parts], axis=0)
+        preact = preact + nt(rows[:, j * half : (j + 1) * half], weights)
+    code = (preact * mask.astype(F32)).astype(BF)
+    proj = jnp.zeros(code.shape, F32)
+    recon = []
+    for j, parts in enumerate(sides):
+        weights = jnp.concatenate([p[:, half + 128 :] for p in parts], axis=0)
+        proj = proj + nt(rows[:, (2 + j) * half : (3 + j) * half], weights)
+        recon.append(jnp.dot(code, weights, preferred_element_type=F32))
+    return code, code.astype(F32) * proj, recon
+
+
 def early_kernel(
-    own, own_mask, from_x, from_y, from_d, enc, dec, mine_0, mine_1, other_1, mine_3, other_3,
+    from_d, from_x, from_y, own, own_mask, enc, dec, mine_0, mine_1, other_1,
     rows, mask, recon, codes, scores, sums, enc_half, other_0, sem,
 ):
     _, y, _, s = place_here()
     tok = own.shape[0]
-    per, lanes = mine_0.shape[0], enc.shape[1]
+    per, lanes = other_0.shape[0], enc.shape[1]
     half = enc_half.shape[0]
     width = 2 * half
     far = pl.ds(pl.multiple_of((1 - s) * half, 128), half)
@@ -235,78 +276,51 @@
             side = s if j % 2 == 0 else 1 - s
             cols = pl.ds(pl.multiple_of(width * (j // 2) + side * half, 128), half)
             rows[at, j * half : (j + 1) * half] = src[:, cols]
+    other_0[:, half : half + 128] = jnp.zeros((per, 128), BF)
     get_enc.wait()
     other_0[:, :half] = nt(pick_latents(per, lanes, y), enc_half[...]).astype(BF)
     get_dec.wait()
-    blank = jnp.zeros((per, half), BF)
-    sides = ((mine_0, mine_1, mine_3), (other_0, other_1, other_3))
-
-    def stack(parts, at, n):
-        return jnp.concatenate(
-            [parts[0][:, at : at + n], parts[1][:, at : at + n], blank[:, :n], parts[2][:, at : at + n]],
-            axis=0,
-        )
-
-    preact = nt(jnp.ones((8, 128), BF), stack(sides[0], half, 128))[:1]
-    for j, parts in enumerate(sides):
-        preact = preact + nt(rows[:, j * half : (j + 1) * half], stack(parts, 0, half))
-    code = (preact * mask[...].astype(F32)).astype(BF)
+    code, score, total = blocks(
+        rows, mask[:, : 2 * per], ((mine_0, mine_1), (other_0, other_1)), half
+    )
     codes[...] = code
-    proj = jnp.zeros(code.shape, F32)
-    for j, parts in enumerate(sides):
-        weights = stack(parts, half + 128, half)
-        proj = proj + nt(rows[:, (2 + j) * half : (3 + j) * half], weights)
-        recon[:, j * half : (j + 1) * half] = jnp.dot(code, weights, preferred_element_type=F32)
-    score = code.astype(F32) * proj
     scores[...] = score
+    for j in range(2):
+        recon[:, j * half : (j + 1) * half] = total[j]
     sums[...] = group_sums(score)
 
 
 def late_kernel(
-    rows, mask, recon, codes, scores, mine_2, other_2,
-    own_recon, own_codes, own_scores, to_x, to_y, to_d, sums,
+    rows, mask, recon, codes, scores, mine_2, other_2, mine_3, other_3, sums, one,
+    own_recon, own_codes, own_scores, to_x, to_y, to_d, sums_23, sums_01,
 ):
     _, _, _, s = place_here()
     per = mine_2.shape[0]
     tok = own_codes.shape[0]
     width = own_recon.shape[1]
     half = width // 2
-    names = codes.shape[1]
-    blank = jnp.zeros((per, half), BF)
-    sides = (mine_2, other_2)
-
-    def stack(part, at, n):
-        return jnp.concatenate([part[:, at : at + n], blank[:, :n]], axis=0)
-
-    preact = nt(jnp.ones((8, 128), BF), stack(mine_2, half, 128))[:1]
-    for j, part in enumerate(sides):
-        preact = preact + nt(rows[:, j * half : (j + 1) * half], stack(part, 0, half))
-    code = (preact * mask[:, 2 * per :].astype(F32)).astype(BF)
-    proj = jnp.zeros(code.shape, F32)
-    outs = (own_recon, to_x, to_y, to_d)
-    for j, part in enumerate(sides):
-        weights = stack(part, half + 128, half)
-        proj = proj + nt(rows[:, (2 + j) * half : (3 + j) * half], weights)
-        total = recon[:, j * half : (j + 1) * half] + jnp.dot(
-            code, weights, preferred_element_type=F32
-        )
+    code, score, total = blocks(
+        rows, mask[:, 2 * per :], ((mine_2, mine_3), (other_2, other_3)), half
+    )
+    for j in range(2):
         cols = pl.ds(pl.multiple_of((s if j == 0 else 1 - s) * half, 128), half)
-        for i, out in enumerate(outs):
-            out[:, cols] = total[i * tok : (i + 1) * tok].astype(out.dtype)
-    score = code.astype(F32) * proj
-    sums[...] = group_sums(score)
-    all_codes = jnp.concatenate([codes[:, : 2 * per], code + codes[:, 2 * per :]], axis=1)
-    all_scores = jnp.concatenate([scores[:, : 2 * per], score + scores[:, 2 * per :]], axis=1)
-    own_codes[...] = all_codes[:tok]
-    own_scores[...] = all_scores[:tok]
+        part = recon[:, j * half : (j + 1) * half] + total[j]
+        for i, out in enumerate((own_recon, to_x, to_y, to_d)):
+            out[:, cols] = part[i * tok : (i + 1) * tok].astype(out.dtype)
+    sums_23[...] = group_sums(score)
+    sums_01[...] = sums[...] + pltpu.roll(one[...], per, 1)
+    own_codes[...] = jnp.concatenate([codes[:tok], code[:tok]], axis=1)
+    own_scores[...] = jnp.concatenate([scores[:tok], score[:tok]], axis=1)
     for i, out in enumerate((to_x, to_y, to_d)):
         at = slice((i + 1) * tok, (i + 2) * tok)
-        out[:, width : width + names] = all_codes[at]
-        out[:, width + names :] = all_scores[at].astype(BF)
+        for j, (first, second) in enumerate(((codes, code), (scores, score))):
+            base = width + 4 * per * j
+            out[:, base : base + 2 * per] = first[at].astype(BF)
+            out[:, base + 2 * per : base + 4 * per] = second[at].astype(BF)
 
 
 def final_kernel(
-    ring, factor, own_recon, own_codes, own_scores, from_x, from_y, from_d, own, dec_bias, ids, row, rest,
+    ring, factor, from_d, from_x, from_y, own_recon, own_codes, own_scores, own, dec_bias, ids, row, rest,
     out_codes, out_scores, out_error, out_totals,
 ):
     x, y, z, _ = place_here()
@@ -392,12 +406,17 @@
         weights_kernel,
         [((per, 2 * half + 128), BF)],
         encoder, decoder, enc_bias.reshape(1, lanes),
-        far=(0, 1),
-        scratch=[pltpu.VMEM((half, lanes), BF), pltpu.SemaphoreType.DMA((2,))],
+        far=(0, 1, 2),
+        scratch=[
+            pltpu.VMEM((half, lanes), BF),
+            pltpu.VMEM((1, lanes), F32),
+            pltpu.SemaphoreType.DMA((9,)),
+        ],
+        vmem=56,
     )
     part_1 = by_z(own, 1)
+    part_2 = by_z(part_1, 1)
     part_3 = by_z(own, -1)
-    part_2 = by_z(part_1, 1)
 
     to_x, to_y, to_d, own_mask = call(
         functools.partial(tokens_kernel, ring),
@@ -406,19 +425,22 @@
         far=(0, 1, 4),
         scratch=[pltpu.SemaphoreType.DMA((6,))],
     )
-    own_rows = to_x
+    own_rows = to_d
+    from_d = by_xy(to_d)
+    from_x = by_x(to_x)
+    from_y = by_y(to_y)
     rows, mask, recon, codes, scores, sums = call(
         early_kernel,
         [
             ((4 * tok, 2 * width), BF),
             ((4 * tok, names), BF),
             ((4 * tok, width), F32),
-            ((4 * tok, names), BF),
-            ((4 * tok, names), F32),
-            ((8, names), F32),
+            ((4 * tok, 2 * per), BF),
+            ((4 * tok, 2 * per), F32),
+            ((8, 2 * per), F32),
         ],
-        own_rows, own_mask, by_x(to_x), by_y(to_y), by_xy(to_d), encoder, decoder,
-        own, part_1, by_core(part_1), part_3, by_core(part_3),
+        from_d, from_x, from_y, own_rows, own_mask, encoder, decoder,
+        own, part_1, by_core(part_1),
         far=(5, 6),
         scratch=[
             pltpu.VMEM((half, lanes), BF),
@@ -426,21 +448,23 @@
             pltpu.SemaphoreType.DMA((2,)),
         ],
     )
-    own_recon, own_codes, own_scores, to_x, to_y, to_d, sums_2 = call(
+    (part_2,) = call(after_kernel, [(part_2.shape, BF)], part_2, codes, far=(1,))
+    own_recon, own_codes, own_scores, to_x, to_y, to_d, sums_23, sums_01 = call(
         late_kernel,
         [((tok, width), F32), ((tok, names), BF), ((tok, names), F32)]
         + [((tok, width + 2 * names), BF)] * 3
-        + [((8, 2 * per), F32)],
-        rows, mask, recon, codes, scores, part_2, by_core(part_2),
+        + [((8, 2 * per), F32)] * 2,
+        rows, mask, recon, codes, scores, part_2, by_core(part_2), part_3, by_core(part_3),
+        sums, by_z(sums, -1),
     )
     from_d = by_xy(to_d)
     from_x = by_x(to_x)
     from_y = by_y(to_y)
 
     row, rest = call(
-        functools.partial(totals_kernel, per),
+        totals_kernel,
         [((1, per), F32)] * 2,
-        sums, by_z(sums, -1), by_z(sums_2, -2), by_z(sums, 1),
+        sums_01, by_z(sums_23, -2), by_z(sums_23, 1),
     )
     factor = (tok * lat_count * 2 * active / lat_count) ** (-0.5)
     latent_codes, attribution, recon_error, latent_totals = call(
@@ -451,7 +475,7 @@
             ((tok, width), BF),
             ((1, per), F32),
         ],
-        own_recon, own_codes, own_scores, from_x, from_y, from_d,
+        from_d, from_x, from_y, own_recon, own_codes, own_scores,
         own_rows, dec_bias.reshape(1, width), block_ids.T,
         permute(row, lambda gg, ll, ss: (ss, ll, gg)),
         permute(rest, lambda gg, ll, ss: (1 - ss, ll, gg)),

time: 67.3 us -> 63.8 us (0.948)
  waiting for transfers between devices: 32.1 us -> 27.6 us
  starting transfers between devices: 22.1 us -> 23.2 us
  local copies, waits for them, and re-layouts: 3.88 us -> 2.94 us
    ppermute x17, waiting for transfers between devices: 32.1 us -> 27.6 us  [permute(): return lax.ppermute(values, AXES, pairs)]
    ppermute x17, starting transfers between devices: 22.1 us -> 23.2 us  [permute(): return lax.ppermute(values, AXES, pairs)]
    unnamed x20 -> x18, local copies, waits for them, and re-layouts: 3.87 us -> 2.93 us
    pallas_call x6 -> x7, Pallas kernels: 7.47 us -> 8.13 us  [call(): pl.pallas_call(kernel, in_specs=[pl.BlockSpec(memory_space=pl.ANY if i in...]
  transfers between devices with their start and end apart: 17 -> 17, of which waited for: 8 -> 9; matrix products, arithmetic and copies ran while one was open for 0% -> 0% of each run, Pallas kernels for 6% -> 5%
where the time goes in v5:
time: 63.8 us; the launch traced here: 62.7 us
  waiting for transfers between devices  27.6 us (43%)
  starting transfers between devices  23.2 us (36%)
  Pallas kernels  8.13 us (13%)
  local copies, waits for them, and re-layouts  2.94 us (5%)
  between operations  0.78 us (1%)
    ppermute x17, waiting for transfers between devices, permute(): return lax.ppermute(values, AXES, pairs)  27.6 us
    ppermute x17, starting transfers between devices, permute(): return lax.ppermute(values, AXES, pairs)  23.2 us
    pallas_call x7, Pallas kernels, call(): pl.pallas_call(kernel, in_specs=[pl.BlockSpec(memory_space=pl.ANY if i in...  8.13 us
    unnamed x18, local copies, waits for them, and re-layouts  2.93 us
  transfers between devices with their start and end apart: 17, of which 9 were waited for; matrix products, arithmetic and copies ran while one was open for 0% of the time, Pallas kernels for 5%

profile of v5, /device:TPU:0, one launch (start us, length us, event | category | flops | bytes accessed | tf_op | source)
XLA Modules:
  0.0 62.7 jit_solution(11442979676272727353)
XLA Ops:
  0.7 2.4 %shard_map.111._.mine_0 = bf16[64,3712]{1,0:T(8,128)(2,1)} custom-call(bf16[3584,128]{1,0:T(8,128)(2,1)} %enc.3, bf16[128,3584]{1,0:T(8,128)(2,1)} %dec.3, f32[1,128]{1,0:T(1,128)} %bitcast.5), custom_call_target="tpu_custom_call" | custom-call | tf_op jit(solution)/shard_map/pallas_call | solution.py:110
  3.1 3.1 %collective-permute-start.3 = (bf16[64,3712]{1,0:T(8,128)(2,1)}, bf16[64,3712]{1,0:T(8,128)(2,1)S(1)}, u32[]{:S(2)}, u32[]{:S(2)}) collective-permute-start(bf16[64,3712]{1,0:T(8,128)(2,1)} %shard_map.111._.mine_0), channel_id=1, source_target_pairs={{0,4},{1,5},{2,6},{3,7},{4,8},{5,9},{6,10},{7,11},{8,12},{9,13},{1... | collective-permute-start | bytes 1425416 | tf_op jit(solution)/shard_map/ppermute | solution.py:388
  6.2 1.0 %copy-done = bf16[64,3712]{1,0:T(8,128)(2,1)S(1)} copy-done((bf16[64,3712]{1,0:T(8,128)(2,1)S(1)}, bf16[64,3712]{1,0:T(8,128)(2,1)}, u32[]{:S(2)}) %copy-start) | copy-done | bytes 475160
  7.2 0.8 %copy-done.6 = s32[32,4,128]{2,1,0:T(4,128)S(1)} copy-done((s32[32,4,128]{2,1,0:T(4,128)S(1)}, s32[32,4,128]{2,1,0:T(4,128)}, u32[]{:S(2)}) %copy-start.6) | copy-done | bytes 65560
  8.1 0.7 %shard_map.112 = (bf16[32,7424]{1,0:T(8,128)(2,1)S(1)}, bf16[32,7424]{1,0:T(8,128)(2,1)S(1)}, bf16[32,7424]{1,0:T(8,128)(2,1)S(1)}, bf16[32,256]{1,0:T(8,128)(2,1)S(1)}) custom-call(bf16[32,3584]{1,0:T(8,128)(2,1)S(1)} %copy-done.4, bf16[32,3584]{1,0:T(8,128)(2,1)S(1)} %copy-done.5, s32[4,32]{1,0:T(4,128)S(1)} %bitcast.3, s32[32,4,128]{2,1,0:T(4,128)S(1)} %copy-done.6, ...), custom_call_target="tpu_custom_call" | custom-call | tf_op jit(solution)/shard_map/pallas_call | solution.py:110
  8.7 2.5 %collective-permute-start = (bf16[32,7424]{1,0:T(8,128)(2,1)S(1)}, bf16[32,7424]{1,0:T(8,128)(2,1)S(1)}, u32[]{:S(2)}, u32[]{:S(2)}) collective-permute-start(bf16[32,7424]{1,0:T(8,128)(2,1)S(1)} %get-tuple-element.28.own), channel_id=1, source_target_pairs={{0,18},{1,19},{2,16},{3,17},{4,22},{5,23},{6,20},{7,21},{8,26},{9,... | collective-permute-start | bytes 1425416 | tf_op jit(solution)/shard_map/ppermute | solution.py:388
  11.2 2.2 %collective-permute-start.7 = (bf16[64,3712]{1,0:T(8,128)(2,1)S(1)}, bf16[64,3712]{1,0:T(8,128)(2,1)S(1)}, u32[]{:S(2)}, u32[]{:S(2)}) collective-permute-start(bf16[64,3712]{1,0:T(8,128)(2,1)S(1)} %copy-done), channel_id=1, source_target_pairs={{0,12},{1,13},{2,14},{3,15},{4,0},{5,1},{6,2},{7,3},{8,4},{9,5},{1... | collective-permute-start | bytes 1425416 | tf_op jit(solution)/shard_map/ppermute | solution.py:388
  13.5 0.5 collective-permute-start.1
  14.0 0.3 collective-permute-start.2
  14.4 5.8 %collective-permute-done.3.mine_1 = bf16[64,3712]{1,0:T(8,128)(2,1)S(1)} collective-permute-done((bf16[64,3712]{1,0:T(8,128)(2,1)}, bf16[64,3712]{1,0:T(8,128)(2,1)S(1)}, u32[]{:S(2)}, u32[]{:S(2)}) %collective-permute-start.3) | collective-permute-done | bytes 475168 | tf_op jit(solution)/shard_map/ppermute | solution.py:388
  20.1 3.4 %collective-permute-done.from_d = bf16[32,7424]{1,0:T(8,128)(2,1)S(1)} collective-permute-done((bf16[32,7424]{1,0:T(8,128)(2,1)S(1)}, bf16[32,7424]{1,0:T(8,128)(2,1)S(1)}, u32[]{:S(2)}, u32[]{:S(2)}) %collective-permute-start) | collective-permute-done | bytes 475168 | tf_op jit(solution)/shard_map/ppermute | solution.py:388
  23.5 1.6 %collective-permute-start.5 = (bf16[64,3712]{1,0:T(8,128)(2,1)S(1)}, bf16[64,3712]{1,0:T(8,128)(2,1)S(1)}, u32[]{:S(2)}, u32[]{:S(2)}) collective-permute-start(bf16[64,3712]{1,0:T(8,128)(2,1)S(1)} %collective-permute-done.3.mine_1), channel_id=1, source_target_pairs={{0,4},{1,5},{2,6},{3,7},{4,8},{5,9},{6,10},{7,11},{8,12},{9,13},{1... | collective-permute-start | bytes 1425416 | tf_op jit(solution)/shard_map/ppermute | solution.py:388
  25.1 4.3 %collective-permute-done.7.mine_3 = bf16[64,3712]{1,0:T(8,128)(2,1)S(1)} collective-permute-done((bf16[64,3712]{1,0:T(8,128)(2,1)S(1)}, bf16[64,3712]{1,0:T(8,128)(2,1)S(1)}, u32[]{:S(2)}, u32[]{:S(2)}) %collective-permute-start.7) | collective-permute-done | bytes 475168 | tf_op jit(solution)/shard_map/ppermute | solution.py:388
  29.5 2.9 %collective-permute-done.1.from_x = bf16[32,7424]{1,0:T(8,128)(2,1)S(1)} collective-permute-done((bf16[32,7424]{1,0:T(8,128)(2,1)S(1)}, bf16[32,7424]{1,0:T(8,128)(2,1)S(1)}, u32[]{:S(2)}, u32[]{:S(2)}) %collective-permute-start.1) | collective-permute-done | bytes 475168 | tf_op jit(solution)/shard_map/ppermute | solution.py:388
  32.3 1.0 %copy-done.1 = bf16[64,3712]{1,0:T(8,128)(2,1)S(1)} copy-done((bf16[64,3712]{1,0:T(8,128)(2,1)S(1)}, bf16[64,3712]{1,0:T(8,128)(2,1)}, u32[]{:S(2)}) %copy-start.1) | copy-done | bytes 475160
  33.4 2.2 %shard_map.113 = (bf16[128,7168]{1,0:T(8,128)(2,1)S(1)}, bf16[128,256]{1,0:T(8,128)(2,1)S(1)}, f32[128,3584]{1,0:T(8,128)S(1)}, bf16[128,128]{1,0:T(8,128)(2,1)S...) custom-call(bf16[32,7424]{1,0:T(8,128)(2,1)S(1)} %collective-permute-done.from_d, ...), custom_call_target="tpu_custom_call" | custom-call | tf_op jit(solution)/shard_map/pallas_call | solution.py:110
  35.6 6.2 %collective-permute-done.5.values = bf16[64,3712]{1,0:T(8,128)(2,1)S(1)} collective-permute-done((bf16[64,3712]{1,0:T(8,128)(2,1)S(1)}, bf16[64,3712]{1,0:T(8,128)(2,1)S(1)}, u32[]{:S(2)}, u32[]{:S(2)}) %collective-permute-start.5) | collective-permute-done | bytes 475168 | tf_op jit(solution)/shard_map/ppermute | solution.py:388
  41.9 1.8 %collective-permute-start.9 = (f32[8,128]{1,0:T(8,128)S(1)}, f32[8,128]{1,0:T(8,128)S(1)}, u32[]{:S(2)}, u32[]{:S(2)}) collective-permute-start(f32[8,128]{1,0:T(8,128)S(1)} %get-tuple-element.37.sums), channel_id=1, source_target_pairs={{0,12},{1,13},{2,14},{3,15},{4,0},{5,1},{6,2},{7,3},{8,4},{9,5},{1... | collective-permute-start | bytes 12296 | tf_op jit(solution)/shard_map/ppermute | solution.py:388
  43.7 1.9 %collective-permute-done.9.one = f32[8,128]{1,0:T(8,128)S(1)} collective-permute-done((f32[8,128]{1,0:T(8,128)S(1)}, f32[8,128]{1,0:T(8,128)S(1)}, u32[]{:S(2)}, u32[]{:S(2)}) %collective-permute-start.9) | collective-permute-done | bytes 4128 | tf_op jit(solution)/shard_map/ppermute | solution.py:388
  45.5 1.5 %shard_map.115 = (f32[32,3584]{1,0:T(8,128)S(1)}, bf16[32,256]{1,0:T(8,128)(2,1)S(1)}, f32[32,256]{1,0:T(8,128)S(1)}, bf16[32,4096]{1,0:T(8,128)(2,1)S(1)}, bf16...) custom-call(bf16[128,7168]{1,0:T(8,128)(2,1)S(1)} %get-tuple-element.32.ro, ...), custom_call_target="tpu_custom_call" | custom-call | tf_op jit(solution)/shard_map/pallas_call | solution.py:110
  47.0 2.5 %collective-permute-start.10 = (bf16[32,4096]{1,0:T(8,128)(2,1)S(1)}, bf16[32,4096]{1,0:T(8,128)(2,1)S(1)}, u32[]{:S(2)}, u32[]{:S(2)}) collective-permute-start(bf16[32,4096]{1,0:T(8,128)(2,1)S(1)} %get-tuple-element.38), channel_id=1, source_target_pairs={{0,18},{1,19},{2,16},{3,17},{4,22},{5,23},{6,20},{7,21},{8,26},{9,... | collective-permute-start | bytes 786440 | tf_op jit(solution)/shard_map/ppermute | solution.py:388
  49.5 0.5 collective-permute-start.11
  50.1 0.5 collective-permute-start.12
  50.6 0.6 collective-permute-start.13
  51.2 3.5 %collective-permute-start.14 = (f32[8,128]{1,0:T(8,128)S(1)}, f32[8,128]{1,0:T(8,128)S(1)}, u32[]{:S(2)}, u32[]{:S(2)}) collective-permute-start(f32[8,128]{1,0:T(8,128)S(1)} %get-tuple-element.45), channel_id=1, source_target_pairs={{0,4},{1,5},{2,6},{3,7},{4,8},{5,9},{6,10},{7,11},{8,12},{9,13},{1... | collective-permute-start | bytes 12296 | tf_op jit(solution)/shard_map/ppermute | solution.py:388
  54.7 0.4 collective-permute-done.13.two
  55.1 1.5 %collective-permute-done.14.three = f32[8,128]{1,0:T(8,128)S(1)} collective-permute-done((f32[8,128]{1,0:T(8,128)S(1)}, f32[8,128]{1,0:T(8,128)S(1)}, u32[]{:S(2)}, u32[]{:S(2)}) %collective-permute-start.14) | collective-permute-done | bytes 4128 | tf_op jit(solution)/shard_map/ppermute | solution.py:388
  56.6 0.1 shard_map.116
  56.7 0.7 %collective-permute-start.15 = (f32[1,64]{1,0:T(1,128)S(1)}, f32[1,64]{1,0:T(1,128)S(1)}, u32[]{:S(2)}, u32[]{:S(2)}) collective-permute-start(f32[1,64]{1,0:T(1,128)S(1)} %get-tuple-element.46), channel_id=1, source_target_pairs={{0,0},{1,16},{2,2},{3,18},{4,4},{5,20},{6,6},{7,22},{8,8},{9,24},{... | collective-permute-start | bytes 776 | tf_op jit(solution)/shard_map/ppermute | solution.py:388
  57.3 2.8 %collective-permute-start.16 = (f32[1,64]{1,0:T(1,128)S(1)}, f32[1,64]{1,0:T(1,128)S(1)}, u32[]{:S(2)}, u32[]{:S(2)}) collective-permute-start(f32[1,64]{1,0:T(1,128)S(1)} %get-tuple-element.47), channel_id=1, source_target_pairs={{0,16},{1,0},{2,18},{3,2},{4,20},{5,4},{6,22},{7,6},{8,24},{9,8},{... | collective-permute-start | bytes 776 | tf_op jit(solution)/shard_map/ppermute | solution.py:388
  60.1 1.3 %collective-permute-done.16.rest = f32[1,64]{1,0:T(1,128)S(1)} collective-permute-done((f32[1,64]{1,0:T(1,128)S(1)}, f32[1,64]{1,0:T(1,128)S(1)}, u32[]{:S(2)}, u32[]{:S(2)}) %collective-permute-start.16) | collective-permute-done | bytes 288 | tf_op jit(solution)/shard_map/ppermute | solution.py:388
  61.4 1.3 %shard_map.117 = (bf16[32,4,128]{2,1,0:T(4,128)(2,1)}, f32[32,4,128]{2,1,0:T(4,128)}, bf16[32,3584]{1,0:T(8,128)(2,1)}, f32[1,64]{1,0:T(1,128)}) custom-call(bf16[32,4096]{1,0:T(8,128)(2,1)S(1)} %collective-permute-done.10.from_d, bf16[32,4096]{1,0:T(8,128)(2,1)S(1)} %collective-permute-done.11.from_x, bf16[32,4096]{1,0:T(8,128)(2,1)S(1)} %collective-permute-done.12.from_y, ...), custom_call_target="tpu_custom_call" | custom-call | tf_op jit(solution)/shard_map/pallas_call | solution.py:110
  (28 shorter events, 0.2 us)
Async XLA Ops:
  0.6 31.7 %copy-start.2 = (bf16[3584,128]{1,0:T(8,128)(2,1)S(1)}, bf16[3584,128]{1,0:T(8,128)(2,1)}, u32[]{:S(2)}) copy-start(bf16[3584,128]{1,0:T(8,128)(2,1)} %enc.3) | copy-start | bytes 2752516
  0.6 31.7 %copy-start.3 = (bf16[128,3584]{1,0:T(8,128)(2,1)S(1)}, bf16[128,3584]{1,0:T(8,128)(2,1)}, u32[]{:S(2)}) copy-start(bf16[128,3584]{1,0:T(8,128)(2,1)} %dec.3) | copy-start | bytes 2752516
  0.7 5.5 %copy-start.7 = (s32[32,4]{0,1:T(4,128)S(1)}, s32[32,4]{0,1:T(4,128)}, u32[]{:S(2)}) copy-start(s32[32,4]{0,1:T(4,128)} %param.10) | copy-start | bytes 1540
  0.7 5.5 %copy-start.4 = (bf16[32,3584]{1,0:T(8,128)(2,1)S(1)}, bf16[32,3584]{1,0:T(8,128)(2,1)}, u32[]{:S(2)}) copy-start(bf16[32,3584]{1,0:T(8,128)(2,1)} %res.1) | copy-start | bytes 688132
  0.7 5.5 %copy-start.5 = (bf16[32,3584]{1,0:T(8,128)(2,1)S(1)}, bf16[32,3584]{1,0:T(8,128)(2,1)}, u32[]{:S(2)}) copy-start(bf16[32,3584]{1,0:T(8,128)(2,1)} %grad.1) | copy-start | bytes 688132
  3.1 17.1 %collective-permute-start.3 = (bf16[64,3712]{1,0:T(8,128)(2,1)}, bf16[64,3712]{1,0:T(8,128)(2,1)S(1)}, u32[]{:S(2)}, u32[]{:S(2)}) collective-permute-start(bf16[64,3712]{1,0:T(8,128)(2,1)} %shard_map.111._.mine_0), channel_id=1, source_target_pairs={{0,4},{1,5},{2,6},{3,7},{4,8},{5,9},{6,10},{7,11},{8,12},{9,13},{1... | collective-permute-start | bytes 1425416 | tf_op jit(solution)/shard_map/ppermute | solution.py:388
  6.2 1.1 %copy-start = (bf16[64,3712]{1,0:T(8,128)(2,1)S(1)}, bf16[64,3712]{1,0:T(8,128)(2,1)}, u32[]{:S(2)}) copy-start(bf16[64,3712]{1,0:T(8,128)(2,1)} %shard_map.111._.mine_0) | copy-start | bytes 1425412
  7.2 0.8 %copy-start.6 = (s32[32,4,128]{2,1,0:T(4,128)S(1)}, s32[32,4,128]{2,1,0:T(4,128)}, u32[]{:S(2)}) copy-start(s32[32,4,128]{2,1,0:T(4,128)} %jump.1) | copy-start | bytes 196612
  8.7 14.8 %collective-permute-start = (bf16[32,7424]{1,0:T(8,128)(2,1)S(1)}, bf16[32,7424]{1,0:T(8,128)(2,1)S(1)}, u32[]{:S(2)}, u32[]{:S(2)}) collective-permute-start(bf16[32,7424]{1,0:T(8,128)(2,1)S(1)} %get-tuple-element.28.own), channel_id=1, source_target_pairs={{0,18},{1,19},{2,16},{3,17},{4,22},{5,23},{6,20},{7,21},{8,26},{9,... | collective-permute-start | bytes 1425416 | tf_op jit(solution)/shard_map/ppermute | solution.py:388
  11.2 18.2 %collective-permute-start.7 = (bf16[64,3712]{1,0:T(8,128)(2,1)S(1)}, bf16[64,3712]{1,0:T(8,128)(2,1)S(1)}, u32[]{:S(2)}, u32[]{:S(2)}) collective-permute-start(bf16[64,3712]{1,0:T(8,128)(2,1)S(1)} %copy-done), channel_id=1, source_target_pairs={{0,12},{1,13},{2,14},{3,15},{4,0},{5,1},{6,2},{7,3},{8,4},{9,5},{1... | collective-permute-start | bytes 1425416 | tf_op jit(solution)/shard_map/ppermute | solution.py:388
  13.5 18.8 %collective-permute-start.1 = (bf16[32,7424]{1,0:T(8,128)(2,1)S(1)}, bf16[32,7424]{1,0:T(8,128)(2,1)S(1)}, u32[]{:S(2)}, u32[]{:S(2)}) collective-permute-start(bf16[32,7424]{1,0:T(8,128)(2,1)S(1)} %get-tuple-element.29), channel_id=1, source_target_pairs={{0,2},{1,3},{2,0},{3,1},{4,6},{5,7},{6,4},{7,5},{8,10},{9,11},{10,... | collective-permute-start | bytes 1425416 | tf_op jit(solution)/shard_map/ppermute | solution.py:388
  14.0 18.3 %collective-permute-start.2 = (bf16[32,7424]{1,0:T(8,128)(2,1)S(1)}, bf16[32,7424]{1,0:T(8,128)(2,1)S(1)}, u32[]{:S(2)}, u32[]{:S(2)}) collective-permute-start(bf16[32,7424]{1,0:T(8,128)(2,1)S(1)} %get-tuple-element.30), channel_id=1, source_target_pairs={{0,16},{1,17},{2,18},{3,19},{4,20},{5,21},{6,22},{7,23},{8,24},{9,... | collective-permute-start | bytes 1425416 | tf_op jit(solution)/shard_map/ppermute | solution.py:388
  20.1 12.2 %collective-permute-start.4 = (bf16[64,3712]{1,0:T(8,128)(2,1)S(1)}, bf16[64,3712]{1,0:T(8,128)(2,1)S(1)}, u32[]{:S(2)}, u32[]{:S(2)}) collective-permute-start(bf16[64,3712]{1,0:T(8,128)(2,1)S(1)} %collective-permute-done.3.mine_1), channel_id=1, source_target_pairs={{0,1},{1,0},{2,3},{3,2},{4,5},{5,4},{6,7},{7,6},{8,9},{9,8},{10,11... | collective-permute-start | bytes 1425416 | tf_op jit(solution)/shard_map/ppermute | solution.py:388
  23.5 18.2 %collective-permute-start.5 = (bf16[64,3712]{1,0:T(8,128)(2,1)S(1)}, bf16[64,3712]{1,0:T(8,128)(2,1)S(1)}, u32[]{:S(2)}, u32[]{:S(2)}) collective-permute-start(bf16[64,3712]{1,0:T(8,128)(2,1)S(1)} %collective-permute-done.3.mine_1), channel_id=1, source_target_pairs={{0,4},{1,5},{2,6},{3,7},{4,8},{5,9},{6,10},{7,11},{8,12},{9,13},{1... | collective-permute-start | bytes 1425416 | tf_op jit(solution)/shard_map/ppermute | solution.py:388
  29.4 14.2 %collective-permute-start.8 = (bf16[64,3712]{1,0:T(8,128)(2,1)S(1)}, bf16[64,3712]{1,0:T(8,128)(2,1)S(1)}, u32[]{:S(2)}, u32[]{:S(2)}) collective-permute-start(bf16[64,3712]{1,0:T(8,128)(2,1)S(1)} %collective-permute-done.7.mine_3), channel_id=1, source_target_pairs={{0,1},{1,0},{2,3},{3,2},{4,5},{5,4},{6,7},{7,6},{8,9},{9,8},{10,11... | collective-permute-start | bytes 1425416 | tf_op jit(solution)/shard_map/ppermute | solution.py:388
  32.3 1.0 %copy-start.1 = (bf16[64,3712]{1,0:T(8,128)(2,1)S(1)}, bf16[64,3712]{1,0:T(8,128)(2,1)}, u32[]{:S(2)}) copy-start(bf16[64,3712]{1,0:T(8,128)(2,1)} %shard_map.111._.mine_0) | copy-start | bytes 1425412
  41.8 3.7 %collective-permute-start.6 = (bf16[64,3712]{1,0:T(8,128)(2,1)S(1)}, bf16[64,3712]{1,0:T(8,128)(2,1)S(1)}, u32[]{:S(2)}, u32[]{:S(2)}) collective-permute-start(bf16[64,3712]{1,0:T(8,128)(2,1)S(1)} %shard_map.114.mine_2), channel_id=1, source_target_pairs={{0,1},{1,0},{2,3},{3,2},{4,5},{5,4},{6,7},{7,6},{8,9},{9,8},{10,11... | collective-permute-start | bytes 1425416 | tf_op jit(solution)/shard_map/ppermute | solution.py:388
  41.9 3.7 %collective-permute-start.9 = (f32[8,128]{1,0:T(8,128)S(1)}, f32[8,128]{1,0:T(8,128)S(1)}, u32[]{:S(2)}, u32[]{:S(2)}) collective-permute-start(f32[8,128]{1,0:T(8,128)S(1)} %get-tuple-element.37.sums), channel_id=1, source_target_pairs={{0,12},{1,13},{2,14},{3,15},{4,0},{5,1},{6,2},{7,3},{8,4},{9,5},{1... | collective-permute-start | bytes 12296 | tf_op jit(solution)/shard_map/ppermute | solution.py:388
  45.5 14.6 %copy-start.8 = (f32[3584]{0:T(1024)S(1)}, f32[3584]{0:T(1024)}, u32[]{:S(2)}) copy-start(f32[3584]{0:T(1024)} %param.15) | copy-start | bytes 43012
  47.0 14.4 %collective-permute-start.10 = (bf16[32,4096]{1,0:T(8,128)(2,1)S(1)}, bf16[32,4096]{1,0:T(8,128)(2,1)S(1)}, u32[]{:S(2)}, u32[]{:S(2)}) collective-permute-start(bf16[32,4096]{1,0:T(8,128)(2,1)S(1)} %get-tuple-element.38), channel_id=1, source_target_pairs={{0,18},{1,19},{2,16},{3,17},{4,22},{5,23},{6,20},{7,21},{8,26},{9,... | collective-permute-start | bytes 786440 | tf_op jit(solution)/shard_map/ppermute | solution.py:388
  49.5 11.9 %collective-permute-start.11 = (bf16[32,4096]{1,0:T(8,128)(2,1)S(1)}, bf16[32,4096]{1,0:T(8,128)(2,1)S(1)}, u32[]{:S(2)}, u32[]{:S(2)}) collective-permute-start(bf16[32,4096]{1,0:T(8,128)(2,1)S(1)} %get-tuple-element.39), channel_id=1, source_target_pairs={{0,2},{1,3},{2,0},{3,1},{4,6},{5,7},{6,4},{7,5},{8,10},{9,11},{10,... | collective-permute-start | bytes 786440 | tf_op jit(solution)/shard_map/ppermute | solution.py:388
  50.1 11.4 %collective-permute-start.12 = (bf16[32,4096]{1,0:T(8,128)(2,1)S(1)}, bf16[32,4096]{1,0:T(8,128)(2,1)S(1)}, u32[]{:S(2)}, u32[]{:S(2)}) collective-permute-start(bf16[32,4096]{1,0:T(8,128)(2,1)S(1)} %get-tuple-element.40), channel_id=1, source_target_pairs={{0,16},{1,17},{2,18},{3,19},{4,20},{5,21},{6,22},{7,23},{8,24},{9,... | collective-permute-start | bytes 786440 | tf_op jit(solution)/shard_map/ppermute | solution.py:388
  50.6 4.5 %collective-permute-start.13 = (f32[8,128]{1,0:T(8,128)S(1)}, f32[8,128]{1,0:T(8,128)S(1)}, u32[]{:S(2)}, u32[]{:S(2)}) collective-permute-start(f32[8,128]{1,0:T(8,128)S(1)} %get-tuple-element.45), channel_id=1, source_target_pairs={{0,8},{1,9},{2,10},{3,11},{4,12},{5,13},{6,14},{7,15},{8,0},{9,1},... | collective-permute-start | bytes 12296 | tf_op jit(solution)/shard_map/ppermute | solution.py:388
  51.2 5.4 %collective-permute-start.14 = (f32[8,128]{1,0:T(8,128)S(1)}, f32[8,128]{1,0:T(8,128)S(1)}, u32[]{:S(2)}, u32[]{:S(2)}) collective-permute-start(f32[8,128]{1,0:T(8,128)S(1)} %get-tuple-element.45), channel_id=1, source_target_pairs={{0,4},{1,5},{2,6},{3,7},{4,8},{5,9},{6,10},{7,11},{8,12},{9,13},{1... | collective-permute-start | bytes 12296 | tf_op jit(solution)/shard_map/ppermute | solution.py:388
  56.7 3.5 %collective-permute-start.15 = (f32[1,64]{1,0:T(1,128)S(1)}, f32[1,64]{1,0:T(1,128)S(1)}, u32[]{:S(2)}, u32[]{:S(2)}) collective-permute-start(f32[1,64]{1,0:T(1,128)S(1)} %get-tuple-element.46), channel_id=1, source_target_pairs={{0,0},{1,16},{2,2},{3,18},{4,4},{5,20},{6,6},{7,22},{8,8},{9,24},{... | collective-permute-start | bytes 776 | tf_op jit(solution)/shard_map/ppermute | solution.py:388
  57.3 4.1 %collective-permute-start.16 = (f32[1,64]{1,0:T(1,128)S(1)}, f32[1,64]{1,0:T(1,128)S(1)}, u32[]{:S(2)}, u32[]{:S(2)}) collective-permute-start(f32[1,64]{1,0:T(1,128)S(1)} %get-tuple-element.47), channel_id=1, source_target_pairs={{0,16},{1,0},{2,18},{3,2},{4,20},{5,4},{6,22},{7,6},{8,24},{9,8},{... | collective-permute-start | bytes 776 | tf_op jit(solution)/shard_map/ppermute | solution.py:388

commit v6 on v5

--- a/solution.py
+++ b/solution.py
@@ -180,8 +180,8 @@
     rest[...] = jnp.where(y == s, total[1:, :per], total[:1, :per])
 
 
-def after_kernel(values, _, out):
-    out[...] = values[...]
+def after_kernel(*refs):
+    del refs
 
 
 def target_block(lane, m, x, z, ring):
@@ -448,7 +448,14 @@
             pltpu.SemaphoreType.DMA((2,)),
         ],
     )
-    (part_2,) = call(after_kernel, [(part_2.shape, BF)], part_2, codes, far=(1,))
+    part_2 = pl.pallas_call(
+        after_kernel,
+        in_specs=[pl.BlockSpec(memory_space=pl.ANY)] * 2,
+        out_specs=pl.BlockSpec(memory_space=pl.ANY),
+        out_shape=jax.ShapeDtypeStruct(part_2.shape, BF),
+        input_output_aliases={0: 0},
+        compiler_params=pltpu.CompilerParams(vmem_limit_bytes=1 << 20),
+    )(part_2, codes)
     own_recon, own_codes, own_scores, to_x, to_y, to_d, sums_23, sums_01 = call(
         late_kernel,
         [((tok, width), F32), ((tok, names), BF), ((tok, names), F32)]

time: 63.8 us -> 63.6 us (level)
    pallas_call x7 -> x6, Pallas kernels: 8.13 us -> 8.09 us  [call(): pl.pallas_call(kernel, in_specs=[pl.BlockSpec(memory_space=pl.ANY if i in...]
where the time goes in v6:
time: 63.6 us; the launch traced here: 62.6 us
  waiting for transfers between devices  27.6 us (43%)
  starting transfers between devices  23.1 us (36%)
  Pallas kernels  8.09 us (13%)
  local copies, waits for them, and re-layouts  2.94 us (5%)
  between operations  0.77 us (1%)
    ppermute x17, waiting for transfers between devices, permute(): return lax.ppermute(values, AXES, pairs)  27.6 us
    ppermute x17, starting transfers between devices, permute(): return lax.ppermute(values, AXES, pairs)  23.1 us
    pallas_call x6, Pallas kernels, call(): pl.pallas_call(kernel, in_specs=[pl.BlockSpec(memory_space=pl.ANY if i in...  8.09 us
    unnamed x18, local copies, waits for them, and re-layouts  2.93 us
  transfers between devices with their start and end apart: 17, of which 9 were waited for; matrix products, arithmetic and copies ran while one was open for 0% of the time, Pallas kernels for 5%

profile of v6, /device:TPU:0, one launch (start us, length us, event | category | flops | bytes accessed | tf_op | source)
XLA Modules:
  0.0 62.6 jit_solution(10022820939360643823)
XLA Ops:
  0.7 2.4 %shard_map.111._.mine_0 = bf16[64,3712]{1,0:T(8,128)(2,1)} custom-call(bf16[3584,128]{1,0:T(8,128)(2,1)} %enc.3, bf16[128,3584]{1,0:T(8,128)(2,1)} %dec.3, f32[1,128]{1,0:T(1,128)} %bitcast.5), custom_call_target="tpu_custom_call" | custom-call | tf_op jit(solution)/shard_map/pallas_call | solution.py:110
  3.1 3.1 %collective-permute-start.3 = (bf16[64,3712]{1,0:T(8,128)(2,1)}, bf16[64,3712]{1,0:T(8,128)(2,1)S(1)}, u32[]{:S(2)}, u32[]{:S(2)}) collective-permute-start(bf16[64,3712]{1,0:T(8,128)(2,1)} %shard_map.111._.mine_0), channel_id=1, source_target_pairs={{0,4},{1,5},{2,6},{3,7},{4,8},{5,9},{6,10},{7,11},{8,12},{9,13},{1... | collective-permute-start | bytes 1425416 | tf_op jit(solution)/shard_map/ppermute | solution.py:388
  6.2 1.0 %copy-done = bf16[64,3712]{1,0:T(8,128)(2,1)S(1)} copy-done((bf16[64,3712]{1,0:T(8,128)(2,1)S(1)}, bf16[64,3712]{1,0:T(8,128)(2,1)}, u32[]{:S(2)}) %copy-start) | copy-done | bytes 475160
  7.2 0.8 %copy-done.6 = s32[32,4,128]{2,1,0:T(4,128)S(1)} copy-done((s32[32,4,128]{2,1,0:T(4,128)S(1)}, s32[32,4,128]{2,1,0:T(4,128)}, u32[]{:S(2)}) %copy-start.6) | copy-done | bytes 65560
  8.1 0.7 %shard_map.112 = (bf16[32,7424]{1,0:T(8,128)(2,1)S(1)}, bf16[32,7424]{1,0:T(8,128)(2,1)S(1)}, bf16[32,7424]{1,0:T(8,128)(2,1)S(1)}, bf16[32,256]{1,0:T(8,128)(2,1)S(1)}) custom-call(bf16[32,3584]{1,0:T(8,128)(2,1)S(1)} %copy-done.4, bf16[32,3584]{1,0:T(8,128)(2,1)S(1)} %copy-done.5, s32[4,32]{1,0:T(4,128)S(1)} %bitcast.3, s32[32,4,128]{2,1,0:T(4,128)S(1)} %copy-done.6, ...), custom_call_target="tpu_custom_call" | custom-call | tf_op jit(solution)/shard_map/pallas_call | solution.py:110
  8.7 2.5 %collective-permute-start = (bf16[32,7424]{1,0:T(8,128)(2,1)S(1)}, bf16[32,7424]{1,0:T(8,128)(2,1)S(1)}, u32[]{:S(2)}, u32[]{:S(2)}) collective-permute-start(bf16[32,7424]{1,0:T(8,128)(2,1)S(1)} %get-tuple-element.28.own), channel_id=1, source_target_pairs={{0,18},{1,19},{2,16},{3,17},{4,22},{5,23},{6,20},{7,21},{8,26},{9,... | collective-permute-start | bytes 1425416 | tf_op jit(solution)/shard_map/ppermute | solution.py:388
  11.2 2.2 %collective-permute-start.7 = (bf16[64,3712]{1,0:T(8,128)(2,1)S(1)}, bf16[64,3712]{1,0:T(8,128)(2,1)S(1)}, u32[]{:S(2)}, u32[]{:S(2)}) collective-permute-start(bf16[64,3712]{1,0:T(8,128)(2,1)S(1)} %copy-done), channel_id=1, source_target_pairs={{0,12},{1,13},{2,14},{3,15},{4,0},{5,1},{6,2},{7,3},{8,4},{9,5},{1... | collective-permute-start | bytes 1425416 | tf_op jit(solution)/shard_map/ppermute | solution.py:388
  13.5 0.5 collective-permute-start.1
  14.0 0.3 collective-permute-start.2
  14.4 5.8 %collective-permute-done.3.mine_1 = bf16[64,3712]{1,0:T(8,128)(2,1)S(1)} collective-permute-done((bf16[64,3712]{1,0:T(8,128)(2,1)}, bf16[64,3712]{1,0:T(8,128)(2,1)S(1)}, u32[]{:S(2)}, u32[]{:S(2)}) %collective-permute-start.3) | collective-permute-done | bytes 475168 | tf_op jit(solution)/shard_map/ppermute | solution.py:388
  20.1 3.4 %collective-permute-done.from_d = bf16[32,7424]{1,0:T(8,128)(2,1)S(1)} collective-permute-done((bf16[32,7424]{1,0:T(8,128)(2,1)S(1)}, bf16[32,7424]{1,0:T(8,128)(2,1)S(1)}, u32[]{:S(2)}, u32[]{:S(2)}) %collective-permute-start) | collective-permute-done | bytes 475168 | tf_op jit(solution)/shard_map/ppermute | solution.py:388
  23.5 1.6 %collective-permute-start.5 = (bf16[64,3712]{1,0:T(8,128)(2,1)S(1)}, bf16[64,3712]{1,0:T(8,128)(2,1)S(1)}, u32[]{:S(2)}, u32[]{:S(2)}) collective-permute-start(bf16[64,3712]{1,0:T(8,128)(2,1)S(1)} %collective-permute-done.3.mine_1), channel_id=1, source_target_pairs={{0,4},{1,5},{2,6},{3,7},{4,8},{5,9},{6,10},{7,11},{8,12},{9,13},{1... | collective-permute-start | bytes 1425416 | tf_op jit(solution)/shard_map/ppermute | solution.py:388
  25.1 4.3 %collective-permute-done.7.mine_3 = bf16[64,3712]{1,0:T(8,128)(2,1)S(1)} collective-permute-done((bf16[64,3712]{1,0:T(8,128)(2,1)S(1)}, bf16[64,3712]{1,0:T(8,128)(2,1)S(1)}, u32[]{:S(2)}, u32[]{:S(2)}) %collective-permute-start.7) | collective-permute-done | bytes 475168 | tf_op jit(solution)/shard_map/ppermute | solution.py:388
  29.5 2.9 %collective-permute-done.1.from_x = bf16[32,7424]{1,0:T(8,128)(2,1)S(1)} collective-permute-done((bf16[32,7424]{1,0:T(8,128)(2,1)S(1)}, bf16[32,7424]{1,0:T(8,128)(2,1)S(1)}, u32[]{:S(2)}, u32[]{:S(2)}) %collective-permute-start.1) | collective-permute-done | bytes 475168 | tf_op jit(solution)/shard_map/ppermute | solution.py:388
  32.3 1.0 %copy-done.1 = bf16[64,3712]{1,0:T(8,128)(2,1)S(1)} copy-done((bf16[64,3712]{1,0:T(8,128)(2,1)S(1)}, bf16[64,3712]{1,0:T(8,128)(2,1)}, u32[]{:S(2)}) %copy-start.1) | copy-done | bytes 475160
  33.4 2.2 %shard_map.113 = (bf16[128,7168]{1,0:T(8,128)(2,1)S(1)}, bf16[128,256]{1,0:T(8,128)(2,1)S(1)}, f32[128,3584]{1,0:T(8,128)S(1)}, bf16[128,128]{1,0:T(8,128)(2,1)S...) custom-call(bf16[32,7424]{1,0:T(8,128)(2,1)S(1)} %collective-permute-done.from_d, ...), custom_call_target="tpu_custom_call" | custom-call | tf_op jit(solution)/shard_map/pallas_call | solution.py:110
  35.6 6.2 %collective-permute-done.5.refs_0_ = bf16[64,3712]{1,0:T(8,128)(2,1)S(1)} collective-permute-done((bf16[64,3712]{1,0:T(8,128)(2,1)S(1)}, bf16[64,3712]{1,0:T(8,128)(2,1)S(1)}, u32[]{:S(2)}, u32[]{:S(2)}) %collective-permute-start.5) | collective-permute-done | bytes 475168 | tf_op jit(solution)/shard_map/ppermute | solution.py:388
  41.8 1.7 %collective-permute-start.9 = (f32[8,128]{1,0:T(8,128)S(1)}, f32[8,128]{1,0:T(8,128)S(1)}, u32[]{:S(2)}, u32[]{:S(2)}) collective-permute-start(f32[8,128]{1,0:T(8,128)S(1)} %get-tuple-element.37.sums), channel_id=1, source_target_pairs={{0,12},{1,13},{2,14},{3,15},{4,0},{5,1},{6,2},{7,3},{8,4},{9,5},{1... | collective-permute-start | bytes 12296 | tf_op jit(solution)/shard_map/ppermute | solution.py:388
  43.5 1.9 %collective-permute-done.9.one = f32[8,128]{1,0:T(8,128)S(1)} collective-permute-done((f32[8,128]{1,0:T(8,128)S(1)}, f32[8,128]{1,0:T(8,128)S(1)}, u32[]{:S(2)}, u32[]{:S(2)}) %collective-permute-start.9) | collective-permute-done | bytes 4128 | tf_op jit(solution)/shard_map/ppermute | solution.py:388
  45.4 1.5 %shard_map.115 = (f32[32,3584]{1,0:T(8,128)S(1)}, bf16[32,256]{1,0:T(8,128)(2,1)S(1)}, f32[32,256]{1,0:T(8,128)S(1)}, bf16[32,4096]{1,0:T(8,128)(2,1)S(1)}, bf16...) custom-call(bf16[128,7168]{1,0:T(8,128)(2,1)S(1)} %get-tuple-element.32.ro, ...), custom_call_target="tpu_custom_call" | custom-call | tf_op jit(solution)/shard_map/pallas_call | solution.py:110
  46.9 2.5 %collective-permute-start.10 = (bf16[32,4096]{1,0:T(8,128)(2,1)S(1)}, bf16[32,4096]{1,0:T(8,128)(2,1)S(1)}, u32[]{:S(2)}, u32[]{:S(2)}) collective-permute-start(bf16[32,4096]{1,0:T(8,128)(2,1)S(1)} %get-tuple-element.38), channel_id=1, source_target_pairs={{0,18},{1,19},{2,16},{3,17},{4,22},{5,23},{6,20},{7,21},{8,26},{9,... | collective-permute-start | bytes 786440 | tf_op jit(solution)/shard_map/ppermute | solution.py:388
  49.4 0.5 collective-permute-start.11
  49.9 0.5 collective-permute-start.12
  50.4 0.6 collective-permute-start.13
  51.0 3.5 %collective-permute-start.14 = (f32[8,128]{1,0:T(8,128)S(1)}, f32[8,128]{1,0:T(8,128)S(1)}, u32[]{:S(2)}, u32[]{:S(2)}) collective-permute-start(f32[8,128]{1,0:T(8,128)S(1)} %get-tuple-element.45), channel_id=1, source_target_pairs={{0,4},{1,5},{2,6},{3,7},{4,8},{5,9},{6,10},{7,11},{8,12},{9,13},{1... | collective-permute-start | bytes 12296 | tf_op jit(solution)/shard_map/ppermute | solution.py:388
  54.5 0.4 collective-permute-done.13.two
  54.9 1.5 %collective-permute-done.14.three = f32[8,128]{1,0:T(8,128)S(1)} collective-permute-done((f32[8,128]{1,0:T(8,128)S(1)}, f32[8,128]{1,0:T(8,128)S(1)}, u32[]{:S(2)}, u32[]{:S(2)}) %collective-permute-start.14) | collective-permute-done | bytes 4128 | tf_op jit(solution)/shard_map/ppermute | solution.py:388
  56.4 0.1 shard_map.116
  56.5 0.7 %collective-permute-start.15 = (f32[1,64]{1,0:T(1,128)S(1)}, f32[1,64]{1,0:T(1,128)S(1)}, u32[]{:S(2)}, u32[]{:S(2)}) collective-permute-start(f32[1,64]{1,0:T(1,128)S(1)} %get-tuple-element.46), channel_id=1, source_target_pairs={{0,0},{1,16},{2,2},{3,18},{4,4},{5,20},{6,6},{7,22},{8,8},{9,24},{... | collective-permute-start | bytes 776 | tf_op jit(solution)/shard_map/ppermute | solution.py:388
  57.2 2.8 %collective-permute-start.16 = (f32[1,64]{1,0:T(1,128)S(1)}, f32[1,64]{1,0:T(1,128)S(1)}, u32[]{:S(2)}, u32[]{:S(2)}) collective-permute-start(f32[1,64]{1,0:T(1,128)S(1)} %get-tuple-element.47), channel_id=1, source_target_pairs={{0,16},{1,0},{2,18},{3,2},{4,20},{5,4},{6,22},{7,6},{8,24},{9,8},{... | collective-permute-start | bytes 776 | tf_op jit(solution)/shard_map/ppermute | solution.py:388
  60.0 1.3 %collective-permute-done.16.rest = f32[1,64]{1,0:T(1,128)S(1)} collective-permute-done((f32[1,64]{1,0:T(1,128)S(1)}, f32[1,64]{1,0:T(1,128)S(1)}, u32[]{:S(2)}, u32[]{:S(2)}) %collective-permute-start.16) | collective-permute-done | bytes 288 | tf_op jit(solution)/shard_map/ppermute | solution.py:388
  61.3 1.3 %shard_map.117 = (bf16[32,4,128]{2,1,0:T(4,128)(2,1)}, f32[32,4,128]{2,1,0:T(4,128)}, bf16[32,3584]{1,0:T(8,128)(2,1)}, f32[1,64]{1,0:T(1,128)}) custom-call(bf16[32,4096]{1,0:T(8,128)(2,1)S(1)} %collective-permute-done.10.from_d, bf16[32,4096]{1,0:T(8,128)(2,1)S(1)} %collective-permute-done.11.from_x, bf16[32,4096]{1,0:T(8,128)(2,1)S(1)} %collective-permute-done.12.from_y, ...), custom_call_target="tpu_custom_call" | custom-call | tf_op jit(solution)/shard_map/pallas_call | solution.py:110
  (28 shorter events, 0.1 us)
Async XLA Ops:
  0.6 31.7 %copy-start.2 = (bf16[3584,128]{1,0:T(8,128)(2,1)S(1)}, bf16[3584,128]{1,0:T(8,128)(2,1)}, u32[]{:S(2)}) copy-start(bf16[3584,128]{1,0:T(8,128)(2,1)} %enc.3) | copy-start | bytes 2752516
  0.6 31.7 %copy-start.3 = (bf16[128,3584]{1,0:T(8,128)(2,1)S(1)}, bf16[128,3584]{1,0:T(8,128)(2,1)}, u32[]{:S(2)}) copy-start(bf16[128,3584]{1,0:T(8,128)(2,1)} %dec.3) | copy-start | bytes 2752516
  0.7 5.5 %copy-start.7 = (s32[32,4]{0,1:T(4,128)S(1)}, s32[32,4]{0,1:T(4,128)}, u32[]{:S(2)}) copy-start(s32[32,4]{0,1:T(4,128)} %param.10) | copy-start | bytes 1540
  0.7 5.5 %copy-start.4 = (bf16[32,3584]{1,0:T(8,128)(2,1)S(1)}, bf16[32,3584]{1,0:T(8,128)(2,1)}, u32[]{:S(2)}) copy-start(bf16[32,3584]{1,0:T(8,128)(2,1)} %res.1) | copy-start | bytes 688132
  0.7 5.5 %copy-start.5 = (bf16[32,3584]{1,0:T(8,128)(2,1)S(1)}, bf16[32,3584]{1,0:T(8,128)(2,1)}, u32[]{:S(2)}) copy-start(bf16[32,3584]{1,0:T(8,128)(2,1)} %grad.1) | copy-start | bytes 688132
  3.1 17.1 %collective-permute-start.3 = (bf16[64,3712]{1,0:T(8,128)(2,1)}, bf16[64,3712]{1,0:T(8,128)(2,1)S(1)}, u32[]{:S(2)}, u32[]{:S(2)}) collective-permute-start(bf16[64,3712]{1,0:T(8,128)(2,1)} %shard_map.111._.mine_0), channel_id=1, source_target_pairs={{0,4},{1,5},{2,6},{3,7},{4,8},{5,9},{6,10},{7,11},{8,12},{9,13},{1... | collective-permute-start | bytes 1425416 | tf_op jit(solution)/shard_map/ppermute | solution.py:388
  6.2 1.1 %copy-start = (bf16[64,3712]{1,0:T(8,128)(2,1)S(1)}, bf16[64,3712]{1,0:T(8,128)(2,1)}, u32[]{:S(2)}) copy-start(bf16[64,3712]{1,0:T(8,128)(2,1)} %shard_map.111._.mine_0) | copy-start | bytes 1425412
  7.2 0.8 %copy-start.6 = (s32[32,4,128]{2,1,0:T(4,128)S(1)}, s32[32,4,128]{2,1,0:T(4,128)}, u32[]{:S(2)}) copy-start(s32[32,4,128]{2,1,0:T(4,128)} %jump.1) | copy-start | bytes 196612
  8.7 14.8 %collective-permute-start = (bf16[32,7424]{1,0:T(8,128)(2,1)S(1)}, bf16[32,7424]{1,0:T(8,128)(2,1)S(1)}, u32[]{:S(2)}, u32[]{:S(2)}) collective-permute-start(bf16[32,7424]{1,0:T(8,128)(2,1)S(1)} %get-tuple-element.28.own), channel_id=1, source_target_pairs={{0,18},{1,19},{2,16},{3,17},{4,22},{5,23},{6,20},{7,21},{8,26},{9,... | collective-permute-start | bytes 1425416 | tf_op jit(solution)/shard_map/ppermute | solution.py:388
  11.2 18.2 %collective-permute-start.7 = (bf16[64,3712]{1,0:T(8,128)(2,1)S(1)}, bf16[64,3712]{1,0:T(8,128)(2,1)S(1)}, u32[]{:S(2)}, u32[]{:S(2)}) collective-permute-start(bf16[64,3712]{1,0:T(8,128)(2,1)S(1)} %copy-done), channel_id=1, source_target_pairs={{0,12},{1,13},{2,14},{3,15},{4,0},{5,1},{6,2},{7,3},{8,4},{9,5},{1... | collective-permute-start | bytes 1425416 | tf_op jit(solution)/shard_map/ppermute | solution.py:388
  13.5 18.8 %collective-permute-start.1 = (bf16[32,7424]{1,0:T(8,128)(2,1)S(1)}, bf16[32,7424]{1,0:T(8,128)(2,1)S(1)}, u32[]{:S(2)}, u32[]{:S(2)}) collective-permute-start(bf16[32,7424]{1,0:T(8,128)(2,1)S(1)} %get-tuple-element.29), channel_id=1, source_target_pairs={{0,2},{1,3},{2,0},{3,1},{4,6},{5,7},{6,4},{7,5},{8,10},{9,11},{10,... | collective-permute-start | bytes 1425416 | tf_op jit(solution)/shard_map/ppermute | solution.py:388
  14.0 18.3 %collective-permute-start.2 = (bf16[32,7424]{1,0:T(8,128)(2,1)S(1)}, bf16[32,7424]{1,0:T(8,128)(2,1)S(1)}, u32[]{:S(2)}, u32[]{:S(2)}) collective-permute-start(bf16[32,7424]{1,0:T(8,128)(2,1)S(1)} %get-tuple-element.30), channel_id=1, source_target_pairs={{0,16},{1,17},{2,18},{3,19},{4,20},{5,21},{6,22},{7,23},{8,24},{9,... | collective-permute-start | bytes 1425416 | tf_op jit(solution)/shard_map/ppermute | solution.py:388
  20.1 12.2 %collective-permute-start.4 = (bf16[64,3712]{1,0:T(8,128)(2,1)S(1)}, bf16[64,3712]{1,0:T(8,128)(2,1)S(1)}, u32[]{:S(2)}, u32[]{:S(2)}) collective-permute-start(bf16[64,3712]{1,0:T(8,128)(2,1)S(1)} %collective-permute-done.3.mine_1), channel_id=1, source_target_pairs={{0,1},{1,0},{2,3},{3,2},{4,5},{5,4},{6,7},{7,6},{8,9},{9,8},{10,11... | collective-permute-start | bytes 1425416 | tf_op jit(solution)/shard_map/ppermute | solution.py:388
  23.5 18.2 %collective-permute-start.5 = (bf16[64,3712]{1,0:T(8,128)(2,1)S(1)}, bf16[64,3712]{1,0:T(8,128)(2,1)S(1)}, u32[]{:S(2)}, u32[]{:S(2)}) collective-permute-start(bf16[64,3712]{1,0:T(8,128)(2,1)S(1)} %collective-permute-done.3.mine_1), channel_id=1, source_target_pairs={{0,4},{1,5},{2,6},{3,7},{4,8},{5,9},{6,10},{7,11},{8,12},{9,13},{1... | collective-permute-start | bytes 1425416 | tf_op jit(solution)/shard_map/ppermute | solution.py:388
  29.4 14.1 %collective-permute-start.8 = (bf16[64,3712]{1,0:T(8,128)(2,1)S(1)}, bf16[64,3712]{1,0:T(8,128)(2,1)S(1)}, u32[]{:S(2)}, u32[]{:S(2)}) collective-permute-start(bf16[64,3712]{1,0:T(8,128)(2,1)S(1)} %collective-permute-done.7.mine_3), channel_id=1, source_target_pairs={{0,1},{1,0},{2,3},{3,2},{4,5},{5,4},{6,7},{7,6},{8,9},{9,8},{10,11... | collective-permute-start | bytes 1425416 | tf_op jit(solution)/shard_map/ppermute | solution.py:388
  32.3 1.0 %copy-start.1 = (bf16[64,3712]{1,0:T(8,128)(2,1)S(1)}, bf16[64,3712]{1,0:T(8,128)(2,1)}, u32[]{:S(2)}) copy-start(bf16[64,3712]{1,0:T(8,128)(2,1)} %shard_map.111._.mine_0) | copy-start | bytes 1425412
  41.8 3.6 %collective-permute-start.6 = (bf16[64,3712]{1,0:T(8,128)(2,1)S(1)}, bf16[64,3712]{1,0:T(8,128)(2,1)S(1)}, u32[]{:S(2)}, u32[]{:S(2)}) collective-permute-start(bf16[64,3712]{1,0:T(8,128)(2,1)S(1)} %shard_map.114.mine_2), channel_id=1, source_target_pairs={{0,1},{1,0},{2,3},{3,2},{4,5},{5,4},{6,7},{7,6},{8,9},{9,8},{10,11... | collective-permute-start | bytes 1425416 | tf_op jit(solution)/shard_map/ppermute | solution.py:388
  41.8 3.6 %collective-permute-start.9 = (f32[8,128]{1,0:T(8,128)S(1)}, f32[8,128]{1,0:T(8,128)S(1)}, u32[]{:S(2)}, u32[]{:S(2)}) collective-permute-start(f32[8,128]{1,0:T(8,128)S(1)} %get-tuple-element.37.sums), channel_id=1, source_target_pairs={{0,12},{1,13},{2,14},{3,15},{4,0},{5,1},{6,2},{7,3},{8,4},{9,5},{1... | collective-permute-start | bytes 12296 | tf_op jit(solution)/shard_map/ppermute | solution.py:388
  45.4 14.6 %copy-start.8 = (f32[3584]{0:T(1024)S(1)}, f32[3584]{0:T(1024)}, u32[]{:S(2)}) copy-start(f32[3584]{0:T(1024)} %param.15) | copy-start | bytes 43012
  46.9 14.4 %collective-permute-start.10 = (bf16[32,4096]{1,0:T(8,128)(2,1)S(1)}, bf16[32,4096]{1,0:T(8,128)(2,1)S(1)}, u32[]{:S(2)}, u32[]{:S(2)}) collective-permute-start(bf16[32,4096]{1,0:T(8,128)(2,1)S(1)} %get-tuple-element.38), channel_id=1, source_target_pairs={{0,18},{1,19},{2,16},{3,17},{4,22},{5,23},{6,20},{7,21},{8,26},{9,... | collective-permute-start | bytes 786440 | tf_op jit(solution)/shard_map/ppermute | solution.py:388
  49.4 11.9 %collective-permute-start.11 = (bf16[32,4096]{1,0:T(8,128)(2,1)S(1)}, bf16[32,4096]{1,0:T(8,128)(2,1)S(1)}, u32[]{:S(2)}, u32[]{:S(2)}) collective-permute-start(bf16[32,4096]{1,0:T(8,128)(2,1)S(1)} %get-tuple-element.39), channel_id=1, source_target_pairs={{0,2},{1,3},{2,0},{3,1},{4,6},{5,7},{6,4},{7,5},{8,10},{9,11},{10,... | collective-permute-start | bytes 786440 | tf_op jit(solution)/shard_map/ppermute | solution.py:388
  49.9 11.4 %collective-permute-start.12 = (bf16[32,4096]{1,0:T(8,128)(2,1)S(1)}, bf16[32,4096]{1,0:T(8,128)(2,1)S(1)}, u32[]{:S(2)}, u32[]{:S(2)}) collective-permute-start(bf16[32,4096]{1,0:T(8,128)(2,1)S(1)} %get-tuple-element.40), channel_id=1, source_target_pairs={{0,16},{1,17},{2,18},{3,19},{4,20},{5,21},{6,22},{7,23},{8,24},{9,... | collective-permute-start | bytes 786440 | tf_op jit(solution)/shard_map/ppermute | solution.py:388
  50.4 4.5 %collective-permute-start.13 = (f32[8,128]{1,0:T(8,128)S(1)}, f32[8,128]{1,0:T(8,128)S(1)}, u32[]{:S(2)}, u32[]{:S(2)}) collective-permute-start(f32[8,128]{1,0:T(8,128)S(1)} %get-tuple-element.45), channel_id=1, source_target_pairs={{0,8},{1,9},{2,10},{3,11},{4,12},{5,13},{6,14},{7,15},{8,0},{9,1},... | collective-permute-start | bytes 12296 | tf_op jit(solution)/shard_map/ppermute | solution.py:388
  51.0 5.4 %collective-permute-start.14 = (f32[8,128]{1,0:T(8,128)S(1)}, f32[8,128]{1,0:T(8,128)S(1)}, u32[]{:S(2)}, u32[]{:S(2)}) collective-permute-start(f32[8,128]{1,0:T(8,128)S(1)} %get-tuple-element.45), channel_id=1, source_target_pairs={{0,4},{1,5},{2,6},{3,7},{4,8},{5,9},{6,10},{7,11},{8,12},{9,13},{1... | collective-permute-start | bytes 12296 | tf_op jit(solution)/shard_map/ppermute | solution.py:388
  56.5 3.5 %collective-permute-start.15 = (f32[1,64]{1,0:T(1,128)S(1)}, f32[1,64]{1,0:T(1,128)S(1)}, u32[]{:S(2)}, u32[]{:S(2)}) collective-permute-start(f32[1,64]{1,0:T(1,128)S(1)} %get-tuple-element.46), channel_id=1, source_target_pairs={{0,0},{1,16},{2,2},{3,18},{4,4},{5,20},{6,6},{7,22},{8,8},{9,24},{... | collective-permute-start | bytes 776 | tf_op jit(solution)/shard_map/ppermute | solution.py:388
  57.2 4.1 %collective-permute-start.16 = (f32[1,64]{1,0:T(1,128)S(1)}, f32[1,64]{1,0:T(1,128)S(1)}, u32[]{:S(2)}, u32[]{:S(2)}) collective-permute-start(f32[1,64]{1,0:T(1,128)S(1)} %get-tuple-element.47), channel_id=1, source_target_pairs={{0,16},{1,0},{2,18},{3,2},{4,20},{5,4},{6,22},{7,6},{8,24},{9,8},{... | collective-permute-start | bytes 776 | tf_op jit(solution)/shard_map/ppermute | solution.py:388

commit v7 on v6

--- a/solution.py
+++ b/solution.py
@@ -101,9 +101,13 @@
     return lax.dot_general(a, b, (((1,), (1,)), ((), ())), preferred_element_type=F32)
 
 
+def along(z):
+    return (4 - z) & 3
+
+
 def place_here():
     lat = lax.axis_index("lat")
-    return lax.rem(lat, 2), lax.axis_index("groups"), lax.div(lat, 2), lax.axis_index("seq")
+    return lax.rem(lat, 2), lax.axis_index("groups"), along(lax.div(lat, 2)), lax.axis_index("seq")
 
 
 def call(kernel, outs, *args, far=(), scratch=(), vmem=24):
@@ -187,7 +191,7 @@
 def target_block(lane, m, x, z, ring):
     turn = z - 2 * m - (lane >= 64).astype(jnp.int32)
     turn = jnp.where(turn < 0, turn + ring, turn)
-    return turn * 2 + x
+    return along(turn) * 2 + x
 
 
 def tokens_kernel(ring, res, grad, ids, jump, _, to_x, to_y, to_d, own_mask, sem):
@@ -349,7 +353,7 @@
             cols = slice(128 * (kk // 2), 128 * (kk // 2) + 128)
             turn = z - kk
             turn = jnp.where(turn < 0, turn + ring, turn)
-            block = turn * 2 + (x ^ x_rel)
+            block = along(turn) * 2 + (x ^ x_rel)
             pair = []
             for src in (code_src, score_src):
                 near, far = src[x_rel][:, cols], src[2 + x_rel][:, cols]
@@ -400,7 +404,9 @@
         return permute(v, lambda gg, ll, ss: (gg, ll, 1 - ss))
 
     def by_z(v, k):
-        return permute(v, lambda gg, ll, ss: (gg, (ll + 2 * k) % lat_count, ss))
+        return permute(
+            v, lambda gg, ll, ss: (gg, 2 * along((along(ll // 2) + k) % ring) + ll % 2, ss)
+        )
 
     (own,) = call(
         weights_kernel,

time: 63.6 us -> 62.6 us (0.984); the launches traced: 62.6 us -> 62.3 us
  starting transfers between devices: 23.1 us -> 18.1 us
  waiting for transfers between devices: 27.6 us -> 32.4 us
    ppermute x17, starting transfers between devices: 23.1 us -> 18.1 us  [permute(): return lax.ppermute(values, AXES, pairs)]
    ppermute x17, waiting for transfers between devices: 27.6 us -> 32.4 us  [permute(): return lax.ppermute(values, AXES, pairs)]
where the time goes in v7:
time: 62.6 us; the launch traced here: 62.3 us
  waiting for transfers between devices  32.4 us (52%)
  starting transfers between devices  18.1 us (29%)
  Pallas kernels  8.09 us (13%)
  local copies, waits for them, and re-layouts  2.94 us (5%)
  between operations  0.77 us (1%)
    ppermute x17, waiting for transfers between devices, permute(): return lax.ppermute(values, AXES, pairs)  32.4 us
    ppermute x17, starting transfers between devices, permute(): return lax.ppermute(values, AXES, pairs)  18.1 us
    pallas_call x6, Pallas kernels, call(): pl.pallas_call(kernel, in_specs=[pl.BlockSpec(memory_space=pl.ANY if i in...  8.09 us
    unnamed x18, local copies, waits for them, and re-layouts  2.93 us
  transfers between devices with their start and end apart: 17, of which 9 were waited for; matrix products, arithmetic and copies ran while one was open for 0% of the time, Pallas kernels for 5%

profile of v7, /device:TPU:0, one launch (start us, length us, event | category | flops | bytes accessed | tf_op | source)
XLA Modules:
  0.0 62.3 jit_solution(1952409334483720926)
XLA Ops:
  0.7 2.4 %shard_map.111._.mine_0 = bf16[64,3712]{1,0:T(8,128)(2,1)} custom-call(bf16[3584,128]{1,0:T(8,128)(2,1)} %enc.3, bf16[128,3584]{1,0:T(8,128)(2,1)} %dec.3, f32[1,128]{1,0:T(1,128)} %bitcast.5), custom_call_target="tpu_custom_call" | custom-call | tf_op jit(solution)/shard_map/pallas_call | solution.py:114
  3.1 5.1 %collective-permute-start.3 = (bf16[64,3712]{1,0:T(8,128)(2,1)}, bf16[64,3712]{1,0:T(8,128)(2,1)S(1)}, u32[]{:S(2)}, u32[]{:S(2)}) collective-permute-start(bf16[64,3712]{1,0:T(8,128)(2,1)} %shard_map.111._.mine_0), channel_id=1, source_target_pairs={{0,12},{1,13},{2,14},{3,15},{4,0},{5,1},{6,2},{7,3},{8,4},{9,5},{1... | collective-permute-start | bytes 1425416 | tf_op jit(solution)/shard_map/ppermute | solution.py:392
  8.2 1.0 %copy-done = bf16[64,3712]{1,0:T(8,128)(2,1)S(1)} copy-done((bf16[64,3712]{1,0:T(8,128)(2,1)S(1)}, bf16[64,3712]{1,0:T(8,128)(2,1)}, u32[]{:S(2)}) %copy-start) | copy-done | bytes 475160
  9.2 0.8 %copy-done.6 = s32[32,4,128]{2,1,0:T(4,128)S(1)} copy-done((s32[32,4,128]{2,1,0:T(4,128)S(1)}, s32[32,4,128]{2,1,0:T(4,128)}, u32[]{:S(2)}) %copy-start.6) | copy-done | bytes 65560
  10.1 0.7 %shard_map.112 = (bf16[32,7424]{1,0:T(8,128)(2,1)S(1)}, bf16[32,7424]{1,0:T(8,128)(2,1)S(1)}, bf16[32,7424]{1,0:T(8,128)(2,1)S(1)}, bf16[32,256]{1,0:T(8,128)(2,1)S(1)}) custom-call(bf16[32,3584]{1,0:T(8,128)(2,1)S(1)} %copy-done.4, bf16[32,3584]{1,0:T(8,128)(2,1)S(1)} %copy-done.5, s32[4,32]{1,0:T(4,128)S(1)} %bitcast.3, s32[32,4,128]{2,1,0:T(4,128)S(1)} %copy-done.6, ...), custom_call_target="tpu_custom_call" | custom-call | tf_op jit(solution)/shard_map/pallas_call | solution.py:114
  10.8 2.5 %collective-permute-start = (bf16[32,7424]{1,0:T(8,128)(2,1)S(1)}, bf16[32,7424]{1,0:T(8,128)(2,1)S(1)}, u32[]{:S(2)}, u32[]{:S(2)}) collective-permute-start(bf16[32,7424]{1,0:T(8,128)(2,1)S(1)} %get-tuple-element.28.own), channel_id=1, source_target_pairs={{0,18},{1,19},{2,16},{3,17},{4,22},{5,23},{6,20},{7,21},{8,26},{9,... | collective-permute-start | bytes 1425416 | tf_op jit(solution)/shard_map/ppermute | solution.py:392
  13.3 0.0 collective-permute-start.7
  13.3 0.5 collective-permute-start.1
  13.8 0.5 collective-permute-start.2
  14.3 5.5 %collective-permute-done.3.mine_1 = bf16[64,3712]{1,0:T(8,128)(2,1)S(1)} collective-permute-done((bf16[64,3712]{1,0:T(8,128)(2,1)}, bf16[64,3712]{1,0:T(8,128)(2,1)S(1)}, u32[]{:S(2)}, u32[]{:S(2)}) %collective-permute-start.3) | collective-permute-done | bytes 475168 | tf_op jit(solution)/shard_map/ppermute | solution.py:392
  19.8 5.7 %collective-permute-done.from_d = bf16[32,7424]{1,0:T(8,128)(2,1)S(1)} collective-permute-done((bf16[32,7424]{1,0:T(8,128)(2,1)S(1)}, bf16[32,7424]{1,0:T(8,128)(2,1)S(1)}, u32[]{:S(2)}, u32[]{:S(2)}) %collective-permute-start) | collective-permute-done | bytes 475168 | tf_op jit(solution)/shard_map/ppermute | solution.py:392
  25.6 0.4 collective-permute-start.5
  26.0 4.8 %collective-permute-done.7.mine_3 = bf16[64,3712]{1,0:T(8,128)(2,1)S(1)} collective-permute-done((bf16[64,3712]{1,0:T(8,128)(2,1)S(1)}, bf16[64,3712]{1,0:T(8,128)(2,1)S(1)}, u32[]{:S(2)}, u32[]{:S(2)}) %collective-permute-start.7) | collective-permute-done | bytes 475168 | tf_op jit(solution)/shard_map/ppermute | solution.py:392
  30.9 0.0 collective-permute-start.8
  30.9 3.5 %collective-permute-done.1.from_x = bf16[32,7424]{1,0:T(8,128)(2,1)S(1)} collective-permute-done((bf16[32,7424]{1,0:T(8,128)(2,1)S(1)}, bf16[32,7424]{1,0:T(8,128)(2,1)S(1)}, u32[]{:S(2)}, u32[]{:S(2)}) %collective-permute-start.1) | collective-permute-done | bytes 475168 | tf_op jit(solution)/shard_map/ppermute | solution.py:392
  34.4 1.0 %copy-done.1 = bf16[64,3712]{1,0:T(8,128)(2,1)S(1)} copy-done((bf16[64,3712]{1,0:T(8,128)(2,1)S(1)}, bf16[64,3712]{1,0:T(8,128)(2,1)}, u32[]{:S(2)}) %copy-start.1) | copy-done | bytes 475160
  35.4 2.2 %shard_map.113 = (bf16[128,7168]{1,0:T(8,128)(2,1)S(1)}, bf16[128,256]{1,0:T(8,128)(2,1)S(1)}, f32[128,3584]{1,0:T(8,128)S(1)}, bf16[128,128]{1,0:T(8,128)(2,1)S...) custom-call(bf16[32,7424]{1,0:T(8,128)(2,1)S(1)} %collective-permute-done.from_d, ...), custom_call_target="tpu_custom_call" | custom-call | tf_op jit(solution)/shard_map/pallas_call | solution.py:114
  37.6 2.3 %collective-permute-done.5.refs_0_ = bf16[64,3712]{1,0:T(8,128)(2,1)S(1)} collective-permute-done((bf16[64,3712]{1,0:T(8,128)(2,1)S(1)}, bf16[64,3712]{1,0:T(8,128)(2,1)S(1)}, u32[]{:S(2)}, u32[]{:S(2)}) %collective-permute-start.5) | collective-permute-done | bytes 475168 | tf_op jit(solution)/shard_map/ppermute | solution.py:392
  39.9 0.5 collective-permute-start.9
  40.4 4.9 %collective-permute-done.9.one = f32[8,128]{1,0:T(8,128)S(1)} collective-permute-done((f32[8,128]{1,0:T(8,128)S(1)}, f32[8,128]{1,0:T(8,128)S(1)}, u32[]{:S(2)}, u32[]{:S(2)}) %collective-permute-start.9) | collective-permute-done | bytes 4128 | tf_op jit(solution)/shard_map/ppermute | solution.py:392
  45.3 1.5 %shard_map.115 = (f32[32,3584]{1,0:T(8,128)S(1)}, bf16[32,256]{1,0:T(8,128)(2,1)S(1)}, f32[32,256]{1,0:T(8,128)S(1)}, bf16[32,4096]{1,0:T(8,128)(2,1)S(1)}, bf16...) custom-call(bf16[128,7168]{1,0:T(8,128)(2,1)S(1)} %get-tuple-element.32.ro, ...), custom_call_target="tpu_custom_call" | custom-call | tf_op jit(solution)/shard_map/pallas_call | solution.py:114
  46.8 2.5 %collective-permute-start.10 = (bf16[32,4096]{1,0:T(8,128)(2,1)S(1)}, bf16[32,4096]{1,0:T(8,128)(2,1)S(1)}, u32[]{:S(2)}, u32[]{:S(2)}) collective-permute-start(bf16[32,4096]{1,0:T(8,128)(2,1)S(1)} %get-tuple-element.38), channel_id=1, source_target_pairs={{0,18},{1,19},{2,16},{3,17},{4,22},{5,23},{6,20},{7,21},{8,26},{9,... | collective-permute-start | bytes 786440 | tf_op jit(solution)/shard_map/ppermute | solution.py:392
  49.3 0.5 collective-permute-start.11
  49.8 0.5 collective-permute-start.12
  50.3 1.5 %collective-permute-start.14 = (f32[8,128]{1,0:T(8,128)S(1)}, f32[8,128]{1,0:T(8,128)S(1)}, u32[]{:S(2)}, u32[]{:S(2)}) collective-permute-start(f32[8,128]{1,0:T(8,128)S(1)} %get-tuple-element.45), channel_id=1, source_target_pairs={{0,12},{1,13},{2,14},{3,15},{4,0},{5,1},{6,2},{7,3},{8,4},{9,5},{1... | collective-permute-start | bytes 12296 | tf_op jit(solution)/shard_map/ppermute | solution.py:392
  51.9 3.0 %collective-permute-done.13.two = f32[8,128]{1,0:T(8,128)S(1)} collective-permute-done((f32[8,128]{1,0:T(8,128)S(1)}, f32[8,128]{1,0:T(8,128)S(1)}, u32[]{:S(2)}, u32[]{:S(2)}) %collective-permute-start.13) | collective-permute-done | bytes 4128 | tf_op jit(solution)/shard_map/ppermute | solution.py:392
  54.9 0.1 shard_map.116
  54.9 0.7 %collective-permute-start.15 = (f32[1,64]{1,0:T(1,128)S(1)}, f32[1,64]{1,0:T(1,128)S(1)}, u32[]{:S(2)}, u32[]{:S(2)}) collective-permute-start(f32[1,64]{1,0:T(1,128)S(1)} %get-tuple-element.46), channel_id=1, source_target_pairs={{0,0},{1,16},{2,2},{3,18},{4,4},{5,20},{6,6},{7,22},{8,8},{9,24},{... | collective-permute-start | bytes 776 | tf_op jit(solution)/shard_map/ppermute | solution.py:392
  55.6 2.8 %collective-permute-start.16 = (f32[1,64]{1,0:T(1,128)S(1)}, f32[1,64]{1,0:T(1,128)S(1)}, u32[]{:S(2)}, u32[]{:S(2)}) collective-permute-start(f32[1,64]{1,0:T(1,128)S(1)} %get-tuple-element.47), channel_id=1, source_target_pairs={{0,16},{1,0},{2,18},{3,2},{4,20},{5,4},{6,22},{7,6},{8,24},{9,8},{... | collective-permute-start | bytes 776 | tf_op jit(solution)/shard_map/ppermute | solution.py:392
  58.4 1.6 %collective-permute-done.16.rest = f32[1,64]{1,0:T(1,128)S(1)} collective-permute-done((f32[1,64]{1,0:T(1,128)S(1)}, f32[1,64]{1,0:T(1,128)S(1)}, u32[]{:S(2)}, u32[]{:S(2)}) %collective-permute-start.16) | collective-permute-done | bytes 288 | tf_op jit(solution)/shard_map/ppermute | solution.py:392
  60.0 1.0 %collective-permute-done.11.from_x = bf16[32,4096]{1,0:T(8,128)(2,1)S(1)} collective-permute-done((bf16[32,4096]{1,0:T(8,128)(2,1)S(1)}, bf16[32,4096]{1,0:T(8,128)(2,1)S(1)}, u32[]{:S(2)}, u32[]{:S(2)}) %collective-permute-start.11) | collective-permute-done | bytes 262176 | tf_op jit(solution)/shard_map/ppermute | solution.py:392
  61.0 1.3 %shard_map.117 = (bf16[32,4,128]{2,1,0:T(4,128)(2,1)}, f32[32,4,128]{2,1,0:T(4,128)}, bf16[32,3584]{1,0:T(8,128)(2,1)}, f32[1,64]{1,0:T(1,128)}) custom-call(bf16[32,4096]{1,0:T(8,128)(2,1)S(1)} %collective-permute-done.10.from_d, bf16[32,4096]{1,0:T(8,128)(2,1)S(1)} %collective-permute-done.11.from_x, bf16[32,4096]{1,0:T(8,128)(2,1)S(1)} %collective-permute-done.12.from_y, ...), custom_call_target="tpu_custom_call" | custom-call | tf_op jit(solution)/shard_map/pallas_call | solution.py:114
  (28 shorter events, 0.1 us)
Async XLA Ops:
  0.6 33.7 %copy-start.2 = (bf16[3584,128]{1,0:T(8,128)(2,1)S(1)}, bf16[3584,128]{1,0:T(8,128)(2,1)}, u32[]{:S(2)}) copy-start(bf16[3584,128]{1,0:T(8,128)(2,1)} %enc.3) | copy-start | bytes 2752516
  0.6 33.7 %copy-start.3 = (bf16[128,3584]{1,0:T(8,128)(2,1)S(1)}, bf16[128,3584]{1,0:T(8,128)(2,1)}, u32[]{:S(2)}) copy-start(bf16[128,3584]{1,0:T(8,128)(2,1)} %dec.3) | copy-start | bytes 2752516
  0.7 7.5 %copy-start.7 = (s32[32,4]{0,1:T(4,128)S(1)}, s32[32,4]{0,1:T(4,128)}, u32[]{:S(2)}) copy-start(s32[32,4]{0,1:T(4,128)} %param.10) | copy-start | bytes 1540
  0.7 7.5 %copy-start.4 = (bf16[32,3584]{1,0:T(8,128)(2,1)S(1)}, bf16[32,3584]{1,0:T(8,128)(2,1)}, u32[]{:S(2)}) copy-start(bf16[32,3584]{1,0:T(8,128)(2,1)} %res.1) | copy-start | bytes 688132
  0.7 7.5 %copy-start.5 = (bf16[32,3584]{1,0:T(8,128)(2,1)S(1)}, bf16[32,3584]{1,0:T(8,128)(2,1)}, u32[]{:S(2)}) copy-start(bf16[32,3584]{1,0:T(8,128)(2,1)} %grad.1) | copy-start | bytes 688132
  3.1 16.7 %collective-permute-start.3 = (bf16[64,3712]{1,0:T(8,128)(2,1)}, bf16[64,3712]{1,0:T(8,128)(2,1)S(1)}, u32[]{:S(2)}, u32[]{:S(2)}) collective-permute-start(bf16[64,3712]{1,0:T(8,128)(2,1)} %shard_map.111._.mine_0), channel_id=1, source_target_pairs={{0,12},{1,13},{2,14},{3,15},{4,0},{5,1},{6,2},{7,3},{8,4},{9,5},{1... | collective-permute-start | bytes 1425416 | tf_op jit(solution)/shard_map/ppermute | solution.py:392
  8.2 1.1 %copy-start = (bf16[64,3712]{1,0:T(8,128)(2,1)S(1)}, bf16[64,3712]{1,0:T(8,128)(2,1)}, u32[]{:S(2)}) copy-start(bf16[64,3712]{1,0:T(8,128)(2,1)} %shard_map.111._.mine_0) | copy-start | bytes 1425412
  9.2 0.8 %copy-start.6 = (s32[32,4,128]{2,1,0:T(4,128)S(1)}, s32[32,4,128]{2,1,0:T(4,128)}, u32[]{:S(2)}) copy-start(s32[32,4,128]{2,1,0:T(4,128)} %jump.1) | copy-start | bytes 196612
  10.8 14.8 %collective-permute-start = (bf16[32,7424]{1,0:T(8,128)(2,1)S(1)}, bf16[32,7424]{1,0:T(8,128)(2,1)S(1)}, u32[]{:S(2)}, u32[]{:S(2)}) collective-permute-start(bf16[32,7424]{1,0:T(8,128)(2,1)S(1)} %get-tuple-element.28.own), channel_id=1, source_target_pairs={{0,18},{1,19},{2,16},{3,17},{4,22},{5,23},{6,20},{7,21},{8,26},{9,... | collective-permute-start | bytes 1425416 | tf_op jit(solution)/shard_map/ppermute | solution.py:392
  13.3 17.6 %collective-permute-start.7 = (bf16[64,3712]{1,0:T(8,128)(2,1)S(1)}, bf16[64,3712]{1,0:T(8,128)(2,1)S(1)}, u32[]{:S(2)}, u32[]{:S(2)}) collective-permute-start(bf16[64,3712]{1,0:T(8,128)(2,1)S(1)} %copy-done), channel_id=1, source_target_pairs={{0,4},{1,5},{2,6},{3,7},{4,8},{5,9},{6,10},{7,11},{8,12},{9,13},{1... | collective-permute-start | bytes 1425416 | tf_op jit(solution)/shard_map/ppermute | solution.py:392
  13.3 21.1 %collective-permute-start.1 = (bf16[32,7424]{1,0:T(8,128)(2,1)S(1)}, bf16[32,7424]{1,0:T(8,128)(2,1)S(1)}, u32[]{:S(2)}, u32[]{:S(2)}) collective-permute-start(bf16[32,7424]{1,0:T(8,128)(2,1)S(1)} %get-tuple-element.29), channel_id=1, source_target_pairs={{0,2},{1,3},{2,0},{3,1},{4,6},{5,7},{6,4},{7,5},{8,10},{9,11},{10,... | collective-permute-start | bytes 1425416 | tf_op jit(solution)/shard_map/ppermute | solution.py:392
  13.8 20.5 %collective-permute-start.2 = (bf16[32,7424]{1,0:T(8,128)(2,1)S(1)}, bf16[32,7424]{1,0:T(8,128)(2,1)S(1)}, u32[]{:S(2)}, u32[]{:S(2)}) collective-permute-start(bf16[32,7424]{1,0:T(8,128)(2,1)S(1)} %get-tuple-element.30), channel_id=1, source_target_pairs={{0,16},{1,17},{2,18},{3,19},{4,20},{5,21},{6,22},{7,23},{8,24},{9,... | collective-permute-start | bytes 1425416 | tf_op jit(solution)/shard_map/ppermute | solution.py:392
  19.8 14.5 %collective-permute-start.4 = (bf16[64,3712]{1,0:T(8,128)(2,1)S(1)}, bf16[64,3712]{1,0:T(8,128)(2,1)S(1)}, u32[]{:S(2)}, u32[]{:S(2)}) collective-permute-start(bf16[64,3712]{1,0:T(8,128)(2,1)S(1)} %collective-permute-done.3.mine_1), channel_id=1, source_target_pairs={{0,1},{1,0},{2,3},{3,2},{4,5},{5,4},{6,7},{7,6},{8,9},{9,8},{10,11... | collective-permute-start | bytes 1425416 | tf_op jit(solution)/shard_map/ppermute | solution.py:392
  25.6 14.3 %collective-permute-start.5 = (bf16[64,3712]{1,0:T(8,128)(2,1)S(1)}, bf16[64,3712]{1,0:T(8,128)(2,1)S(1)}, u32[]{:S(2)}, u32[]{:S(2)}) collective-permute-start(bf16[64,3712]{1,0:T(8,128)(2,1)S(1)} %collective-permute-done.3.mine_1), channel_id=1, source_target_pairs={{0,12},{1,13},{2,14},{3,15},{4,0},{5,1},{6,2},{7,3},{8,4},{9,5},{1... | collective-permute-start | bytes 1425416 | tf_op jit(solution)/shard_map/ppermute | solution.py:392
  30.9 9.5 %collective-permute-start.8 = (bf16[64,3712]{1,0:T(8,128)(2,1)S(1)}, bf16[64,3712]{1,0:T(8,128)(2,1)S(1)}, u32[]{:S(2)}, u32[]{:S(2)}) collective-permute-start(bf16[64,3712]{1,0:T(8,128)(2,1)S(1)} %collective-permute-done.7.mine_3), channel_id=1, source_target_pairs={{0,1},{1,0},{2,3},{3,2},{4,5},{5,4},{6,7},{7,6},{8,9},{9,8},{10,11... | collective-permute-start | bytes 1425416 | tf_op jit(solution)/shard_map/ppermute | solution.py:392
  34.4 1.0 %copy-start.1 = (bf16[64,3712]{1,0:T(8,128)(2,1)S(1)}, bf16[64,3712]{1,0:T(8,128)(2,1)}, u32[]{:S(2)}) copy-start(bf16[64,3712]{1,0:T(8,128)(2,1)} %shard_map.111._.mine_0) | copy-start | bytes 1425412
  39.9 5.4 %collective-permute-start.6 = (bf16[64,3712]{1,0:T(8,128)(2,1)S(1)}, bf16[64,3712]{1,0:T(8,128)(2,1)S(1)}, u32[]{:S(2)}, u32[]{:S(2)}) collective-permute-start(bf16[64,3712]{1,0:T(8,128)(2,1)S(1)} %shard_map.114.mine_2), channel_id=1, source_target_pairs={{0,1},{1,0},{2,3},{3,2},{4,5},{5,4},{6,7},{7,6},{8,9},{9,8},{10,11... | collective-permute-start | bytes 1425416 | tf_op jit(solution)/shard_map/ppermute | solution.py:392
  39.9 5.4 %collective-permute-start.9 = (f32[8,128]{1,0:T(8,128)S(1)}, f32[8,128]{1,0:T(8,128)S(1)}, u32[]{:S(2)}, u32[]{:S(2)}) collective-permute-start(f32[8,128]{1,0:T(8,128)S(1)} %get-tuple-element.37.sums), channel_id=1, source_target_pairs={{0,4},{1,5},{2,6},{3,7},{4,8},{5,9},{6,10},{7,11},{8,12},{9,13},{1... | collective-permute-start | bytes 12296 | tf_op jit(solution)/shard_map/ppermute | solution.py:392
  45.3 13.1 %copy-start.8 = (f32[3584]{0:T(1024)S(1)}, f32[3584]{0:T(1024)}, u32[]{:S(2)}) copy-start(f32[3584]{0:T(1024)} %param.15) | copy-start | bytes 43012
  46.8 13.2 %collective-permute-start.10 = (bf16[32,4096]{1,0:T(8,128)(2,1)S(1)}, bf16[32,4096]{1,0:T(8,128)(2,1)S(1)}, u32[]{:S(2)}, u32[]{:S(2)}) collective-permute-start(bf16[32,4096]{1,0:T(8,128)(2,1)S(1)} %get-tuple-element.38), channel_id=1, source_target_pairs={{0,18},{1,19},{2,16},{3,17},{4,22},{5,23},{6,20},{7,21},{8,26},{9,... | collective-permute-start | bytes 786440 | tf_op jit(solution)/shard_map/ppermute | solution.py:392
  49.3 11.7 %collective-permute-start.11 = (bf16[32,4096]{1,0:T(8,128)(2,1)S(1)}, bf16[32,4096]{1,0:T(8,128)(2,1)S(1)}, u32[]{:S(2)}, u32[]{:S(2)}) collective-permute-start(bf16[32,4096]{1,0:T(8,128)(2,1)S(1)} %get-tuple-element.39), channel_id=1, source_target_pairs={{0,2},{1,3},{2,0},{3,1},{4,6},{5,7},{6,4},{7,5},{8,10},{9,11},{10,... | collective-permute-start | bytes 786440 | tf_op jit(solution)/shard_map/ppermute | solution.py:392
  49.8 11.2 %collective-permute-start.12 = (bf16[32,4096]{1,0:T(8,128)(2,1)S(1)}, bf16[32,4096]{1,0:T(8,128)(2,1)S(1)}, u32[]{:S(2)}, u32[]{:S(2)}) collective-permute-start(bf16[32,4096]{1,0:T(8,128)(2,1)S(1)} %get-tuple-element.40), channel_id=1, source_target_pairs={{0,16},{1,17},{2,18},{3,19},{4,20},{5,21},{6,22},{7,23},{8,24},{9,... | collective-permute-start | bytes 786440 | tf_op jit(solution)/shard_map/ppermute | solution.py:392
  50.3 4.5 %collective-permute-start.13 = (f32[8,128]{1,0:T(8,128)S(1)}, f32[8,128]{1,0:T(8,128)S(1)}, u32[]{:S(2)}, u32[]{:S(2)}) collective-permute-start(f32[8,128]{1,0:T(8,128)S(1)} %get-tuple-element.45), channel_id=1, source_target_pairs={{0,8},{1,9},{2,10},{3,11},{4,12},{5,13},{6,14},{7,15},{8,0},{9,1},... | collective-permute-start | bytes 12296 | tf_op jit(solution)/shard_map/ppermute | solution.py:392
  50.3 4.5 %collective-permute-start.14 = (f32[8,128]{1,0:T(8,128)S(1)}, f32[8,128]{1,0:T(8,128)S(1)}, u32[]{:S(2)}, u32[]{:S(2)}) collective-permute-start(f32[8,128]{1,0:T(8,128)S(1)} %get-tuple-element.45), channel_id=1, source_target_pairs={{0,12},{1,13},{2,14},{3,15},{4,0},{5,1},{6,2},{7,3},{8,4},{9,5},{1... | collective-permute-start | bytes 12296 | tf_op jit(solution)/shard_map/ppermute | solution.py:392
  54.9 3.5 %collective-permute-start.15 = (f32[1,64]{1,0:T(1,128)S(1)}, f32[1,64]{1,0:T(1,128)S(1)}, u32[]{:S(2)}, u32[]{:S(2)}) collective-permute-start(f32[1,64]{1,0:T(1,128)S(1)} %get-tuple-element.46), channel_id=1, source_target_pairs={{0,0},{1,16},{2,2},{3,18},{4,4},{5,20},{6,6},{7,22},{8,8},{9,24},{... | collective-permute-start | bytes 776 | tf_op jit(solution)/shard_map/ppermute | solution.py:392
  55.6 4.4 %collective-permute-start.16 = (f32[1,64]{1,0:T(1,128)S(1)}, f32[1,64]{1,0:T(1,128)S(1)}, u32[]{:S(2)}, u32[]{:S(2)}) collective-permute-start(f32[1,64]{1,0:T(1,128)S(1)} %get-tuple-element.47), channel_id=1, source_target_pairs={{0,16},{1,0},{2,18},{3,2},{4,20},{5,4},{6,22},{7,6},{8,24},{9,8},{... | collective-permute-start | bytes 776 | tf_op jit(solution)/shard_map/ppermute | solution.py:392

commit v8 on v7

--- a/solution.py
+++ b/solution.py
@@ -176,10 +176,10 @@
         copy.wait()
 
 
-def totals_kernel(early, two, three, row, rest):
+def totals_kernel(early, one, two, three, row, rest):
     _, y, _, s = place_here()
     per = row.shape[1]
-    total = early[:2] + two[:2] + pltpu.roll(three[...], per, 1)[:2]
+    total = early[:2] + two[:2] + pltpu.roll(one[...] + three[...], per, 1)[:2]
     row[...] = jnp.where(y == s, total[:1, :per], total[1:, :per])
     rest[...] = jnp.where(y == s, total[1:, :per], total[:1, :per])
 
@@ -295,8 +295,8 @@
 
 
 def late_kernel(
-    rows, mask, recon, codes, scores, mine_2, other_2, mine_3, other_3, sums, one,
-    own_recon, own_codes, own_scores, to_x, to_y, to_d, sums_23, sums_01,
+    rows, mask, recon, codes, scores, mine_2, other_2, mine_3, other_3,
+    own_recon, own_codes, own_scores, to_x, to_y, to_d, sums_23,
 ):
     _, _, _, s = place_here()
     per = mine_2.shape[0]
@@ -312,7 +312,6 @@
         for i, out in enumerate((own_recon, to_x, to_y, to_d)):
             out[:, cols] = part[i * tok : (i + 1) * tok].astype(out.dtype)
     sums_23[...] = group_sums(score)
-    sums_01[...] = sums[...] + pltpu.roll(one[...], per, 1)
     own_codes[...] = jnp.concatenate([codes[:tok], code[:tok]], axis=1)
     own_scores[...] = jnp.concatenate([scores[:tok], score[:tok]], axis=1)
     for i, out in enumerate((to_x, to_y, to_d)):
@@ -462,13 +461,12 @@
         input_output_aliases={0: 0},
         compiler_params=pltpu.CompilerParams(vmem_limit_bytes=1 << 20),
     )(part_2, codes)
-    own_recon, own_codes, own_scores, to_x, to_y, to_d, sums_23, sums_01 = call(
+    own_recon, own_codes, own_scores, to_x, to_y, to_d, sums_23 = call(
         late_kernel,
         [((tok, width), F32), ((tok, names), BF), ((tok, names), F32)]
         + [((tok, width + 2 * names), BF)] * 3
-        + [((8, 2 * per), F32)] * 2,
+        + [((8, 2 * per), F32)],
         rows, mask, recon, codes, scores, part_2, by_core(part_2), part_3, by_core(part_3),
-        sums, by_z(sums, -1),
     )
     from_d = by_xy(to_d)
     from_x = by_x(to_x)
@@ -477,7 +475,7 @@
     row, rest = call(
         totals_kernel,
         [((1, per), F32)] * 2,
-        sums_01, by_z(sums_23, -2), by_z(sums_23, 1),
+        sums, by_z(sums, -1), by_z(sums_23, -2), by_z(sums_23, 1),
     )
     factor = (tok * lat_count * 2 * active / lat_count) ** (-0.5)
     latent_codes, attribution, recon_error, latent_totals = call(

time: 62.6 us -> 62.9 us (level); the launches traced: 62.3 us -> 61.9 us
  waiting for transfers between devices: 32.4 us -> 28.6 us
  starting transfers between devices: 18.1 us -> 21.5 us
    ppermute x17, waiting for transfers between devices: 32.4 us -> 28.6 us  [permute(): return lax.ppermute(values, AXES, pairs)]
    ppermute x17, starting transfers between devices: 18.1 us -> 21.5 us  [permute(): return lax.ppermute(values, AXES, pairs)]
where the time goes in v8:
time: 62.9 us; the launch traced here: 61.9 us
  waiting for transfers between devices  28.6 us (45%)
  starting transfers between devices  21.5 us (34%)
  Pallas kernels  8.08 us (13%)
  local copies, waits for them, and re-layouts  2.94 us (5%)
  between operations  0.77 us (1%)
    ppermute x17, waiting for transfers between devices, permute(): return lax.ppermute(values, AXES, pairs)  28.6 us
    ppermute x17, starting transfers between devices, permute(): return lax.ppermute(values, AXES, pairs)  21.5 us
    pallas_call x6, Pallas kernels, call(): pl.pallas_call(kernel, in_specs=[pl.BlockSpec(memory_space=pl.ANY if i in...  8.08 us
    unnamed x18, local copies, waits for them, and re-layouts  2.93 us
  transfers between devices with their start and end apart: 17, of which 9 were waited for; matrix products, arithmetic and copies ran while one was open for 0% of the time, Pallas kernels for 5%

profile of v8, /device:TPU:0, one launch (start us, length us, event | category | flops | bytes accessed | tf_op | source)
XLA Modules:
  0.0 61.9 jit_solution(11156802130630789403)
XLA Ops:
  0.7 2.4 %shard_map.111._.mine_0 = bf16[64,3712]{1,0:T(8,128)(2,1)} custom-call(bf16[3584,128]{1,0:T(8,128)(2,1)} %enc.3, bf16[128,3584]{1,0:T(8,128)(2,1)} %dec.3, f32[1,128]{1,0:T(1,128)} %bitcast.5), custom_call_target="tpu_custom_call" | custom-call | tf_op jit(solution)/shard_map/pallas_call | solution.py:114
  3.1 5.1 %collective-permute-start.3 = (bf16[64,3712]{1,0:T(8,128)(2,1)}, bf16[64,3712]{1,0:T(8,128)(2,1)S(1)}, u32[]{:S(2)}, u32[]{:S(2)}) collective-permute-start(bf16[64,3712]{1,0:T(8,128)(2,1)} %shard_map.111._.mine_0), channel_id=1, source_target_pairs={{0,12},{1,13},{2,14},{3,15},{4,0},{5,1},{6,2},{7,3},{8,4},{9,5},{1... | collective-permute-start | bytes 1425416 | tf_op jit(solution)/shard_map/ppermute | solution.py:391
  8.2 1.0 %copy-done = bf16[64,3712]{1,0:T(8,128)(2,1)S(1)} copy-done((bf16[64,3712]{1,0:T(8,128)(2,1)S(1)}, bf16[64,3712]{1,0:T(8,128)(2,1)}, u32[]{:S(2)}) %copy-start) | copy-done | bytes 475160
  9.2 0.8 %copy-done.6 = s32[32,4,128]{2,1,0:T(4,128)S(1)} copy-done((s32[32,4,128]{2,1,0:T(4,128)S(1)}, s32[32,4,128]{2,1,0:T(4,128)}, u32[]{:S(2)}) %copy-start.6) | copy-done | bytes 65560
  10.1 0.7 %shard_map.112 = (bf16[32,7424]{1,0:T(8,128)(2,1)S(1)}, bf16[32,7424]{1,0:T(8,128)(2,1)S(1)}, bf16[32,7424]{1,0:T(8,128)(2,1)S(1)}, bf16[32,256]{1,0:T(8,128)(2,1)S(1)}) custom-call(bf16[32,3584]{1,0:T(8,128)(2,1)S(1)} %copy-done.4, bf16[32,3584]{1,0:T(8,128)(2,1)S(1)} %copy-done.5, s32[4,32]{1,0:T(4,128)S(1)} %bitcast.3, s32[32,4,128]{2,1,0:T(4,128)S(1)} %copy-done.6, ...), custom_call_target="tpu_custom_call" | custom-call | tf_op jit(solution)/shard_map/pallas_call | solution.py:114
  10.8 2.5 %collective-permute-start = (bf16[32,7424]{1,0:T(8,128)(2,1)S(1)}, bf16[32,7424]{1,0:T(8,128)(2,1)S(1)}, u32[]{:S(2)}, u32[]{:S(2)}) collective-permute-start(bf16[32,7424]{1,0:T(8,128)(2,1)S(1)} %get-tuple-element.27.own), channel_id=1, source_target_pairs={{0,18},{1,19},{2,16},{3,17},{4,22},{5,23},{6,20},{7,21},{8,26},{9,... | collective-permute-start | bytes 1425416 | tf_op jit(solution)/shard_map/ppermute | solution.py:391
  13.3 0.0 collective-permute-start.7
  13.3 0.5 collective-permute-start.1
  13.8 0.5 collective-permute-start.2
  14.3 5.5 %collective-permute-done.3.mine_1 = bf16[64,3712]{1,0:T(8,128)(2,1)S(1)} collective-permute-done((bf16[64,3712]{1,0:T(8,128)(2,1)}, bf16[64,3712]{1,0:T(8,128)(2,1)S(1)}, u32[]{:S(2)}, u32[]{:S(2)}) %collective-permute-start.3) | collective-permute-done | bytes 475168 | tf_op jit(solution)/shard_map/ppermute | solution.py:391
  19.8 5.7 %collective-permute-done.from_d = bf16[32,7424]{1,0:T(8,128)(2,1)S(1)} collective-permute-done((bf16[32,7424]{1,0:T(8,128)(2,1)S(1)}, bf16[32,7424]{1,0:T(8,128)(2,1)S(1)}, u32[]{:S(2)}, u32[]{:S(2)}) %collective-permute-start) | collective-permute-done | bytes 475168 | tf_op jit(solution)/shard_map/ppermute | solution.py:391
  25.6 0.4 collective-permute-start.5
  26.0 4.8 %collective-permute-done.7.mine_3 = bf16[64,3712]{1,0:T(8,128)(2,1)S(1)} collective-permute-done((bf16[64,3712]{1,0:T(8,128)(2,1)S(1)}, bf16[64,3712]{1,0:T(8,128)(2,1)S(1)}, u32[]{:S(2)}, u32[]{:S(2)}) %collective-permute-start.7) | collective-permute-done | bytes 475168 | tf_op jit(solution)/shard_map/ppermute | solution.py:391
  30.9 3.5 %collective-permute-done.1.from_x = bf16[32,7424]{1,0:T(8,128)(2,1)S(1)} collective-permute-done((bf16[32,7424]{1,0:T(8,128)(2,1)S(1)}, bf16[32,7424]{1,0:T(8,128)(2,1)S(1)}, u32[]{:S(2)}, u32[]{:S(2)}) %collective-permute-start.1) | collective-permute-done | bytes 475168 | tf_op jit(solution)/shard_map/ppermute | solution.py:391
  34.4 1.0 %copy-done.1 = bf16[64,3712]{1,0:T(8,128)(2,1)S(1)} copy-done((bf16[64,3712]{1,0:T(8,128)(2,1)S(1)}, bf16[64,3712]{1,0:T(8,128)(2,1)}, u32[]{:S(2)}) %copy-start.1) | copy-done | bytes 475160
  35.4 2.2 %shard_map.113 = (bf16[128,7168]{1,0:T(8,128)(2,1)S(1)}, bf16[128,256]{1,0:T(8,128)(2,1)S(1)}, f32[128,3584]{1,0:T(8,128)S(1)}, bf16[128,128]{1,0:T(8,128)(2,1)S...) custom-call(bf16[32,7424]{1,0:T(8,128)(2,1)S(1)} %collective-permute-done.from_d, ...), custom_call_target="tpu_custom_call" | custom-call | tf_op jit(solution)/shard_map/pallas_call | solution.py:114
  37.6 2.3 %collective-permute-done.5.refs_0_ = bf16[64,3712]{1,0:T(8,128)(2,1)S(1)} collective-permute-done((bf16[64,3712]{1,0:T(8,128)(2,1)S(1)}, bf16[64,3712]{1,0:T(8,128)(2,1)S(1)}, u32[]{:S(2)}, u32[]{:S(2)}) %collective-permute-start.5) | collective-permute-done | bytes 475168 | tf_op jit(solution)/shard_map/ppermute | solution.py:391
  39.9 1.8 %collective-permute-done.6.other_2 = bf16[64,3712]{1,0:T(8,128)(2,1)S(1)} collective-permute-done((bf16[64,3712]{1,0:T(8,128)(2,1)S(1)}, bf16[64,3712]{1,0:T(8,128)(2,1)S(1)}, u32[]{:S(2)}, u32[]{:S(2)}) %collective-permute-start.6) | collective-permute-done | bytes 475168 | tf_op jit(solution)/shard_map/ppermute | solution.py:391
  41.7 1.5 %shard_map.115 = (f32[32,3584]{1,0:T(8,128)S(1)}, bf16[32,256]{1,0:T(8,128)(2,1)S(1)}, f32[32,256]{1,0:T(8,128)S(1)}, bf16[32,4096]{1,0:T(8,128)(2,1)S(1)}, bf16...) custom-call(bf16[128,7168]{1,0:T(8,128)(2,1)S(1)} %get-tuple-element.31.rows, ...), custom_call_target="tpu_custom_call" | custom-call | tf_op jit(solution)/shard_map/pallas_call | solution.py:114
  43.2 1.6 %collective-permute-start.10 = (bf16[32,4096]{1,0:T(8,128)(2,1)S(1)}, bf16[32,4096]{1,0:T(8,128)(2,1)S(1)}, u32[]{:S(2)}, u32[]{:S(2)}) collective-permute-start(bf16[32,4096]{1,0:T(8,128)(2,1)S(1)} %get-tuple-element.37), channel_id=1, source_target_pairs={{0,2},{1,3},{2,0},{3,1},{4,6},{5,7},{6,4},{7,5},{8,10},{9,11},{10,... | collective-permute-start | bytes 786440 | tf_op jit(solution)/shard_map/ppermute | solution.py:391
  44.8 1.5 %collective-permute-start.11 = (bf16[32,4096]{1,0:T(8,128)(2,1)S(1)}, bf16[32,4096]{1,0:T(8,128)(2,1)S(1)}, u32[]{:S(2)}, u32[]{:S(2)}) collective-permute-start(bf16[32,4096]{1,0:T(8,128)(2,1)S(1)} %get-tuple-element.38), channel_id=1, source_target_pairs={{0,16},{1,17},{2,18},{3,19},{4,20},{5,21},{6,22},{7,23},{8,24},{9,... | collective-permute-start | bytes 786440 | tf_op jit(solution)/shard_map/ppermute | solution.py:391
  46.3 0.5 collective-permute-start.9
  46.8 0.5 collective-permute-start.12
  47.2 3.4 %collective-permute-start.13 = (f32[8,128]{1,0:T(8,128)S(1)}, f32[8,128]{1,0:T(8,128)S(1)}, u32[]{:S(2)}, u32[]{:S(2)}) collective-permute-start(f32[8,128]{1,0:T(8,128)S(1)} %get-tuple-element.43), channel_id=1, source_target_pairs={{0,8},{1,9},{2,10},{3,11},{4,12},{5,13},{6,14},{7,15},{8,0},{9,1},... | collective-permute-start | bytes 12296 | tf_op jit(solution)/shard_map/ppermute | solution.py:391
  50.7 1.5 %collective-permute-done.12.one = f32[8,128]{1,0:T(8,128)S(1)} collective-permute-done((f32[8,128]{1,0:T(8,128)S(1)}, f32[8,128]{1,0:T(8,128)S(1)}, u32[]{:S(2)}, u32[]{:S(2)}) %collective-permute-start.12) | collective-permute-done | bytes 4128 | tf_op jit(solution)/shard_map/ppermute | solution.py:391
  52.2 1.5 %collective-permute-start.14 = (f32[8,128]{1,0:T(8,128)S(1)}, f32[8,128]{1,0:T(8,128)S(1)}, u32[]{:S(2)}, u32[]{:S(2)}) collective-permute-start(f32[8,128]{1,0:T(8,128)S(1)} %get-tuple-element.43), channel_id=1, source_target_pairs={{0,12},{1,13},{2,14},{3,15},{4,0},{5,1},{6,2},{7,3},{8,4},{9,5},{1... | collective-permute-start | bytes 12296 | tf_op jit(solution)/shard_map/ppermute | solution.py:391
  53.7 2.1 %collective-permute-done.14.three = f32[8,128]{1,0:T(8,128)S(1)} collective-permute-done((f32[8,128]{1,0:T(8,128)S(1)}, f32[8,128]{1,0:T(8,128)S(1)}, u32[]{:S(2)}, u32[]{:S(2)}) %collective-permute-start.14) | collective-permute-done | bytes 4128 | tf_op jit(solution)/shard_map/ppermute | solution.py:391
  55.8 0.1 shard_map.116
  55.9 0.7 %collective-permute-start.15 = (f32[1,64]{1,0:T(1,128)S(1)}, f32[1,64]{1,0:T(1,128)S(1)}, u32[]{:S(2)}, u32[]{:S(2)}) collective-permute-start(f32[1,64]{1,0:T(1,128)S(1)} %get-tuple-element.44), channel_id=1, source_target_pairs={{0,0},{1,16},{2,2},{3,18},{4,4},{5,20},{6,6},{7,22},{8,8},{9,24},{... | collective-permute-start | bytes 776 | tf_op jit(solution)/shard_map/ppermute | solution.py:391
  56.5 2.8 %collective-permute-start.16 = (f32[1,64]{1,0:T(1,128)S(1)}, f32[1,64]{1,0:T(1,128)S(1)}, u32[]{:S(2)}, u32[]{:S(2)}) collective-permute-start(f32[1,64]{1,0:T(1,128)S(1)} %get-tuple-element.45), channel_id=1, source_target_pairs={{0,16},{1,0},{2,18},{3,2},{4,20},{5,4},{6,22},{7,6},{8,24},{9,8},{... | collective-permute-start | bytes 776 | tf_op jit(solution)/shard_map/ppermute | solution.py:391
  59.3 1.3 %collective-permute-done.16.rest = f32[1,64]{1,0:T(1,128)S(1)} collective-permute-done((f32[1,64]{1,0:T(1,128)S(1)}, f32[1,64]{1,0:T(1,128)S(1)}, u32[]{:S(2)}, u32[]{:S(2)}) %collective-permute-start.16) | collective-permute-done | bytes 288 | tf_op jit(solution)/shard_map/ppermute | solution.py:391
  60.6 1.3 %shard_map.117 = (bf16[32,4,128]{2,1,0:T(4,128)(2,1)}, f32[32,4,128]{2,1,0:T(4,128)}, bf16[32,3584]{1,0:T(8,128)(2,1)}, f32[1,64]{1,0:T(1,128)}) custom-call(bf16[32,4096]{1,0:T(8,128)(2,1)S(1)} %collective-permute-done.9.from_d, bf16[32,4096]{1,0:T(8,128)(2,1)S(1)} %collective-permute-done.10.from_x, bf16[32,4096]{1,0:T(8,128)(2,1)S(1)} %collective-permute-done.11.from_y, ...), custom_call_target="tpu_custom_call" | custom-call | tf_op jit(solution)/shard_map/pallas_call | solution.py:114
  (28 shorter events, 0.1 us)
Async XLA Ops:
  0.6 33.7 %copy-start.2 = (bf16[3584,128]{1,0:T(8,128)(2,1)S(1)}, bf16[3584,128]{1,0:T(8,128)(2,1)}, u32[]{:S(2)}) copy-start(bf16[3584,128]{1,0:T(8,128)(2,1)} %enc.3) | copy-start | bytes 2752516
  0.6 33.7 %copy-start.3 = (bf16[128,3584]{1,0:T(8,128)(2,1)S(1)}, bf16[128,3584]{1,0:T(8,128)(2,1)}, u32[]{:S(2)}) copy-start(bf16[128,3584]{1,0:T(8,128)(2,1)} %dec.3) | copy-start | bytes 2752516
  0.7 7.5 %copy-start.7 = (s32[32,4]{0,1:T(4,128)S(1)}, s32[32,4]{0,1:T(4,128)}, u32[]{:S(2)}) copy-start(s32[32,4]{0,1:T(4,128)} %param.10) | copy-start | bytes 1540
  0.7 7.5 %copy-start.4 = (bf16[32,3584]{1,0:T(8,128)(2,1)S(1)}, bf16[32,3584]{1,0:T(8,128)(2,1)}, u32[]{:S(2)}) copy-start(bf16[32,3584]{1,0:T(8,128)(2,1)} %res.1) | copy-start | bytes 688132
  0.7 7.5 %copy-start.5 = (bf16[32,3584]{1,0:T(8,128)(2,1)S(1)}, bf16[32,3584]{1,0:T(8,128)(2,1)}, u32[]{:S(2)}) copy-start(bf16[32,3584]{1,0:T(8,128)(2,1)} %grad.1) | copy-start | bytes 688132
  3.1 16.7 %collective-permute-start.3 = (bf16[64,3712]{1,0:T(8,128)(2,1)}, bf16[64,3712]{1,0:T(8,128)(2,1)S(1)}, u32[]{:S(2)}, u32[]{:S(2)}) collective-permute-start(bf16[64,3712]{1,0:T(8,128)(2,1)} %shard_map.111._.mine_0), channel_id=1, source_target_pairs={{0,12},{1,13},{2,14},{3,15},{4,0},{5,1},{6,2},{7,3},{8,4},{9,5},{1... | collective-permute-start | bytes 1425416 | tf_op jit(solution)/shard_map/ppermute | solution.py:391
  8.2 1.1 %copy-start = (bf16[64,3712]{1,0:T(8,128)(2,1)S(1)}, bf16[64,3712]{1,0:T(8,128)(2,1)}, u32[]{:S(2)}) copy-start(bf16[64,3712]{1,0:T(8,128)(2,1)} %shard_map.111._.mine_0) | copy-start | bytes 1425412
  9.2 0.8 %copy-start.6 = (s32[32,4,128]{2,1,0:T(4,128)S(1)}, s32[32,4,128]{2,1,0:T(4,128)}, u32[]{:S(2)}) copy-start(s32[32,4,128]{2,1,0:T(4,128)} %jump.1) | copy-start | bytes 196612
  10.8 14.8 %collective-permute-start = (bf16[32,7424]{1,0:T(8,128)(2,1)S(1)}, bf16[32,7424]{1,0:T(8,128)(2,1)S(1)}, u32[]{:S(2)}, u32[]{:S(2)}) collective-permute-start(bf16[32,7424]{1,0:T(8,128)(2,1)S(1)} %get-tuple-element.27.own), channel_id=1, source_target_pairs={{0,18},{1,19},{2,16},{3,17},{4,22},{5,23},{6,20},{7,21},{8,26},{9,... | collective-permute-start | bytes 1425416 | tf_op jit(solution)/shard_map/ppermute | solution.py:391
  13.3 17.6 %collective-permute-start.7 = (bf16[64,3712]{1,0:T(8,128)(2,1)S(1)}, bf16[64,3712]{1,0:T(8,128)(2,1)S(1)}, u32[]{:S(2)}, u32[]{:S(2)}) collective-permute-start(bf16[64,3712]{1,0:T(8,128)(2,1)S(1)} %copy-done), channel_id=1, source_target_pairs={{0,4},{1,5},{2,6},{3,7},{4,8},{5,9},{6,10},{7,11},{8,12},{9,13},{1... | collective-permute-start | bytes 1425416 | tf_op jit(solution)/shard_map/ppermute | solution.py:391
  13.3 21.1 %collective-permute-start.1 = (bf16[32,7424]{1,0:T(8,128)(2,1)S(1)}, bf16[32,7424]{1,0:T(8,128)(2,1)S(1)}, u32[]{:S(2)}, u32[]{:S(2)}) collective-permute-start(bf16[32,7424]{1,0:T(8,128)(2,1)S(1)} %get-tuple-element.28), channel_id=1, source_target_pairs={{0,2},{1,3},{2,0},{3,1},{4,6},{5,7},{6,4},{7,5},{8,10},{9,11},{10,... | collective-permute-start | bytes 1425416 | tf_op jit(solution)/shard_map/ppermute | solution.py:391
  13.8 20.5 %collective-permute-start.2 = (bf16[32,7424]{1,0:T(8,128)(2,1)S(1)}, bf16[32,7424]{1,0:T(8,128)(2,1)S(1)}, u32[]{:S(2)}, u32[]{:S(2)}) collective-permute-start(bf16[32,7424]{1,0:T(8,128)(2,1)S(1)} %get-tuple-element.29), channel_id=1, source_target_pairs={{0,16},{1,17},{2,18},{3,19},{4,20},{5,21},{6,22},{7,23},{8,24},{9,... | collective-permute-start | bytes 1425416 | tf_op jit(solution)/shard_map/ppermute | solution.py:391
  19.8 14.5 %collective-permute-start.4 = (bf16[64,3712]{1,0:T(8,128)(2,1)S(1)}, bf16[64,3712]{1,0:T(8,128)(2,1)S(1)}, u32[]{:S(2)}, u32[]{:S(2)}) collective-permute-start(bf16[64,3712]{1,0:T(8,128)(2,1)S(1)} %collective-permute-done.3.mine_1), channel_id=1, source_target_pairs={{0,1},{1,0},{2,3},{3,2},{4,5},{5,4},{6,7},{7,6},{8,9},{9,8},{10,11... | collective-permute-start | bytes 1425416 | tf_op jit(solution)/shard_map/ppermute | solution.py:391
  25.6 14.3 %collective-permute-start.5 = (bf16[64,3712]{1,0:T(8,128)(2,1)S(1)}, bf16[64,3712]{1,0:T(8,128)(2,1)S(1)}, u32[]{:S(2)}, u32[]{:S(2)}) collective-permute-start(bf16[64,3712]{1,0:T(8,128)(2,1)S(1)} %collective-permute-done.3.mine_1), channel_id=1, source_target_pairs={{0,12},{1,13},{2,14},{3,15},{4,0},{5,1},{6,2},{7,3},{8,4},{9,5},{1... | collective-permute-start | bytes 1425416 | tf_op jit(solution)/shard_map/ppermute | solution.py:391
  30.9 9.0 %collective-permute-start.8 = (bf16[64,3712]{1,0:T(8,128)(2,1)S(1)}, bf16[64,3712]{1,0:T(8,128)(2,1)S(1)}, u32[]{:S(2)}, u32[]{:S(2)}) collective-permute-start(bf16[64,3712]{1,0:T(8,128)(2,1)S(1)} %collective-permute-done.7.mine_3), channel_id=1, source_target_pairs={{0,1},{1,0},{2,3},{3,2},{4,5},{5,4},{6,7},{7,6},{8,9},{9,8},{10,11... | collective-permute-start | bytes 1425416 | tf_op jit(solution)/shard_map/ppermute | solution.py:391
  34.4 1.0 %copy-start.1 = (bf16[64,3712]{1,0:T(8,128)(2,1)S(1)}, bf16[64,3712]{1,0:T(8,128)(2,1)}, u32[]{:S(2)}) copy-start(bf16[64,3712]{1,0:T(8,128)(2,1)} %shard_map.111._.mine_0) | copy-start | bytes 1425412
  39.9 1.8 %collective-permute-start.6 = (bf16[64,3712]{1,0:T(8,128)(2,1)S(1)}, bf16[64,3712]{1,0:T(8,128)(2,1)S(1)}, u32[]{:S(2)}, u32[]{:S(2)}) collective-permute-start(bf16[64,3712]{1,0:T(8,128)(2,1)S(1)} %shard_map.114.mine_2), channel_id=1, source_target_pairs={{0,1},{1,0},{2,3},{3,2},{4,5},{5,4},{6,7},{7,6},{8,9},{9,8},{10,11... | collective-permute-start | bytes 1425416 | tf_op jit(solution)/shard_map/ppermute | solution.py:391
  41.7 17.6 %copy-start.8 = (f32[3584]{0:T(1024)S(1)}, f32[3584]{0:T(1024)}, u32[]{:S(2)}) copy-start(f32[3584]{0:T(1024)} %param.15) | copy-start | bytes 43012
  43.2 17.4 %collective-permute-start.10 = (bf16[32,4096]{1,0:T(8,128)(2,1)S(1)}, bf16[32,4096]{1,0:T(8,128)(2,1)S(1)}, u32[]{:S(2)}, u32[]{:S(2)}) collective-permute-start(bf16[32,4096]{1,0:T(8,128)(2,1)S(1)} %get-tuple-element.37), channel_id=1, source_target_pairs={{0,2},{1,3},{2,0},{3,1},{4,6},{5,7},{6,4},{7,5},{8,10},{9,11},{10,... | collective-permute-start | bytes 786440 | tf_op jit(solution)/shard_map/ppermute | solution.py:391
  44.8 15.8 %collective-permute-start.11 = (bf16[32,4096]{1,0:T(8,128)(2,1)S(1)}, bf16[32,4096]{1,0:T(8,128)(2,1)S(1)}, u32[]{:S(2)}, u32[]{:S(2)}) collective-permute-start(bf16[32,4096]{1,0:T(8,128)(2,1)S(1)} %get-tuple-element.38), channel_id=1, source_target_pairs={{0,16},{1,17},{2,18},{3,19},{4,20},{5,21},{6,22},{7,23},{8,24},{9,... | collective-permute-start | bytes 786440 | tf_op jit(solution)/shard_map/ppermute | solution.py:391
  46.3 14.3 %collective-permute-start.9 = (bf16[32,4096]{1,0:T(8,128)(2,1)S(1)}, bf16[32,4096]{1,0:T(8,128)(2,1)S(1)}, u32[]{:S(2)}, u32[]{:S(2)}) collective-permute-start(bf16[32,4096]{1,0:T(8,128)(2,1)S(1)} %get-tuple-element.36), channel_id=1, source_target_pairs={{0,18},{1,19},{2,16},{3,17},{4,22},{5,23},{6,20},{7,21},{8,26},{9,... | collective-permute-start | bytes 786440 | tf_op jit(solution)/shard_map/ppermute | solution.py:391
  46.8 5.4 %collective-permute-start.12 = (f32[8,128]{1,0:T(8,128)S(1)}, f32[8,128]{1,0:T(8,128)S(1)}, u32[]{:S(2)}, u32[]{:S(2)}) collective-permute-start(f32[8,128]{1,0:T(8,128)S(1)} %get-tuple-element.42.early), channel_id=1, source_target_pairs={{0,4},{1,5},{2,6},{3,7},{4,8},{5,9},{6,10},{7,11},{8,12},{9,13},{1... | collective-permute-start | bytes 12296 | tf_op jit(solution)/shard_map/ppermute | solution.py:391
  47.2 6.5 %collective-permute-start.13 = (f32[8,128]{1,0:T(8,128)S(1)}, f32[8,128]{1,0:T(8,128)S(1)}, u32[]{:S(2)}, u32[]{:S(2)}) collective-permute-start(f32[8,128]{1,0:T(8,128)S(1)} %get-tuple-element.43), channel_id=1, source_target_pairs={{0,8},{1,9},{2,10},{3,11},{4,12},{5,13},{6,14},{7,15},{8,0},{9,1},... | collective-permute-start | bytes 12296 | tf_op jit(solution)/shard_map/ppermute | solution.py:391
  52.2 3.6 %collective-permute-start.14 = (f32[8,128]{1,0:T(8,128)S(1)}, f32[8,128]{1,0:T(8,128)S(1)}, u32[]{:S(2)}, u32[]{:S(2)}) collective-permute-start(f32[8,128]{1,0:T(8,128)S(1)} %get-tuple-element.43), channel_id=1, source_target_pairs={{0,12},{1,13},{2,14},{3,15},{4,0},{5,1},{6,2},{7,3},{8,4},{9,5},{1... | collective-permute-start | bytes 12296 | tf_op jit(solution)/shard_map/ppermute | solution.py:391
  55.9 3.5 %collective-permute-start.15 = (f32[1,64]{1,0:T(1,128)S(1)}, f32[1,64]{1,0:T(1,128)S(1)}, u32[]{:S(2)}, u32[]{:S(2)}) collective-permute-start(f32[1,64]{1,0:T(1,128)S(1)} %get-tuple-element.44), channel_id=1, source_target_pairs={{0,0},{1,16},{2,2},{3,18},{4,4},{5,20},{6,6},{7,22},{8,8},{9,24},{... | collective-permute-start | bytes 776 | tf_op jit(solution)/shard_map/ppermute | solution.py:391
  56.5 4.1 %collective-permute-start.16 = (f32[1,64]{1,0:T(1,128)S(1)}, f32[1,64]{1,0:T(1,128)S(1)}, u32[]{:S(2)}, u32[]{:S(2)}) collective-permute-start(f32[1,64]{1,0:T(1,128)S(1)} %get-tuple-element.45), channel_id=1, source_target_pairs={{0,16},{1,0},{2,18},{3,2},{4,20},{5,4},{6,22},{7,6},{8,24},{9,8},{... | collective-permute-start | bytes 776 | tf_op jit(solution)/shard_map/ppermute | solution.py:391
